TPU v7x, 32 devices: a whole 2x2x4 slice. The times are simulated.
32 devices in a mesh: section: 8 (over y, x, core), ctx: 4 (over z).
Axes of the slice: x: 2, y: 2, z: 4, core: 2. Of those that a mesh axis runs over, the one named last changes fastest.
Arguments:
- streams: bfloat16 [8, 512, 5120], P('section', 'ctx'), may hold values from -6 to 6
- conv_weight: bfloat16 [8, 4, 5120], P('section'), may hold values from -3 to 3
- beta_logit: float32 [8, 512, 16], P('section', 'ctx'), may hold values from -12 to 3
- gate_log: float32 [8, 512, 8], P('section', 'ctx'), may hold values from -2 to 0
- norm_gain: float32 [8, 1024], P('section'), may hold values from 0.25 to 1.75
- w_out: bfloat16 [8, 1024, 2048], P('section', None, 'ctx'), may hold values from -0.1875 to 0.1875
Outputs:
- handed: bfloat16 [8, 512, 2048], P('section', 'ctx')
All inputs are finite; a program needn't handle non-finite values.
Results may differ from a plain program's by a relative error of at most 0.0049.
Values may be sent and summed in bfloat16 or wider, within the bound.
No kernel may reach another device: no remote copies, remote signals or barrier semaphores. Data moves between devices by JAX's collectives and lax.ppermute only.
A program may use at most 128 MiB of HBM per device.

v0:
```python
import jax
import jax.numpy as jnp
from jax import lax
from jax.sharding import PartitionSpec as P

HEAD_TOTAL = 8
HK = 128
STEPS = 2
CONV = 4
SPAN = 128


highest = lax.Precision.HIGHEST


def shifted(value, axis, steps):
    count = lax.axis_size(axis)
    first, last = (max(0, -steps), min(count, count - steps))
    return lax.ppermute(value, axis, [(source, source + steps) for source in range(first, last)])


def entering(value, axis, join, neutral):
    count, mine = (lax.axis_size(axis), lax.axis_index(axis))
    pieces = jax.tree.map(lambda part: lax.all_gather(part, axis), value)
    total = jax.tree.map(
        lambda part, zero: jnp.full_like(part, 0) + jnp.asarray(zero, part.dtype), value, neutral
    )

    def turn(position, total):
        longer = join(total, jax.tree.map(lambda part: part[position], pieces))
        return jax.tree.map(lambda new, old: jnp.where(position < mine, new, old), longer, total)

    return lax.fori_loop(0, count - 1, turn, total)


def passed_along(value, axis, steps):
    count = lax.axis_size(axis)
    pairs = [(source, (source + steps) % count) for source in range(count)]
    return lax.ppermute(value, axis, pairs)


def mix_taps(extended, tap_weights):
    tok_count = extended.shape[0] - tap_weights.shape[0] + 1
    summed = jnp.zeros((tok_count, extended.shape[1]), jnp.float32)
    for offset in range(tap_weights.shape[0]):
        summed = summed + tap_weights[offset].astype(jnp.float32) * extended[
            offset : offset + tok_count
        ].astype(jnp.float32)
    return jax.nn.silu(summed)


def unit_rows(vectors):
    return vectors * lax.rsqrt(jnp.sum(vectors * vectors, axis=-1, keepdims=True) + 1e-06)


def head_major(active, beta_logit, gate_log):
    tok_count = active.shape[0]
    head_width = HEAD_TOTAL * HK
    queries = unit_rows(active[:, :head_width].reshape(tok_count, HEAD_TOTAL, HK)).transpose(
        1, 0, 2
    )
    keys_all = unit_rows(
        active[:, head_width : (1 + STEPS) * head_width].reshape(tok_count, STEPS, HEAD_TOTAL, HK)
    )
    keys_all = keys_all.transpose(2, 0, 1, 3).reshape(HEAD_TOTAL, tok_count * STEPS, HK)
    values_all = active[:, (1 + STEPS) * head_width :].reshape(tok_count, STEPS, HEAD_TOTAL, HK)
    values_all = values_all.transpose(2, 0, 1, 3).reshape(HEAD_TOTAL, tok_count * STEPS, HK)
    step_size = (
        jax.nn.sigmoid(beta_logit.reshape(tok_count, STEPS, HEAD_TOTAL))
        .transpose(2, 0, 1)
        .reshape(HEAD_TOTAL, tok_count * STEPS)
    )
    opening = (lax.broadcasted_iota(jnp.int32, (1, STEPS, 1), 1) == 0).astype(gate_log.dtype)
    log_gate = (
        (gate_log[:, None, :] * opening).transpose(2, 0, 1).reshape(HEAD_TOTAL, tok_count * STEPS)
    )
    return (queries, keys_all, values_all, step_size, log_gate)


def span_terms(queries, keys_all, values_all, step_size, log_gate):
    head_count, virtual, head_dim = keys_all.shape
    blocks = virtual // SPAN
    per_block = SPAN // STEPS
    queries = queries.reshape(head_count, blocks, per_block, head_dim)
    keys_all = keys_all.reshape(head_count, blocks, SPAN, head_dim)
    values_all = values_all.reshape(head_count, blocks, SPAN, head_dim)
    step_size = step_size.reshape(head_count, blocks, SPAN)
    cumulate = jnp.cumsum(log_gate.reshape(head_count, blocks, SPAN), axis=-1)
    query_log = cumulate[..., STEPS - 1 :: STEPS]
    row_index = lax.broadcasted_iota(jnp.int32, (SPAN, SPAN), 0)
    col_index = lax.broadcasted_iota(jnp.int32, (SPAN, SPAN), 1)
    strict = col_index < row_index
    spread = cumulate[..., :, None] - cumulate[..., None, :]
    damping = jnp.where(strict, jnp.exp(jnp.where(strict, spread, 0.0)), 0.0)
    key_inner = jnp.einsum("hcid,hcjd->hcij", keys_all, keys_all, precision=highest)
    unit_lower = (
        jnp.eye(SPAN, dtype=key_inner.dtype) + step_size[..., :, None] * damping * key_inner
    )
    right_sides = jnp.concatenate(
        [step_size[..., None] * values_all, (step_size * jnp.exp(cumulate))[..., None] * keys_all],
        axis=-1,
    )
    solved = jax.scipy.linalg.solve_triangular(
        unit_lower, right_sides, lower=True, unit_diagonal=True
    )
    value_part = solved[..., :head_dim]
    key_part = solved[..., head_dim:]
    to_end = keys_all * jnp.exp(cumulate[..., -1:] - cumulate)[..., None]
    carried = jnp.exp(cumulate[..., -1])[..., None, None] * jnp.eye(head_dim, dtype=key_inner.dtype)
    carried = carried - jnp.einsum("hcid,hcie->hcde", to_end, key_part, precision=highest)
    written = jnp.einsum("hcid,hcie->hcde", to_end, value_part, precision=highest)
    query_row = lax.broadcasted_iota(jnp.int32, (per_block, SPAN), 0) * STEPS + STEPS - 1
    query_col = lax.broadcasted_iota(jnp.int32, (per_block, SPAN), 1)
    allowed = query_col <= query_row
    query_spread = query_log[..., :, None] - cumulate[..., None, :]
    query_damping = jnp.where(allowed, jnp.exp(jnp.where(allowed, query_spread, 0.0)), 0.0)
    scores = jnp.einsum("hcpd,hcid->hcpi", queries, keys_all, precision=highest) * query_damping
    direct = jnp.einsum("hcpi,hcie->hcpe", scores, value_part, precision=highest)
    reach_map = queries * jnp.exp(query_log)[..., None] - jnp.einsum(
        "hcpi,hcie->hcpe", scores, key_part, precision=highest
    )
    return (
        jnp.moveaxis(carried, 1, 0),
        jnp.moveaxis(written, 1, 0),
        jnp.moveaxis(direct, 1, 0),
        jnp.moveaxis(reach_map, 1, 0),
    )


def advance(state_now, piece_terms):
    carried, written, direct, reach_map = piece_terms
    span_out = direct + jnp.einsum("hpd,hde->hpe", reach_map, state_now, precision=highest)
    state_now = jnp.einsum("hde,hef->hdf", carried, state_now, precision=highest) + written
    return (state_now, span_out)


def normalize(outputs, norm_gain):
    tok_count = outputs.shape[0]
    inverse_rms = lax.rsqrt(jnp.mean(outputs * outputs, axis=-1, keepdims=True) + 1e-05)
    return (
        (outputs * inverse_rms * norm_gain.reshape(HEAD_TOTAL, HK))
        .reshape(tok_count, HEAD_TOTAL * HK)
        .astype(jnp.bfloat16)
    )


def combine_pairs(earlier_pair, later_pair):
    first_map, first_add = earlier_pair
    second_map, second_add = later_pair
    joined_map = jnp.einsum("hde,hef->hdf", second_map, first_map, precision=highest)
    joined_add = jnp.einsum("hde,hef->hdf", second_map, first_add, precision=highest) + second_add
    return (joined_map, joined_add)


def compose_step(carried_in, piece_terms):
    so_far, added_state = carried_in
    next_map = jnp.einsum("hde,hef->hdf", piece_terms[0], so_far, precision=highest)
    next_add = (
        jnp.einsum("hde,hef->hdf", piece_terms[0], added_state, precision=highest) + piece_terms[1]
    )
    return ((next_map, next_add), None)


def on_device(streams, conv_weight, beta_logit, gate_log, norm_gain, w_out):
    own_rows = streams[0]
    tok_count = own_rows.shape[0]
    rim_rows = shifted(own_rows[tok_count - (CONV - 1) :], "ctx", 1)
    active = mix_taps(jnp.concatenate([rim_rows, own_rows], axis=0), conv_weight[0])
    span_parts = span_terms(*head_major(active, beta_logit[0], gate_log[0]))
    identity_map = jnp.broadcast_to(jnp.eye(HK, dtype=jnp.float32), (HEAD_TOTAL, HK, HK))
    nothing = jnp.zeros((HEAD_TOTAL, HK, HK), jnp.float32)
    (total_map, total_add), _ = lax.scan(compose_step, (identity_map, nothing), span_parts)
    _, incoming = entering((total_map, total_add), "ctx", combine_pairs, (identity_map, nothing))
    _, outputs = lax.scan(advance, incoming, span_parts)
    outputs = outputs.transpose(0, 2, 1, 3).reshape(tok_count, HEAD_TOTAL, HK)
    normed = normalize(outputs, norm_gain[0])
    local_cols = w_out[0]
    mixed_rows = jnp.dot(
        normed,
        lax.all_gather(local_cols, "ctx", axis=1, tiled=True),
        preferred_element_type=jnp.float32,
    ).astype(jnp.bfloat16)
    return passed_along(mixed_rows[None], "section", 1)


def solution(mesh):
    placed = (
        P("section", "ctx", None),
        P("section", None, None),
        P("section", "ctx", None),
        P("section", "ctx", None),
        P("section", None),
        P("section", None, "ctx"),
    )
    return jax.shard_map(
        on_device, mesh=mesh, in_specs=placed, out_specs=P("section", "ctx", None), check_vma=False
    )
```

profile of v0, /device:TPU:24, one launch (start us, length us, event | category | flops | bytes accessed | tf_op | source)
XLA Modules:
  0.0 385.2 jit_solution(1799050040102169868)
XLA Ops:
  13.5 1.8 divide_multiply_fusion
  18.4 1.5 copy.89
  19.9 2.4 fusion.43
  22.3 157.9 %custom-call.4 = f32[8,2,1,128,128]{3,4,2,1,0:T(8,128)} custom-call(f32[8,2,1,128,128]{4,3,2,1,0:T(8,128)S(1)} %fusion.43), custom_call_target="InvertDiagBlocksLowerTriangular" | custom-call | tf_op jit(solution)/shard_map/jit(_solve_triangular)/vmap(vmap())/triangular_solve | solution.py:103
  180.2 1.9 broadcast_multiply_fusion
  182.1 2.0 fusion.35
  184.2 2.2 convolution_bitcast_fusion
  186.5 2.2 fusion.39
  188.9 2.9 while.40
  196.2 2.1 convolution_multiply_fusion.1
  198.4 1.9 convolution_bitcast_fusion.2
  201.3 36.9 %all-gather.7.cloned.1.call-done = f32[32,128,128]{2,1,0:T(8,128)} async-done(((f32[8,128,128]{2,1,0:T(8,128)}), f32[32,128,128]{2,1,0:T(8,128)}) %all-gather.7.cloned.1.call-update) | async-done | bytes 2097168 | tf_op jit(solution)/shard_map/all_gather | solution.py:24
  238.3 46.3 %all-gather.9.cloned.1.call-done = f32[32,128,128]{2,1,0:T(8,128)} async-done(((f32[8,128,128]{2,1,0:T(8,128)}), f32[32,128,128]{2,1,0:T(8,128)}) %all-gather.9.cloned.1.call-update) | async-done | bytes 2097168 | tf_op jit(solution)/shard_map/all_gather | solution.py:24
  284.5 5.8 %while.41 = (s32[]{:T(128)}, f32[8,128,128]{2,1,0:T(8,128)S(1)}, s32[]{:T(128)}, f32[4,8,128,128]{3,2,1,0:T(8,128)}, f32[4,8,128,128]{3,2,1,0:T(8,128)}, /*index=5*/s32[]{:T(128)}, s32[]{:T(128)}) while((s32[]{:T(128)}, f32[8,128,128]{2,1,0:T(8,128)S(1)}, s32[]{:T(128)}, f32[4,8,128,128]{3,2,1,0:T(8,128)}, ...), condition=%wide.region_5.6_spmd.clone, body=%wide.region_4.5_spmd.clone.sunk | while | flops 201850880 | bytes 3672671 | solution.py:33
  284.6 1.9 fusion.97
  286.5 1.9 fusion.97
  288.5 1.9 fusion.97
  290.4 6.0 %while.39 = (s32[]{:T(128)}, f32[8,128,128]{2,1,0:T(8,128)S(1)}, f32[2,8,64,128]{3,2,1,0:T(8,128)}, f32[2,8,128,128]{3,2,1,0:T(8,128)S(1)}, f32[2,8,128,128]{3,2...) while((s32[]{:T(128)}, f32[8,128,128]{2,1,0:T(8,128)S(1)}, ...), condition=%wide.region_8.9_spmd, body=%wide.region_7.8_spmd.sunk | while | flops 302186496 | bytes 4458581 | solution.py:174
  290.4 2.3 fusion.89
  293.4 2.3 fusion.89
  297.7 1.4 copy.105
  299.1 66.0 %all-gather.11.cloned.1.call-done = bf16[1,1024,2048]{2,1,0:T(8,128)(2,1)} async-done(((bf16[1,1024,512]{2,1,0:T(8,128)(2,1)}), bf16[1,1024,2048]{2,1,0:T(8,128)(2,1)}) %all-gather.11.cloned.1.call-update) | async-done | bytes 4194320 | tf_op jit(solution)/shard_map/all_gather | solution.py:180
  365.3 3.0 fusion.32
  368.4 9.5 %collective-permute-done.1 = bf16[1,128,2048]{2,1,0:T(8,128)(2,1)S(1)} collective-permute-done((bf16[1,128,2048]{2,1,0:T(8,128)(2,1)S(1)}, bf16[1,128,2048]{2,1,0:T(8,128)(2,1)S(1)}, u32[]{:S(2)}, u32[]{:S(2)}) %collective-permute-start.1) | collective-permute-done | bytes 524320 | tf_op jit(solution)/shard_map/ppermute | solution.py:39
  (99 shorter events, 22.2 us)
Async XLA Ops:
  6.5 6.9 %copy-start.7 = (bf16[1,128,5120]{2,1,0:T(8,128)(2,1)S(1)}, bf16[1,128,5120]{2,1,0:T(8,128)(2,1)}, u32[]{:S(2)}) copy-start(bf16[1,128,5120]{2,1,0:T(8,128)(2,1)} %param.12) | copy-start | bytes 3932164
  6.5 231.7 %all-gather.7.cloned.1.call-start = ((), (), s32[]{:S(2)}) async-start(), calls=%async_computation | async-start | bytes 2621440 | tf_op jit(solution)/shard_map/all_gather | solution.py:24
  7.6 5.9 %collective-permute-start = (bf16[3,5120]{1,0:T(4,128)(2,1)S(1)}, bf16[3,5120]{1,0:T(4,128)(2,1)S(1)}, u32[]{:S(2)}, u32[]{:S(2)}) collective-permute-start(bf16[3,5120]{1,0:T(4,128)(2,1)S(1)} %slice_bitcast_fusion.3), channel_id=1, source_target_pairs={{0,1},{1,2},{2,3},{4,5},{5,6},{6,7},{8,9},{9,10},{10,11},{12,13},{... | collective-permute-start | bytes 92168 | tf_op jit(solution)/shard_map/ppermute | solution.py:19
  15.3 1.5 copy-start.6
  18.2 168.3 %copy-start = (f32[8,128,2,128]{3,2,1,0:T(2,128)}, f32[8,128,2,128]{3,2,1,0:T(2,128)S(1)}, u32[]{:S(2)}) copy-start(f32[8,128,2,128]{3,2,1,0:T(2,128)S(1)} %copy.83) | copy-start | bytes 3145732
  180.2 1.9 copy-start.8
  184.1 2.3 copy-start.3
  191.7 0.8 copy-start.2
  191.8 1.0 copy-start.5
  192.6 92.0 %all-gather.9.cloned.1.call-start = ((), (), s32[]{:S(2)}) async-start(), calls=%async_computation.1 | async-start | bytes 2621440 | tf_op jit(solution)/shard_map/all_gather | solution.py:24
  193.3 171.7 %all-gather.11.cloned.1.call-start = ((), (), s32[]{:S(2)}) async-start(), calls=%async_computation.2 | async-start | bytes 5242880 | tf_op jit(solution)/shard_map/all_gather | solution.py:180
  194.3 1.9 copy-start.1
  195.7 2.7 copy-start.4
  290.3 74.9 %copy-start.9 = (f32[1,1024]{1,0:T(1,128)S(1)}, f32[1,1024]{1,0:T(1,128)}, u32[]{:S(2)}) copy-start(f32[1,1024]{1,0:T(1,128)} %param.16) | copy-start | bytes 12292
  368.3 9.6 %collective-permute-start.1 = (bf16[1,128,2048]{2,1,0:T(8,128)(2,1)S(1)}, bf16[1,128,2048]{2,1,0:T(8,128)(2,1)S(1)}, u32[]{:S(2)}, u32[]{:S(2)}) collective-permute-start(bf16[1,128,2048]{2,1,0:T(8,128)(2,1)S(1)} %fusion.32), channel_id=1, source_target_pairs={{0,4},{4,8},{8,12},{12,16},{16,20},{20,24},{24,28},{28,0},{1,5},{5... | collective-permute-start | bytes 1572872 | tf_op jit(solution)/shard_map/ppermute | solution.py:39
Sparse Core Ops, SparseCore 0:
  192.7 45.5 all-gather.6
  239.8 44.6 all-gather.8
  286.1 78.9 all-gather.10
where the time goes:
time: 390 us; the launch traced here: 385 us
  other arithmetic  167 us (43%)
  waiting for transfers between devices  160 us (41%)
  matrix products  31 us (8%)
  between operations  13.6 us (3%)
  local copies, waits for them, and re-layouts  11.8 us (3%)
    another operation x2, other arithmetic, span_terms(): jax.scipy.linalg.solve_triangular(unit_lower, right_sides, lower=True, un...  158 us
    all_gather x2, waiting for transfers between devices, entering(): pieces = jax.tree.map(lambda part: lax.all_gather(part, axis), value)  83.2 us
    all_gather x1, waiting for transfers between devices, on_device(): lax.all_gather(local_cols, 'ctx', axis=1, tiled=True)  66 us
    ppermute x1, waiting for transfers between devices, passed_along(): return lax.ppermute(value, axis, pairs)  9.45 us
  transfers between devices with their start and end apart: 5, of which 5 were waited for; matrix products, arithmetic and copies ran while one was open for 7% of the time, Pallas kernels for 0%

commit v1 on v0

v1 whole, which is shorter than its diff:
```python
import functools
import jax
import jax.numpy as jnp
from jax import lax
from jax.experimental import pallas as pl
from jax.experimental.pallas import tpu as pltpu
from jax.sharding import PartitionSpec as P

HK = 128
STEPS = 2
CONV = 4
LEVELS = (1, 2, 4, 8, 16, 32)
f32, bf16 = jnp.float32, jnp.bfloat16


def dot(a, b):
    return jnp.dot(a, b, preferred_element_type=f32)


def split(x):
    high = x.astype(bf16)
    return high, (x - high.astype(f32)).astype(bf16)


def dot3(a, b):
    ah, al = split(a)
    bh, bl = split(b)
    return dot(
        jnp.concatenate([ah, ah, al], axis=1), jnp.concatenate([bh, bl, bh], axis=0)
    )


def pair_rows(left, right):
    zero = jnp.zeros_like(left)
    return jnp.concatenate(
        [jnp.concatenate([left, zero], axis=1), jnp.concatenate([zero, right], axis=1)], axis=0
    )


def blockwise(x):
    return pair_rows(x[:, :HK], x[:, HK:])


def pick(table, lane):
    index = lax.broadcasted_iota(jnp.int32, table.shape, 1)
    return jnp.sum(jnp.where(index == lane, table, 0.0), axis=1, keepdims=True)


def terms_kernel(group, heads, *refs):
    xs, rims, taps = refs[0:5], refs[5:10], refs[10:15]
    beta_ref, gate_ref = refs[15:17]
    map_ref, add_ref, direct_ref, reach_ref = refs[17:21]
    ext = refs[21]
    toks = xs[0].shape[0]
    half = toks // 2
    step = pl.program_id(0)

    acts = []
    for part in range(5):
        ext[part, 8 - (CONV - 1) : 8] = rims[part][...].astype(f32)
        ext[part, 8:] = xs[part][...].astype(f32)
        total = None
        for tap in range(CONV):
            low = 8 - (CONV - 1) + tap
            term = taps[part][tap : tap + 1].astype(f32) * ext[part, low : low + toks]
            total = term if total is None else total + term
        acts.append(total * (1.0 / (1.0 + jnp.exp(-total))))

    virt = lax.broadcasted_iota(jnp.int32, (2 * half, toks), 0)
    tok = lax.broadcasted_iota(jnp.int32, (2 * half, toks), 1)
    virt_t = lax.broadcasted_iota(jnp.int32, (toks, 2 * half), 1)
    tok_t = lax.broadcasted_iota(jnp.int32, (toks, 2 * half), 0)
    gates = gate_ref[...]
    gates_t = gates.T
    steps = 1.0 / (1.0 + jnp.exp(-beta_ref[...]))
    sums, sums_t = [], []
    for u in range(2):
        inside = (tok >= u * half) & (tok - u * half <= virt % half)
        inside_t = (tok_t >= u * half) & (tok_t - u * half <= virt_t % half)
        sums.append(
            jnp.dot(inside.astype(f32), gates, precision=lax.Precision.HIGHEST, preferred_element_type=f32)
        )
        sums_t.append(
            jnp.dot(gates_t, inside_t.astype(f32), precision=lax.Precision.HIGHEST, preferred_element_type=f32)
        )

    size = 2 * half
    row = lax.broadcasted_iota(jnp.int32, (size, size), 0)
    col = lax.broadcasted_iota(jnp.int32, (size, size), 1)
    row_tok, col_tok = row % half, col % half
    strict = (col_tok < row_tok) | ((col_tok == row_tok) & (col < row))
    upto = (col_tok <= row_tok)[:half]
    eye = (row == col).astype(f32)
    same = row_tok == col_tok
    twice = lambda x: jnp.concatenate([x, x], axis=1)
    level_masks = [
        twice(
            ((row_tok // (2 * b)) == (col_tok // (2 * b)))
            & ((row_tok // b) % 2 == 1)
            & ((col_tok // b) % 2 == 0)
        )
        for b in LEVELS
    ]

    rows_of = lambda x, u: x[u * half : (u + 1) * half]
    work = []
    for i in range(group):
        head = step * group + i
        lanes = slice(i * HK, (i + 1) * HK)
        unit = lambda x: x * lax.rsqrt(jnp.sum(x * x, axis=-1, keepdims=True) + 1e-06)
        q = unit(acts[0][:, lanes])
        k0, k1 = unit(acts[1][:, lanes]), unit(acts[2][:, lanes])
        v0, v1 = acts[3][:, lanes], acts[4][:, lanes]
        b0, b1 = pick(steps, head), pick(steps, heads + head)
        for u in range(2):
            keys = jnp.concatenate([rows_of(k0, u), rows_of(k1, u)], axis=0)
            vals = jnp.concatenate([rows_of(v0, u), rows_of(v1, u)], axis=0)
            size_col = jnp.concatenate([rows_of(b0, u), rows_of(b1, u)], axis=0)
            c_col = pick(sums[u], head)
            index = lax.broadcasted_iota(jnp.int32, sums_t[u].shape, 0)
            c_row = jnp.sum(jnp.where(index == head, sums_t[u], 0.0), axis=0, keepdims=True)
            c_end = c_col[half - 1 : half]
            queries = rows_of(q, u)
            keys_t = keys.T
            gram = dot3(jnp.concatenate([keys, queries], axis=0), keys_t)
            damp = jnp.exp(jnp.minimum(c_col[:half] - c_row, 0.0))
            lower = jnp.where(
                strict, size_col * jnp.concatenate([damp, damp], axis=0) * gram[:size], 0.0
            )
            scores = jnp.where(upto, damp * gram[size:], 0.0)
            grown = jnp.exp(c_col)
            right = jnp.concatenate([size_col * vals, (size_col * grown) * keys], axis=1)
            to_end_t = keys_t * jnp.exp(c_end - c_row)
            outer = jnp.concatenate([to_end_t, scores], axis=0)
            work.append((lower, right, outer, queries * grown[:half], jnp.exp(c_end) * eye))

    lows, invs = [], []
    for i in range(group):
        low = jnp.concatenate([work[2 * i][0], work[2 * i + 1][0]], axis=1)
        lows.append(low.astype(bf16))
        invs.append((twice(eye) - jnp.where(twice(same), low, 0.0)).astype(bf16))
    for mask in level_masks:
        inner = [
            dot(jnp.where(mask, lows[i], jnp.zeros_like(lows[i])), blockwise(invs[i])).astype(bf16)
            for i in range(group)
        ]
        invs = [
            invs[i] - dot(invs[i], blockwise(inner[i])).astype(bf16) for i in range(group)
        ]

    results = []
    for i in range(group):
        for u in range(2):
            lower, right, outer, reach0, map0 = work[2 * i + u]
            inv = invs[i][:, u * HK : (u + 1) * HK]
            first = dot(inv, right.astype(bf16))
            rest = right - first - dot3(lower, first)
            solved = first + dot(inv, rest.astype(bf16))
            both = dot3(outer, solved)
            results.append(
                (
                    map0 - both[:size, HK:],
                    both[:size, :HK],
                    both[size:, :HK],
                    reach0 - both[size:, HK:],
                )
            )
    for i in range(group):
        map1, add1, direct1, reach1 = results[2 * i]
        map2, add2, direct2, reach2 = results[2 * i + 1]
        joined = dot3(
            jnp.concatenate([map2, reach2], axis=0), jnp.concatenate([map1, add1], axis=1)
        )
        lanes = slice(i * HK, (i + 1) * HK)
        map_ref[i] = joined[:size, :HK]
        add_ref[i] = joined[:size, HK:] + add2
        direct_ref[:half, lanes] = direct1
        direct_ref[half:, lanes] = joined[size:, HK:] + direct2
        reach_ref[:half, lanes] = reach1
        reach_ref[half:, lanes] = joined[size:, :HK]


def shard_terms(streams, rim, conv_weight, beta_logit, gate_log, group=4):
    toks, channels = streams.shape
    heads = gate_log.shape[1]
    width = group * HK
    blocks = heads // group
    spec = lambda rows, part: pl.BlockSpec((rows, width), lambda g, part=part: (0, part * blocks + g))
    whole = lambda x: pl.BlockSpec(x.shape, lambda g: (0,) * x.ndim)
    flops = 60 * heads * 2 * 128 * 128 * 256
    return pl.pallas_call(
        functools.partial(terms_kernel, group, heads),
        grid=(blocks,),
        in_specs=[spec(toks, p) for p in range(5)]
        + [spec(rim.shape[0], p) for p in range(5)]
        + [spec(conv_weight.shape[0], p) for p in range(5)]
        + [whole(beta_logit), whole(gate_log)],
        out_specs=[
            pl.BlockSpec((group, HK, HK), lambda g: (g, 0, 0)),
            pl.BlockSpec((group, HK, HK), lambda g: (g, 0, 0)),
            pl.BlockSpec((toks, width), lambda g: (0, g)),
            pl.BlockSpec((toks, width), lambda g: (0, g)),
        ],
        out_shape=[
            jax.ShapeDtypeStruct((heads, HK, HK), f32),
            jax.ShapeDtypeStruct((heads, HK, HK), f32),
            jax.ShapeDtypeStruct((toks, heads * HK), f32),
            jax.ShapeDtypeStruct((toks, heads * HK), f32),
        ],
        scratch_shapes=[pltpu.VMEM((5, 8 + toks, width), f32)],
        compiler_params=pltpu.CompilerParams(vmem_limit_bytes=48 * 2**20),
        cost_estimate=pl.CostEstimate(flops=flops, bytes_accessed=4 * 2**20, transcendentals=0),
    )(*[streams] * 5, *[rim] * 5, *[conv_weight] * 5, beta_logit, gate_log)


def hand_on_kernel(map_ref, add_ref, state_ref, out_ref):
    for head in range(map_ref.shape[0]):
        high, low = split(map_ref[head])
        state = state_ref[head]
        grown = dot(
            jnp.concatenate([high, low], axis=1), jnp.concatenate([state, state], axis=0)
        )
        out_ref[head] = (grown + add_ref[head]).astype(bf16)


def hand_on(total_map, total_add, state):
    heads = total_map.shape[0]
    return pl.pallas_call(
        hand_on_kernel,
        out_shape=jax.ShapeDtypeStruct(state.shape, bf16),
        compiler_params=pltpu.CompilerParams(vmem_limit_bytes=16 * 2**20),
        cost_estimate=pl.CostEstimate(
            flops=4 * heads * HK**3, bytes_accessed=heads * HK * HK * 12, transcendentals=0
        ),
    )(total_map, total_add, state)


def project_kernel(count, *refs):
    states = refs[: count - 1]
    direct_ref, reach_ref, gain_ref, own_ref = refs[count - 1 : count + 3]
    rights = refs[count + 3 : 2 * count + 2]
    lefts = refs[2 * count + 2 : 3 * count + 1]
    out_ref, slots, sems = refs[3 * count + 1 :]
    mine = lax.axis_index("ctx")
    heads = states[0].shape[0]
    cols = own_ref.shape[1]

    def copy(source, slot):
        return pltpu.make_async_copy(source, slots.at[slot], sems.at[slot])

    copy(own_ref, 0).start()
    for turn in range(1, count):
        pl.when(mine >= turn)(lambda: copy(rights[turn - 1], turn).start())
        pl.when(mine < turn)(lambda: copy(lefts[count - turn - 1], turn).start())
    parts = []
    for head in range(heads):
        lanes = slice(head * HK, (head + 1) * HK)
        state = states[0][head]
        for other in states[1:]:
            state = state + other[head]
        high, low = split(reach_ref[:, lanes])
        out = direct_ref[:, lanes] + dot(
            jnp.concatenate([high, low], axis=1), jnp.concatenate([state, state], axis=0)
        )
        inverse = lax.rsqrt(jnp.mean(out * out, axis=-1, keepdims=True) + 1e-05)
        parts.append((out * inverse * gain_ref[:, lanes]).astype(bf16))
    normed = jnp.concatenate(parts, axis=1)
    for turn in range(count):
        copy(own_ref, turn).wait()
        owner = lax.rem(mine + count - turn, count)
        place = pl.ds(pl.multiple_of(owner * cols, HK), cols)
        out_ref[:, place] = dot(normed, slots[turn]).astype(bf16)


def project(states, direct, reach, gain, own, rights, lefts):
    count = len(states) + 1
    toks, width = direct.shape
    cols = own.shape[1]
    vmem = pl.BlockSpec(memory_space=pltpu.VMEM)
    hbm = pl.BlockSpec(memory_space=pl.ANY)
    return pl.pallas_call(
        functools.partial(project_kernel, count),
        in_specs=[vmem] * (count - 1) + [vmem] * 3 + [hbm] * (2 * count - 1),
        out_specs=vmem,
        out_shape=jax.ShapeDtypeStruct((toks, count * cols), bf16),
        scratch_shapes=[
            pltpu.VMEM((count, width, cols), bf16),
            pltpu.SemaphoreType.DMA((count,)),
        ],
        compiler_params=pltpu.CompilerParams(vmem_limit_bytes=32 * 2**20),
        cost_estimate=pl.CostEstimate(
            flops=2 * toks * width * count * cols,
            bytes_accessed=2 * width * count * cols,
            transcendentals=0,
        ),
    )(*states, direct, reach, gain, own, *rights, *lefts)


def moved(value, pairs):
    return lax.ppermute(value, "ctx", pairs)


def on_device(streams, conv_weight, beta_logit, gate_log, norm_gain, w_out):
    count = lax.axis_size("ctx")
    toks = streams.shape[1]
    rim = moved(streams[0, toks - (CONV - 1) :], [(c, c + 1) for c in range(count - 1)])
    rights, lefts = [w_out[0]], [w_out[0]]
    for turn in range(1, count):
        rights.append(moved(rights[-1], [(c, c + 1) for c in range(turn - 1, count - 1)]))
        lefts.append(moved(lefts[-1], [(c, c - 1) for c in range(1, count - turn + 1)]))
    total_map, total_add, direct, reach = shard_terms(
        streams[0], rim, conv_weight[0], beta_logit[0], gate_log[0]
    )
    states = [moved(total_add.astype(bf16), [(0, 1)])]
    for turn in range(1, count - 1):
        states.append(moved(hand_on(total_map, total_add, states[-1]), [(turn, turn + 1)]))
    mixed = project(states, direct, reach, norm_gain, w_out[0], rights[1:], lefts[1:])
    sections = lax.axis_size("section")
    return lax.ppermute(
        mixed[None], "section", [(s, (s + 1) % sections) for s in range(sections)]
    )


def solution(mesh):
    placed = (
        P("section", "ctx", None),
        P("section", None, None),
        P("section", "ctx", None),
        P("section", "ctx", None),
        P("section", None),
        P("section", None, "ctx"),
    )
    return jax.shard_map(
        on_device, mesh=mesh, in_specs=placed, out_specs=P("section", "ctx", None), check_vma=False
    )
```

time: 390 us -> 110 us (0.28); the launches traced: 385 us -> 109 us
  other arithmetic: 167 us -> 0.04 us
  waiting for transfers between devices: 160 us -> 71.1 us
  matrix products: 31 us -> 0 us
  Pallas kernels: 0 us -> 17.8 us
  between operations: 13.6 us -> 0.2 us
  starting transfers between devices: 1.7 us -> 15 us
  local copies, waits for them, and re-layouts: 11.8 us -> 5.39 us
    another operation x3 -> x0, other arithmetic: 158 us -> none  [the longest x2 158 us: span_terms(): jax.scipy.linalg.solve_triangular(unit_lower, right_sides, lower=True, un...]
    all_gather x3 -> x0, waiting for transfers between devices: 149 us -> none  [the longest x2 83.2 us: entering(): pieces = jax.tree.map(lambda part: lax.all_gather(part, axis), value)]
    ppermute x2 -> x11, waiting for transfers between devices: 9.82 us -> 71.1 us  [the longest x10 61.6 us: moved(): return lax.ppermute(value, 'ctx', pairs)]
    dot_general x18 -> x0, matrix products: 29 us -> none  [the longest x3 5.62 us: combine_pairs(): jnp.einsum('hde,hef->hdf', second_map, first_add, precision=highest)]
    pallas_call x0 -> x4, Pallas kernels: none -> 17.8 us  [the longest x1 15.3 us: shard_terms(): pl.pallas_call(functools.partial(terms_kernel, group, heads), grid=(block...]
    ppermute x2 -> x11, starting transfers between devices: 1.4 us -> 15 us  [the longest x10 14.9 us: moved(): return lax.ppermute(value, 'ctx', pairs)]
  transfers between devices with their start and end apart: 5 -> 11, of which waited for: 5 -> 4; matrix products, arithmetic and copies ran while one was open for 7% -> 2% of each run, Pallas kernels for 0% -> 14%
where the time goes in v1:
time: 110 us; the launch traced here: 109 us
  waiting for transfers between devices  71.1 us (65%)
  Pallas kernels  17.8 us (16%)
  starting transfers between devices  15 us (14%)
  local copies, waits for them, and re-layouts  5.39 us (5%)
    ppermute x10, waiting for transfers between devices, moved(): return lax.ppermute(value, 'ctx', pairs)  61.6 us
    pallas_call x1, Pallas kernels, shard_terms(): pl.pallas_call(functools.partial(terms_kernel, group, heads), grid=(block...  15.3 us
    ppermute x10, starting transfers between devices, moved(): return lax.ppermute(value, 'ctx', pairs)  14.9 us
    ppermute x1, waiting for transfers between devices, on_device(): lax.ppermute(mixed[None], 'section', [(s, (s + 1) % sections) for s in ra...  9.49 us
    unnamed x11, local copies, waits for them, and re-layouts  4.48 us
  transfers between devices with their start and end apart: 11, of which 4 were waited for; matrix products, arithmetic and copies ran while one was open for 2% of the time, Pallas kernels for 14%

profile of v1, /device:TPU:24, one launch (start us, length us, event | category | flops | bytes accessed | tf_op | source)
XLA Modules:
  0.0 109.5 jit_solution(18151815118170653389)
XLA Ops:
  0.0 1.3 %collective-permute-start.4 = (bf16[1024,512]{1,0:T(8,128)(2,1)}, bf16[1024,512]{1,0:T(8,128)(2,1)S(1)}, u32[]{:S(2)}, u32[]{:S(2)}) collective-permute-start(bf16[1024,512]{1,0:T(8,128)(2,1)} %bitcast.8), channel_id=1, source_target_pairs={{0,1},{1,2},{2,3},{4,5},{5,6},{6,7},{8,9},{9,10},{10,11},{12,13},{... | collective-permute-start | bytes 3145736 | tf_op jit(solution)/shard_map/ppermute | solution.py:300
  1.3 4.6 %collective-permute-start.7 = (bf16[1024,512]{1,0:T(8,128)(2,1)}, bf16[1024,512]{1,0:T(8,128)(2,1)S(1)}, u32[]{:S(2)}, u32[]{:S(2)}) collective-permute-start(bf16[1024,512]{1,0:T(8,128)(2,1)} %bitcast.9), channel_id=1, source_target_pairs={{1,0},{2,1},{3,2},{5,4},{6,5},{7,6},{9,8},{10,9},{11,10},{13,12},{... | collective-permute-start | bytes 3145736 | tf_op jit(solution)/shard_map/ppermute | solution.py:300
  5.9 21.1 %collective-permute-done.4.refs_7_ = bf16[1024,512]{1,0:T(8,128)(2,1)S(1)} collective-permute-done((bf16[1024,512]{1,0:T(8,128)(2,1)}, bf16[1024,512]{1,0:T(8,128)(2,1)S(1)}, u32[]{:S(2)}, u32[]{:S(2)}) %collective-permute-start.4) | collective-permute-done | bytes 1048608 | tf_op jit(solution)/shard_map/ppermute | solution.py:300
  27.0 1.3 %collective-permute-start.5 = (bf16[1024,512]{1,0:T(8,128)(2,1)S(1)}, bf16[1024,512]{1,0:T(8,128)(2,1)S(1)}, u32[]{:S(2)}, u32[]{:S(2)}) collective-permute-start(bf16[1024,512]{1,0:T(8,128)(2,1)S(1)} %collective-permute-done.4.refs_7_), channel_id=1, source_target_pairs={{1,2},{2,3},{5,6},{6,7},{9,10},{10,11},{13,14},{14,15},{17,18},{18... | collective-permute-start | bytes 3145736 | tf_op jit(solution)/shard_map/ppermute | solution.py:300
  28.3 1.6 %collective-permute-start.8 = (bf16[1024,512]{1,0:T(8,128)(2,1)S(1)}, bf16[1024,512]{1,0:T(8,128)(2,1)}, u32[]{:S(2)}, u32[]{:S(2)}) collective-permute-start(bf16[1024,512]{1,0:T(8,128)(2,1)S(1)} %collective-permute-done.7.refs_10_), channel_id=1, source_target_pairs={{1,0},{2,1},{5,4},{6,5},{9,8},{10,9},{13,12},{14,13},{17,16},{18,1... | collective-permute-start | bytes 3145736 | tf_op jit(solution)/shard_map/ppermute | solution.py:300
  29.9 0.9 slice_bitcast_fusion
  30.9 1.3 %collective-permute-start = (bf16[3,5120]{1,0:T(4,128)(2,1)S(1)}, bf16[3,5120]{1,0:T(4,128)(2,1)S(1)}, u32[]{:S(2)}, u32[]{:S(2)}) collective-permute-start(bf16[3,5120]{1,0:T(4,128)(2,1)S(1)} %slice_bitcast_fusion), channel_id=1, source_target_pairs={{0,1},{1,2},{2,3},{4,5},{5,6},{6,7},{8,9},{9,10},{10,11},{12,13},{... | collective-permute-start | bytes 92168 | tf_op jit(solution)/shard_map/ppermute | solution.py:300
  32.2 0.8 copy.7
  33.0 0.8 copy.8
  33.7 19.6 %collective-permute-done.5.refs_8_ = bf16[1024,512]{1,0:T(8,128)(2,1)S(1)} collective-permute-done((bf16[1024,512]{1,0:T(8,128)(2,1)S(1)}, bf16[1024,512]{1,0:T(8,128)(2,1)S(1)}, u32[]{:S(2)}, u32[]{:S(2)}) %collective-permute-start.5) | collective-permute-done | bytes 1048608 | tf_op jit(solution)/shard_map/ppermute | solution.py:300
  53.3 1.3 %collective-permute-start.6 = (bf16[1024,512]{1,0:T(8,128)(2,1)S(1)}, bf16[1024,512]{1,0:T(8,128)(2,1)S(1)}, u32[]{:S(2)}, u32[]{:S(2)}) collective-permute-start(bf16[1024,512]{1,0:T(8,128)(2,1)S(1)} %collective-permute-done.5.refs_8_), channel_id=1, source_target_pairs={{2,3},{6,7},{10,11},{14,15},{18,19},{22,23},{26,27},{30,31}} | collective-permute-start | bytes 3145736 | tf_op jit(solution)/shard_map/ppermute | solution.py:300
  54.6 0.7 collective-permute-start.9
  55.4 1.3 %copy-done.2 = bf16[1,128,5120]{2,1,0:T(8,128)(2,1)S(1)} copy-done((bf16[1,128,5120]{2,1,0:T(8,128)(2,1)S(1)}, bf16[1,128,5120]{2,1,0:T(8,128)(2,1)}, u32[]{:S(2)}) %copy-start.2) | copy-done | bytes 1310744
  56.7 0.8 copy-done.3
  57.5 15.3 %shard_map.64 = (f32[8,128,128]{2,1,0:T(8,128)S(1)}, f32[8,128,128]{2,1,0:T(8,128)S(1)}, f32[128,1024]{1,0:T(8,128)S(1)}, f32[128,1024]{1,0:T(8,128)S(1)}) custom-call(bf16[128,5120]{1,0:T(8,128)(2,1)S(1)} %bitcast.14, bf16[128,5120]{1,0:T(8,128)(2,1)S(1)} %bitcast.15, bf16[128,5120]{1,0:T(8,128)(2,1)S(1)} %bitcast.16, bf16[128,5120]{1,0:T(8,128)(2,1)S(1)} %bitcast.17, ...), custom_call_target="tpu_custom_call" | custom-call | flops 4026531840 | bytes 4194304 | tf_op jit(solution)/shard_map/pallas_call | solution.py:191
  72.8 0.7 collective-permute-start.1
  73.5 0.3 shard_map.65
  73.8 0.8 collective-permute-start.2
  74.6 0.3 shard_map.66
  74.9 1.3 %collective-permute-start.3 = (bf16[8,128,128]{2,1,0:T(8,128)(2,1)S(1)}, bf16[8,128,128]{2,1,0:T(8,128)(2,1)S(1)}, u32[]{:S(2)}, u32[]{:S(2)}) collective-permute-start(bf16[8,128,128]{2,1,0:T(8,128)(2,1)S(1)} %shard_map.66), channel_id=1, source_target_pairs={{2,3},{6,7},{10,11},{14,15},{18,19},{22,23},{26,27},{30,31}} | collective-permute-start | bytes 786440 | tf_op jit(solution)/shard_map/ppermute | solution.py:300
  76.2 20.9 %collective-permute-done.3.refs_2_ = bf16[8,128,128]{2,1,0:T(8,128)(2,1)S(1)} collective-permute-done((bf16[8,128,128]{2,1,0:T(8,128)(2,1)S(1)}, bf16[8,128,128]{2,1,0:T(8,128)(2,1)S(1)}, u32[]{:S(2)}, u32[]{:S(2)}) %collective-permute-start.3) | collective-permute-done | bytes 262176 | tf_op jit(solution)/shard_map/ppermute | solution.py:300
  97.1 2.0 %shard_map.67 = bf16[128,2048]{1,0:T(8,128)(2,1)S(1)} custom-call(bf16[8,128,128]{2,1,0:T(8,128)(2,1)S(1)} %collective-permute-done.1.state_ref.refs_0_, bf16[8,128,128]{2,1,0:T(8,128)(2,1)S(1)} %collective-permute-done.2.state_ref.refs_1_, bf16[8,128,128]{2,1,0:T(8,128)(2,1)S(1)} %collective-permute-done.3.refs_2_, ...), custom_call_target="tpu_custom_call" | custom-call | flops 536870912 | bytes 4194304 | tf_op jit(solution)/shard_map/pallas_call | solution.py:281
  99.2 9.5 %collective-permute-done.10 = bf16[1,128,2048]{2,1,0:T(8,128)(2,1)S(1)} collective-permute-done((bf16[1,128,2048]{2,1,0:T(8,128)(2,1)S(1)}, bf16[1,128,2048]{2,1,0:T(8,128)(2,1)S(1)}, u32[]{:S(2)}, u32[]{:S(2)}) %collective-permute-start.10) | collective-permute-done | bytes 524320 | tf_op jit(solution)/shard_map/ppermute | solution.py:319
  108.7 0.8 copy.10
  (15 shorter events, 0.1 us)
Async XLA Ops:
  0.0 27.0 %collective-permute-start.4 = (bf16[1024,512]{1,0:T(8,128)(2,1)}, bf16[1024,512]{1,0:T(8,128)(2,1)S(1)}, u32[]{:S(2)}, u32[]{:S(2)}) collective-permute-start(bf16[1024,512]{1,0:T(8,128)(2,1)} %bitcast.8), channel_id=1, source_target_pairs={{0,1},{1,2},{2,3},{4,5},{5,6},{6,7},{8,9},{9,10},{10,11},{12,13},{... | collective-permute-start | bytes 3145736 | tf_op jit(solution)/shard_map/ppermute | solution.py:300
  1.3 27.0 %collective-permute-start.7 = (bf16[1024,512]{1,0:T(8,128)(2,1)}, bf16[1024,512]{1,0:T(8,128)(2,1)S(1)}, u32[]{:S(2)}, u32[]{:S(2)}) collective-permute-start(bf16[1024,512]{1,0:T(8,128)(2,1)} %bitcast.9), channel_id=1, source_target_pairs={{1,0},{2,1},{3,2},{5,4},{6,5},{7,6},{9,8},{10,9},{11,10},{13,12},{... | collective-permute-start | bytes 3145736 | tf_op jit(solution)/shard_map/ppermute | solution.py:300
  27.0 26.3 %collective-permute-start.5 = (bf16[1024,512]{1,0:T(8,128)(2,1)S(1)}, bf16[1024,512]{1,0:T(8,128)(2,1)S(1)}, u32[]{:S(2)}, u32[]{:S(2)}) collective-permute-start(bf16[1024,512]{1,0:T(8,128)(2,1)S(1)} %collective-permute-done.4.refs_7_), channel_id=1, source_target_pairs={{1,2},{2,3},{5,6},{6,7},{9,10},{10,11},{13,14},{14,15},{17,18},{18... | collective-permute-start | bytes 3145736 | tf_op jit(solution)/shard_map/ppermute | solution.py:300
  28.3 26.3 %collective-permute-start.8 = (bf16[1024,512]{1,0:T(8,128)(2,1)S(1)}, bf16[1024,512]{1,0:T(8,128)(2,1)}, u32[]{:S(2)}, u32[]{:S(2)}) collective-permute-start(bf16[1024,512]{1,0:T(8,128)(2,1)S(1)} %collective-permute-done.7.refs_10_), channel_id=1, source_target_pairs={{1,0},{2,1},{5,4},{6,5},{9,8},{10,9},{13,12},{14,13},{17,16},{18,1... | collective-permute-start | bytes 3145736 | tf_op jit(solution)/shard_map/ppermute | solution.py:300
  30.9 24.5 %collective-permute-start = (bf16[3,5120]{1,0:T(4,128)(2,1)S(1)}, bf16[3,5120]{1,0:T(4,128)(2,1)S(1)}, u32[]{:S(2)}, u32[]{:S(2)}) collective-permute-start(bf16[3,5120]{1,0:T(4,128)(2,1)S(1)} %slice_bitcast_fusion), channel_id=1, source_target_pairs={{0,1},{1,2},{2,3},{4,5},{5,6},{6,7},{8,9},{9,10},{10,11},{12,13},{... | collective-permute-start | bytes 92168 | tf_op jit(solution)/shard_map/ppermute | solution.py:300
  53.3 43.8 %collective-permute-start.6 = (bf16[1024,512]{1,0:T(8,128)(2,1)S(1)}, bf16[1024,512]{1,0:T(8,128)(2,1)S(1)}, u32[]{:S(2)}, u32[]{:S(2)}) collective-permute-start(bf16[1024,512]{1,0:T(8,128)(2,1)S(1)} %collective-permute-done.5.refs_8_), channel_id=1, source_target_pairs={{2,3},{6,7},{10,11},{14,15},{18,19},{22,23},{26,27},{30,31}} | collective-permute-start | bytes 3145736 | tf_op jit(solution)/shard_map/ppermute | solution.py:300
  54.6 42.5 %collective-permute-start.9 = (bf16[1024,512]{1,0:T(8,128)(2,1)}, bf16[1024,512]{1,0:T(8,128)(2,1)S(1)}, u32[]{:S(2)}, u32[]{:S(2)}) collective-permute-start(bf16[1024,512]{1,0:T(8,128)(2,1)} %collective-permute-done.8.refs_11_), channel_id=1, source_target_pairs={{1,0},{5,4},{9,8},{13,12},{17,16},{21,20},{25,24},{29,28}} | collective-permute-start | bytes 3145736 | tf_op jit(solution)/shard_map/ppermute | solution.py:300
  55.4 1.3 %copy-start.2 = (bf16[1,128,5120]{2,1,0:T(8,128)(2,1)S(1)}, bf16[1,128,5120]{2,1,0:T(8,128)(2,1)}, u32[]{:S(2)}) copy-start(bf16[1,128,5120]{2,1,0:T(8,128)(2,1)} %param.6) | copy-start | bytes 3932164
  56.7 0.8 copy-start.3
  72.8 0.7 collective-permute-start.1
  73.5 23.6 %copy-start = (bf16[1,1024,512]{2,1,0:T(8,128)(2,1)S(1)}, bf16[1,1024,512]{2,1,0:T(8,128)(2,1)}, u32[]{:S(2)}) copy-start(bf16[1,1024,512]{2,1,0:T(8,128)(2,1)} %param.11) | copy-start | bytes 3145732
  73.5 23.6 %copy-start.1 = (f32[1,1024]{1,0:T(1,128)S(1)}, f32[1,1024]{1,0:T(1,128)}, u32[]{:S(2)}) copy-start(f32[1,1024]{1,0:T(1,128)} %refs_5_.1) | copy-start | bytes 12292
  73.8 0.8 collective-permute-start.2
  74.9 22.2 %collective-permute-start.3 = (bf16[8,128,128]{2,1,0:T(8,128)(2,1)S(1)}, bf16[8,128,128]{2,1,0:T(8,128)(2,1)S(1)}, u32[]{:S(2)}, u32[]{:S(2)}) collective-permute-start(bf16[8,128,128]{2,1,0:T(8,128)(2,1)S(1)} %shard_map.66), channel_id=1, source_target_pairs={{2,3},{6,7},{10,11},{14,15},{18,19},{22,23},{26,27},{30,31}} | collective-permute-start | bytes 786440 | tf_op jit(solution)/shard_map/ppermute | solution.py:300
  99.1 9.6 %collective-permute-start.10 = (bf16[1,128,2048]{2,1,0:T(8,128)(2,1)S(1)}, bf16[1,128,2048]{2,1,0:T(8,128)(2,1)S(1)}, u32[]{:S(2)}, u32[]{:S(2)}) collective-permute-start(bf16[1,128,2048]{2,1,0:T(8,128)(2,1)S(1)} %bitcast.11), channel_id=1, source_target_pairs={{0,4},{4,8},{8,12},{12,16},{16,20},{20,24},{24,28},{28,0},{1,5},{5... | collective-permute-start | bytes 1572872 | tf_op jit(solution)/shard_map/ppermute | solution.py:319

commit v2 on v1

v2 whole, which is shorter than its diff:
```python
import functools
import jax
import jax.numpy as jnp
from jax import lax
from jax.experimental import pallas as pl
from jax.experimental.pallas import tpu as pltpu
from jax.sharding import PartitionSpec as P

HK = 128
STEPS = 2
CONV = 4
LEVELS = (1, 2, 4, 8, 16, 32)
f32, bf16 = jnp.float32, jnp.bfloat16


def dot(a, b):
    return jnp.dot(a, b, preferred_element_type=f32)


def split(x):
    high = x.astype(bf16)
    return high, (x - high.astype(f32)).astype(bf16)


def dot3(a, b):
    ah, al = split(a)
    bh, bl = split(b)
    return dot(
        jnp.concatenate([ah, ah, al], axis=1), jnp.concatenate([bh, bl, bh], axis=0)
    )


def pair_rows(left, right):
    zero = jnp.zeros_like(left)
    return jnp.concatenate(
        [jnp.concatenate([left, zero], axis=1), jnp.concatenate([zero, right], axis=1)], axis=0
    )


def blockwise(x):
    return pair_rows(x[:, :HK], x[:, HK:])


def pick(table, lane):
    index = lax.broadcasted_iota(jnp.int32, table.shape, 1)
    return jnp.sum(jnp.where(index == lane, table, 0.0), axis=1, keepdims=True)


def half_terms(u, heads, half, acts, beta_t, gate_t):
    size, toks = STEPS * half, 2 * half
    virt = lax.broadcasted_iota(jnp.int32, (size, toks), 0)
    tok = lax.broadcasted_iota(jnp.int32, (size, toks), 1)
    inside = ((tok >= u * half) & (tok - u * half <= virt % half)).astype(f32)
    exact = dict(precision=lax.Precision.HIGHEST, preferred_element_type=f32)
    over_lanes = (((1,), (1,)), ((), ()))
    sums = lax.dot_general(inside, gate_t, over_lanes, **exact)
    sums_t = lax.dot_general(gate_t, inside, over_lanes, **exact)
    steps = (1.0 / (1.0 + jnp.exp(-beta_t))).T[u * half : (u + 1) * half]

    row = lax.broadcasted_iota(jnp.int32, (size, size), 0)
    col = lax.broadcasted_iota(jnp.int32, (size, size), 1)
    row_tok, col_tok = row % half, col % half
    strict = (col_tok < row_tok) | ((col_tok == row_tok) & (col < row))
    upto = (col_tok <= row_tok)[:half]
    eye = (row == col).astype(f32)
    same = row_tok == col_tok
    twice = lambda x: jnp.concatenate([x, x], axis=1)
    level_masks = [
        twice(
            ((row_tok // (2 * b)) == (col_tok // (2 * b)))
            & ((row_tok // b) % 2 == 1)
            & ((col_tok // b) % 2 == 0)
        )
        for b in LEVELS
    ]

    work = []
    for head in range(heads):
        lanes = slice(head * HK, (head + 1) * HK)
        unit = lambda x: x * lax.rsqrt(jnp.sum(x * x, axis=-1, keepdims=True) + 1e-06)
        queries = unit(acts[0][:, lanes])
        keys = unit(jnp.concatenate([acts[1][:, lanes], acts[2][:, lanes]], axis=0))
        vals = jnp.concatenate([acts[3][:, lanes], acts[4][:, lanes]], axis=0)
        size_col = jnp.concatenate([pick(steps, head), pick(steps, heads + head)], axis=0)
        c_col = pick(sums, head)
        c_row = sums_t[head : head + 1]
        c_end = c_col[half - 1 : half]
        keys_t = keys.T
        gram = dot3(jnp.concatenate([keys, queries], axis=0), keys_t)
        damp = jnp.exp(jnp.minimum(c_col[:half] - c_row, 0.0))
        lower = jnp.where(
            strict, size_col * jnp.concatenate([damp, damp], axis=0) * gram[:size], 0.0
        )
        scores = jnp.where(upto, damp * gram[size:], 0.0)
        grown = jnp.exp(c_col)
        right = jnp.concatenate([size_col * vals, (size_col * grown) * keys], axis=1)
        to_end_t = keys_t * jnp.exp(c_end - c_row)
        outer = jnp.concatenate([to_end_t, scores], axis=0)
        work.append((lower, right, outer, queries * grown[:half], jnp.exp(c_end) * eye))

    pairs = range(heads // 2)
    lows, invs = [], []
    for i in pairs:
        low = jnp.concatenate([work[2 * i][0], work[2 * i + 1][0]], axis=1)
        lows.append(low.astype(bf16))
        invs.append((twice(eye) - jnp.where(twice(same), low, 0.0)).astype(bf16))
    for mask in level_masks:
        inner = [
            dot(jnp.where(mask, lows[i], jnp.zeros_like(lows[i])), blockwise(invs[i])).astype(bf16)
            for i in pairs
        ]
        invs = [invs[i] - dot(invs[i], blockwise(inner[i])).astype(bf16) for i in pairs]

    results = []
    for head in range(heads):
        lower, right, outer, reach0, map0 = work[head]
        inv = invs[head // 2][:, head % 2 * HK : (head % 2 + 1) * HK]
        first = dot(inv, right.astype(bf16))
        rest = right - first - dot3(lower, first)
        solved = first + dot(inv, rest.astype(bf16))
        both = dot3(outer, solved)
        results.append(
            (
                map0 - both[:size, HK:],
                both[:size, :HK],
                both[size:, :HK],
                reach0 - both[size:, HK:],
            )
        )
    return results


def activations(ext, taps_ref, half, heads):
    width = heads * HK
    acts = []
    for part in range(5):
        lanes = slice(part * width, (part + 1) * width)
        total = None
        for tap in range(CONV):
            low = 8 - (CONV - 1) + tap
            term = taps_ref[tap : tap + 1, lanes].astype(f32) * ext[low : low + half, lanes]
            total = term if total is None else total + term
        acts.append(total * (1.0 / (1.0 + jnp.exp(-total))))
    return acts


def later_kernel(x_ref, taps_ref, beta_ref, gate_ref, map_ref, add_ref, direct_ref, reach_ref, ext):
    heads, toks = gate_ref.shape
    half = toks // 2
    ext[...] = x_ref[half - 16 :].astype(f32)[8:]
    acts = activations(ext, taps_ref, half, heads)
    found = half_terms(1, heads, half, acts, beta_ref[...], gate_ref[...])
    for head, (map2, add2, direct2, reach2) in enumerate(found):
        lanes = slice(head * HK, (head + 1) * HK)
        map_ref[head] = map2
        add_ref[head] = add2
        direct_ref[:, lanes] = direct2
        reach_ref[:, lanes] = reach2


def earlier_kernel(
    x_ref, rim_ref, taps_ref, beta_ref, gate_ref, map2_ref, add2_ref, direct2_ref, reach2_ref,
    map_ref, add_ref, sent_ref, direct_ref, reach_ref, ext,
):
    heads, toks = gate_ref.shape
    half = toks // 2
    ext[8 - (CONV - 1) : 8] = rim_ref[...].astype(f32)
    ext[8:] = x_ref[:half].astype(f32)
    acts = activations(ext, taps_ref, half, heads)
    found = half_terms(0, heads, half, acts, beta_ref[...], gate_ref[...])
    for head, (map1, add1, direct1, reach1) in enumerate(found):
        lanes = slice(head * HK, (head + 1) * HK)
        joined = dot3(
            jnp.concatenate([map2_ref[head], reach2_ref[:, lanes]], axis=0),
            jnp.concatenate([map1, add1], axis=1),
        )
        total = joined[:HK, HK:] + add2_ref[head]
        map_ref[head] = joined[:HK, :HK]
        add_ref[head] = total
        sent_ref[head] = total.astype(bf16)
        direct_ref[:half, lanes] = direct1
        direct_ref[half:, lanes] = joined[HK:, HK:] + direct2_ref[:, lanes]
        reach_ref[:half, lanes] = reach1
        reach_ref[half:, lanes] = joined[HK:, :HK]


def shard_terms(streams, rim, conv_weight, beta_t, gate_t):
    toks, channels = streams.shape
    heads = gate_t.shape[0]
    half = toks // 2
    vmem = pl.BlockSpec(memory_space=pltpu.VMEM)
    shape = jax.ShapeDtypeStruct
    square = (heads, HK, HK)
    params = dict(
        scratch_shapes=[pltpu.VMEM((8 + half, channels), f32)],
        compiler_params=pltpu.CompilerParams(vmem_limit_bytes=40 * 2**20),
        cost_estimate=pl.CostEstimate(
            flops=30 * heads * HK**3 * 2, bytes_accessed=4 * 2**20, transcendentals=0
        ),
    )
    later = pl.pallas_call(
        later_kernel,
        in_specs=[vmem] * 4,
        out_specs=[vmem] * 4,
        out_shape=[shape(square, f32)] * 2 + [shape((half, heads * HK), f32)] * 2,
        **params,
    )(streams, conv_weight, beta_t, gate_t)
    return pl.pallas_call(
        earlier_kernel,
        in_specs=[vmem] * 9,
        out_specs=[vmem] * 5,
        out_shape=[shape(square, f32)] * 2
        + [shape(square, bf16)]
        + [shape((toks, heads * HK), f32)] * 2,
        **params,
    )(streams, rim, conv_weight, beta_t, gate_t, *later)


def hand_on_kernel(map_ref, add_ref, state_ref, out_ref):
    for head in range(map_ref.shape[0]):
        high, low = split(map_ref[head])
        state = state_ref[head]
        grown = dot(
            jnp.concatenate([high, low], axis=1), jnp.concatenate([state, state], axis=0)
        )
        out_ref[head] = (grown + add_ref[head]).astype(bf16)


def hand_on(total_map, total_add, state):
    heads = total_map.shape[0]
    return pl.pallas_call(
        hand_on_kernel,
        out_shape=jax.ShapeDtypeStruct(state.shape, bf16),
        compiler_params=pltpu.CompilerParams(vmem_limit_bytes=16 * 2**20),
        cost_estimate=pl.CostEstimate(
            flops=4 * heads * HK**3, bytes_accessed=heads * HK * HK * 12, transcendentals=0
        ),
    )(total_map, total_add, state)


def project_kernel(count, *refs):
    states = refs[: count - 1]
    direct_ref, reach_ref, gain_ref, own_ref = refs[count - 1 : count + 3]
    rights = refs[count + 3 : 2 * count + 2]
    lefts = refs[2 * count + 2 : 3 * count + 1]
    out_ref, slots, sems = refs[3 * count + 1 :]
    mine = lax.axis_index("ctx")
    heads = states[0].shape[0]
    cols = own_ref.shape[1]

    def copy(source, slot):
        return pltpu.make_async_copy(source, slots.at[slot], sems.at[slot])

    copy(own_ref, 0).start()
    for turn in range(1, count):
        pl.when(mine >= turn)(lambda: copy(rights[turn - 1], turn).start())
        pl.when(mine < turn)(lambda: copy(lefts[count - turn - 1], turn).start())
    parts = []
    for head in range(heads):
        lanes = slice(head * HK, (head + 1) * HK)
        state = states[0][head]
        for other in states[1:]:
            state = state + other[head]
        high, low = split(reach_ref[:, lanes])
        out = direct_ref[:, lanes] + dot(
            jnp.concatenate([high, low], axis=1), jnp.concatenate([state, state], axis=0)
        )
        inverse = lax.rsqrt(jnp.mean(out * out, axis=-1, keepdims=True) + 1e-05)
        parts.append((out * inverse * gain_ref[:, lanes]).astype(bf16))
    normed = jnp.concatenate(parts, axis=1)
    for turn in range(count):
        copy(own_ref, turn).wait()
        owner = lax.rem(mine + count - turn, count)
        place = pl.ds(pl.multiple_of(owner * cols, HK), cols)
        out_ref[:, place] = dot(normed, slots[turn]).astype(bf16)


def project(states, direct, reach, gain, own, rights, lefts):
    count = len(states) + 1
    toks, width = direct.shape
    cols = own.shape[1]
    vmem = pl.BlockSpec(memory_space=pltpu.VMEM)
    hbm = pl.BlockSpec(memory_space=pl.ANY)
    return pl.pallas_call(
        functools.partial(project_kernel, count),
        in_specs=[vmem] * (count - 1) + [vmem] * 3 + [hbm] * (2 * count - 1),
        out_specs=vmem,
        out_shape=jax.ShapeDtypeStruct((toks, count * cols), bf16),
        scratch_shapes=[
            pltpu.VMEM((count, width, cols), bf16),
            pltpu.SemaphoreType.DMA((count,)),
        ],
        compiler_params=pltpu.CompilerParams(vmem_limit_bytes=32 * 2**20),
        cost_estimate=pl.CostEstimate(
            flops=2 * toks * width * count * cols,
            bytes_accessed=2 * width * count * cols,
            transcendentals=0,
        ),
    )(*states, direct, reach, gain, own, *rights, *lefts)


def norm_kernel(direct_ref, reach_ref, gain_ref, *refs):
    states, out_ref = refs[:-1], refs[-1]
    for head in range(states[0].shape[0]):
        lanes = slice(head * HK, (head + 1) * HK)
        state = states[0][head]
        for other in states[1:]:
            state = state + other[head]
        high, low = split(reach_ref[:, lanes])
        out = direct_ref[:, lanes] + dot(
            jnp.concatenate([high, low], axis=1), jnp.concatenate([state, state], axis=0)
        )
        inverse = lax.rsqrt(jnp.mean(out * out, axis=-1, keepdims=True) + 1e-05)
        out_ref[:, lanes] = (out * inverse * gain_ref[:, lanes]).astype(bf16)


def normalize(direct, reach, gain, states):
    vmem = pl.BlockSpec(memory_space=pltpu.VMEM)
    return pl.pallas_call(
        norm_kernel,
        in_specs=[vmem] * (3 + len(states)),
        out_specs=vmem,
        out_shape=jax.ShapeDtypeStruct(direct.shape, bf16),
        compiler_params=pltpu.CompilerParams(vmem_limit_bytes=16 * 2**20),
        cost_estimate=pl.CostEstimate(
            flops=4 * direct.size * HK, bytes_accessed=10 * direct.size, transcendentals=0
        ),
    )(direct, reach, gain, *states)


def own_columns_kernel(rows_ref, own_ref, left_ref, right_ref, two_ref, one_ref):
    mine = lax.axis_index("ctx")
    rows = rows_ref[...]
    cols = own_ref.shape[1]
    two_ref[:, :cols] = dot(rows, own_ref[...]).astype(bf16)

    @pl.when(mine < 2)
    def _():
        two_ref[:, cols:] = dot(rows, right_ref[...]).astype(bf16)
        one_ref[...] = dot(rows, left_ref[...]).astype(bf16)

    @pl.when(mine >= 2)
    def _():
        two_ref[:, cols:] = dot(rows, left_ref[...]).astype(bf16)
        one_ref[...] = dot(rows, right_ref[...]).astype(bf16)


def others_columns_kernel(far_ref, near_ref, own_ref, left_ref, right_ref, two_ref, one_ref):
    mine = lax.axis_index("ctx")
    cols = own_ref.shape[1]
    far = far_ref[...]
    two_ref[:, :cols] = dot(far, own_ref[...]).astype(bf16)

    @pl.when(mine < 2)
    def _():
        two_ref[:, cols:] = dot(far, left_ref[...]).astype(bf16)
        one_ref[...] = dot(near_ref[...], left_ref[...]).astype(bf16)

    @pl.when(mine >= 2)
    def _():
        two_ref[:, cols:] = dot(far, right_ref[...]).astype(bf16)
        one_ref[...] = dot(near_ref[...], right_ref[...]).astype(bf16)


def columns(kernel, rows, own, left, right):
    vmem = pl.BlockSpec(memory_space=pltpu.VMEM)
    toks, cols = rows[0].shape[0], own.shape[1]
    return pl.pallas_call(
        kernel,
        in_specs=[vmem] * (len(rows) + 3),
        out_specs=[vmem] * 2,
        out_shape=[
            jax.ShapeDtypeStruct((toks, 2 * cols), bf16),
            jax.ShapeDtypeStruct((toks, cols), bf16),
        ],
        compiler_params=pltpu.CompilerParams(vmem_limit_bytes=32 * 2**20),
        cost_estimate=pl.CostEstimate(
            flops=6 * own.size * toks, bytes_accessed=8 * own.size, transcendentals=0
        ),
    )(*rows, own, left, right)


def assemble_kernel(own_two, own_one, far_two, near_one, out_ref, sems):
    mine = lax.axis_index("ctx")
    cols = own_one.shape[1]
    first, second = pl.ds(0, cols), pl.ds(cols, cols)
    sources = (
        (own_two.at[:, first], own_two.at[:, second], far_two.at[:, first], far_two.at[:, second]),
        (own_one, own_two.at[:, first], own_two.at[:, second], near_one),
        (near_one, own_two.at[:, second], own_two.at[:, first], own_one),
        (far_two.at[:, second], far_two.at[:, first], own_two.at[:, second], own_two.at[:, first]),
    )
    for place, blocks in enumerate(sources):

        @pl.when(mine == place)
        def _():
            copies = [
                pltpu.make_async_copy(
                    block, out_ref.at[:, pl.ds(index * cols, cols)], sems.at[index]
                )
                for index, block in enumerate(blocks)
            ]
            for copy in copies:
                copy.start()
            for copy in copies:
                copy.wait()


def assemble(parts):
    vmem = pl.BlockSpec(memory_space=pltpu.VMEM)
    toks, cols = parts[1].shape
    return pl.pallas_call(
        assemble_kernel,
        in_specs=[vmem] * 4,
        out_specs=pl.BlockSpec(memory_space=pl.ANY),
        out_shape=jax.ShapeDtypeStruct((toks, 4 * cols), bf16),
        scratch_shapes=[pltpu.SemaphoreType.DMA((4,))],
        cost_estimate=pl.CostEstimate(
            flops=0, bytes_accessed=16 * toks * cols, transcendentals=0
        ),
    )(*parts)


def moved(value, pairs):
    return lax.ppermute(value, "ctx", pairs)


def handed(value, pairs):
    sections, count = lax.axis_size("section"), lax.axis_size("ctx")
    return lax.ppermute(
        value,
        ("section", "ctx"),
        [
            (s * count + a, (s + 1) % sections * count + b)
            for s in range(sections)
            for a, b in pairs
        ],
    )


def on_device(streams, conv_weight, beta_logit, gate_log, norm_gain, w_out):
    count = lax.axis_size("ctx")
    toks = streams.shape[1]
    rim = moved(streams[0, toks - (CONV - 1) :], [(c, c + 1) for c in range(count - 1)])
    own = w_out[0]
    rights = [moved(own, [(c, c + 1) for c in range(count - 1)])]
    lefts = [moved(own, [(c, c - 1) for c in range(1, count)])]
    if count != 4:
        for turn in range(2, count):
            rights.append(moved(rights[-1], [(c, c + 1) for c in range(turn - 1, count - 1)]))
            lefts.append(moved(lefts[-1], [(c, c - 1) for c in range(1, count - turn + 1)]))
    total_map, total_add, sent, direct, reach = shard_terms(
        streams[0], rim, conv_weight[0], beta_logit[0].T, gate_log[0].T
    )
    states = [moved(sent, [(0, 1)])]
    for turn in range(1, count - 1):
        states.append(moved(hand_on(total_map, total_add, states[-1]), [(turn, turn + 1)]))
    if count != 4:
        mixed = project(states, direct, reach, norm_gain, own, rights, lefts)
        return handed(mixed, [(c, c) for c in range(count)])[None]
    early = normalize(direct, reach, norm_gain, states[:-1])
    near = moved(early, [(1, 2), (2, 1)])
    normed = normalize(direct, reach, norm_gain, states)
    far = moved(normed, [(0, 2), (3, 1)])
    own_two, own_one = columns(own_columns_kernel, [normed], own, rights[0], lefts[0])
    far_two, near_one = columns(others_columns_kernel, [far, near], own, rights[0], lefts[0])
    return assemble(
        [
            handed(own_two, [(c, c) for c in range(4)]),
            handed(own_one, [(1, 1), (2, 2)]),
            handed(far_two, [(1, 3), (2, 0)]),
            handed(near_one, [(1, 2), (2, 1)]),
        ]
    )[None]


def solution(mesh):
    placed = (
        P("section", "ctx", None),
        P("section", None, None),
        P("section", "ctx", None),
        P("section", "ctx", None),
        P("section", None),
        P("section", None, "ctx"),
    )
    return jax.shard_map(
        on_device, mesh=mesh, in_specs=placed, out_specs=P("section", "ctx", None), check_vma=False
    )
```

time: 110 us -> 85.5 us (0.78)
  the two profiles are of different devices: /device:TPU:24 before, /device:TPU:8 now
where the time goes in v2:
time: 85.5 us; the launch traced here: 85 us
  waiting for transfers between devices  31.2 us (36%)
  starting transfers between devices  27.6 us (32%)
  Pallas kernels  19.9 us (23%)
  local copies, waits for them, and re-layouts  5.84 us (7%)
    ppermute x8, waiting for transfers between devices, moved(): return lax.ppermute(value, 'ctx', pairs)  25.9 us
    ppermute x8, starting transfers between devices, moved(): return lax.ppermute(value, 'ctx', pairs)  19.2 us
    ppermute x4, starting transfers between devices, handed(): lax.ppermute(value, ('section', 'ctx'), [(s * count + a, (s + 1) % sectio...  8.4 us
    pallas_call x1, Pallas kernels, shard_terms(): pl.pallas_call(earlier_kernel, in_specs=[vmem] * 9, out_specs=[vmem] * 5,...  7.86 us
    pallas_call x1, Pallas kernels, shard_terms(): pl.pallas_call(later_kernel, in_specs=[vmem] * 4, out_specs=[vmem] * 4, o...  7.21 us
    ppermute x4, waiting for transfers between devices, handed(): lax.ppermute(value, ('section', 'ctx'), [(s * count + a, (s + 1) % sectio...  5.29 us
    unnamed x20, local copies, waits for them, and re-layouts  4.93 us
    pallas_call x1, Pallas kernels, assemble(): pl.pallas_call(assemble_kernel, in_specs=[vmem] * 4, out_specs=pl.BlockSp...  1.95 us
  transfers between devices with their start and end apart: 12, of which 6 were waited for; matrix products, arithmetic and copies ran while one was open for 1% of the time, Pallas kernels for 21%

profile of v2, /device:TPU:8, one launch (start us, length us, event | category | flops | bytes accessed | tf_op | source)
XLA Modules:
  0.0 85.0 jit_solution(8167519163110811886)
XLA Ops:
  0.0 3.5 %collective-permute-start.4 = (bf16[1024,512]{1,0:T(8,128)(2,1)}, bf16[1024,512]{1,0:T(8,128)(2,1)S(1)}, u32[]{:S(2)}, u32[]{:S(2)}) collective-permute-start(bf16[1024,512]{1,0:T(8,128)(2,1)} %bitcast.12), channel_id=1, source_target_pairs={{0,1},{1,2},{2,3},{4,5},{5,6},{6,7},{8,9},{9,10},{10,11},{12,13},{... | collective-permute-start | bytes 3145736 | tf_op jit(solution)/shard_map/ppermute | solution.py:425
  3.5 2.4 %collective-permute-start.5 = (bf16[1024,512]{1,0:T(8,128)(2,1)}, bf16[1024,512]{1,0:T(8,128)(2,1)S(1)}, u32[]{:S(2)}, u32[]{:S(2)}) collective-permute-start(bf16[1024,512]{1,0:T(8,128)(2,1)} %bitcast.13), channel_id=1, source_target_pairs={{1,0},{2,1},{3,2},{5,4},{6,5},{7,6},{9,8},{10,9},{11,10},{13,12},{... | collective-permute-start | bytes 3145736 | tf_op jit(solution)/shard_map/ppermute | solution.py:425
  5.9 0.9 %slice_bitcast_fusion = bf16[3,5120]{1,0:T(4,128)(2,1)S(1)} fusion(bf16[1,128,5120]{2,1,0:T(8,128)(2,1)} %param.6), kind=kLoop, calls=%fused_computation | loop fusion | bytes 61440 | tf_op jit(solution)/shard_map/squeeze | solution.py:444
  6.8 3.4 %collective-permute-start = (bf16[3,5120]{1,0:T(4,128)(2,1)S(1)}, bf16[3,5120]{1,0:T(4,128)(2,1)S(1)}, u32[]{:S(2)}, u32[]{:S(2)}) collective-permute-start(bf16[3,5120]{1,0:T(4,128)(2,1)S(1)} %slice_bitcast_fusion), channel_id=1, source_target_pairs={{0,1},{1,2},{2,3},{4,5},{5,6},{6,7},{8,9},{9,10},{10,11},{12,13},{... | collective-permute-start | bytes 92168 | tf_op jit(solution)/shard_map/ppermute | solution.py:425
  10.3 1.3 %copy-done.2 = bf16[1,128,5120]{2,1,0:T(8,128)(2,1)S(1)} copy-done((bf16[1,128,5120]{2,1,0:T(8,128)(2,1)S(1)}, bf16[1,128,5120]{2,1,0:T(8,128)(2,1)}, u32[]{:S(2)}) %copy-start.2) | copy-done | bytes 1310744
  11.6 0.8 copy-done.3
  13.7 7.2 %shard_map.64 = (f32[8,128,128]{2,1,0:T(8,128)S(1)}, f32[8,128,128]{2,1,0:T(8,128)S(1)}, f32[64,1024]{1,0:T(8,128)S(1)}, f32[64,1024]{1,0:T(8,128)S(1)}) custom-call(bf16[128,5120]{1,0:T(8,128)(2,1)S(1)} %bitcast.16, bf16[4,5120]{1,0:T(4,128)(2,1)S(1)} %bitcast.18, f32[16,128]{1,0:T(8,128)S(1)} %bitcast.20, f32[8,128]{1,0:T(8,128)S(1)} %bitcast.22), custom_call_target="tpu_custom_call" | custom-call | flops 1006632960 | bytes 4194304 | tf_op jit(solution)/shard_map/pallas_call | solution.py:201
  21.0 6.9 %collective-permute-done.rim_ref = bf16[3,5120]{1,0:T(4,128)(2,1)S(1)} collective-permute-done((bf16[3,5120]{1,0:T(4,128)(2,1)S(1)}, bf16[3,5120]{1,0:T(4,128)(2,1)S(1)}, u32[]{:S(2)}, u32[]{:S(2)}) %collective-permute-start) | collective-permute-done | bytes 30752 | tf_op jit(solution)/shard_map/ppermute | solution.py:425
  27.9 7.9 %shard_map.65 = (f32[8,128,128]{2,1,0:T(8,128)S(1)}, f32[8,128,128]{2,1,0:T(8,128)S(1)}, bf16[8,128,128]{2,1,0:T(8,128)(2,1)S(1)}, f32[128,1024]{1,0:T(8,128)S(1)}, f32[128,1024]{1,0:T(8,128)S(1)}) custom-call(bf16[128,5120]{1,0:T(8,128)(2,1)S(1)} %bitcast.17, bf16[3,5120]{1,0:T(4,128)(2,1)S(1)} %collective-permute-done.rim_ref, ...), custom_call_target="tpu_custom_call" | custom-call | flops 1006632960 | bytes 4194304 | tf_op jit(solution)/shard_map/pallas_call | solution.py:208
  35.7 1.3 %collective-permute-start.1 = (bf16[8,128,128]{2,1,0:T(8,128)(2,1)S(1)}, bf16[8,128,128]{2,1,0:T(8,128)(2,1)S(1)}, u32[]{:S(2)}, u32[]{:S(2)}) collective-permute-start(bf16[8,128,128]{2,1,0:T(8,128)(2,1)S(1)} %get-tuple-element.24), channel_id=1, source_target_pairs={{0,1},{4,5},{8,9},{12,13},{16,17},{20,21},{24,25},{28,29}} | collective-permute-start | bytes 786440 | tf_op jit(solution)/shard_map/ppermute | solution.py:425
  37.0 7.8 %collective-permute-done.1.state_ref.refs_0_ = bf16[8,128,128]{2,1,0:T(8,128)(2,1)S(1)} collective-permute-done((bf16[8,128,128]{2,1,0:T(8,128)(2,1)S(1)}, bf16[8,128,128]{2,1,0:T(8,128)(2,1)S(1)}, u32[]{:S(2)}, u32[]{:S(2)}) %collective-permute-start.1) | collective-permute-done | bytes 262176 | tf_op jit(solution)/shard_map/ppermute | solution.py:425
  45.1 1.5 %collective-permute-start.2 = (bf16[8,128,128]{2,1,0:T(8,128)(2,1)S(1)}, bf16[8,128,128]{2,1,0:T(8,128)(2,1)S(1)}, u32[]{:S(2)}, u32[]{:S(2)}) collective-permute-start(bf16[8,128,128]{2,1,0:T(8,128)(2,1)S(1)} %shard_map.66), channel_id=1, source_target_pairs={{1,2},{5,6},{9,10},{13,14},{17,18},{21,22},{25,26},{29,30}} | collective-permute-start | bytes 786440 | tf_op jit(solution)/shard_map/ppermute | solution.py:425
  46.6 3.8 %collective-permute-done.2.state_ref.refs_1_ = bf16[8,128,128]{2,1,0:T(8,128)(2,1)S(1)} collective-permute-done((bf16[8,128,128]{2,1,0:T(8,128)(2,1)S(1)}, bf16[8,128,128]{2,1,0:T(8,128)(2,1)S(1)}, u32[]{:S(2)}, u32[]{:S(2)}) %collective-permute-start.2) | collective-permute-done | bytes 262176 | tf_op jit(solution)/shard_map/ppermute | solution.py:425
  51.9 5.2 %collective-permute-start.9 = (bf16[128,1024]{1,0:T(8,128)(2,1)S(1)}, bf16[128,1024]{1,0:T(8,128)(2,1)S(1)}, u32[]{:S(2)}, u32[]{:S(2)}) collective-permute-start(bf16[128,1024]{1,0:T(8,128)(2,1)S(1)} %shard_map.70), channel_id=1, source_target_pairs={{1,2},{2,1},{5,6},{6,5},{9,10},{10,9},{13,14},{14,13},{17,18},{18,... | collective-permute-start | bytes 786440 | tf_op jit(solution)/shard_map/ppermute | solution.py:425
  57.4 1.3 %collective-permute-start.8 = (bf16[128,1024]{1,0:T(8,128)(2,1)S(1)}, bf16[128,1024]{1,0:T(8,128)(2,1)S(1)}, u32[]{:S(2)}, u32[]{:S(2)}) collective-permute-start(bf16[128,1024]{1,0:T(8,128)(2,1)S(1)} %shard_map.68.rows_ref), channel_id=1, source_target_pairs={{0,2},{3,1},{4,6},{7,5},{8,10},{11,9},{12,14},{15,13},{16,18},{19,... | collective-permute-start | bytes 786440 | tf_op jit(solution)/shard_map/ppermute | solution.py:425
  58.8 0.8 shard_map.69
  59.6 7.4 %collective-permute-done.9.near_ref = bf16[128,1024]{1,0:T(8,128)(2,1)S(1)} collective-permute-done((bf16[128,1024]{1,0:T(8,128)(2,1)S(1)}, bf16[128,1024]{1,0:T(8,128)(2,1)S(1)}, u32[]{:S(2)}, u32[]{:S(2)}) %collective-permute-start.9) | collective-permute-done | bytes 262176 | tf_op jit(solution)/shard_map/ppermute | solution.py:425
  67.0 0.8 shard_map.71
  67.8 1.3 %collective-permute-start.10 = (bf16[128,1024]{1,0:T(8,128)(2,1)S(1)}, bf16[128,1024]{1,0:T(8,128)(2,1)S(1)}, u32[]{:S(2)}, u32[]{:S(2)}) collective-permute-start(bf16[128,1024]{1,0:T(8,128)(2,1)S(1)} %get-tuple-element.29), channel_id=1, source_target_pairs={{1,7},{2,4},{5,11},{6,8},{9,15},{10,12},{13,19},{14,16},{17,23},{1... | collective-permute-start | bytes 786440 | tf_op jit(solution)/shard_map/ppermute | solution.py:430
  69.1 2.8 %collective-permute-start.7 = (bf16[128,512]{1,0:T(8,128)(2,1)S(1)}, bf16[128,512]{1,0:T(8,128)(2,1)S(1)}, u32[]{:S(2)}, u32[]{:S(2)}) collective-permute-start(bf16[128,512]{1,0:T(8,128)(2,1)S(1)} %get-tuple-element.28), channel_id=1, source_target_pairs={{1,5},{2,6},{5,9},{6,10},{9,13},{10,14},{13,17},{14,18},{17,21},{1... | collective-permute-start | bytes 393224 | tf_op jit(solution)/shard_map/ppermute | solution.py:430
  71.9 4.3 %collective-permute-start.11 = (bf16[128,512]{1,0:T(8,128)(2,1)S(1)}, bf16[128,512]{1,0:T(8,128)(2,1)S(1)}, u32[]{:S(2)}, u32[]{:S(2)}) collective-permute-start(bf16[128,512]{1,0:T(8,128)(2,1)S(1)} %get-tuple-element.30), channel_id=1, source_target_pairs={{1,6},{2,5},{5,10},{6,9},{9,14},{10,13},{13,18},{14,17},{17,22},{1... | collective-permute-start | bytes 393224 | tf_op jit(solution)/shard_map/ppermute | solution.py:430
  76.3 5.1 %collective-permute-done.11.near_one = bf16[128,512]{1,0:T(8,128)(2,1)S(1)} collective-permute-done((bf16[128,512]{1,0:T(8,128)(2,1)S(1)}, bf16[128,512]{1,0:T(8,128)(2,1)S(1)}, u32[]{:S(2)}, u32[]{:S(2)}) %collective-permute-start.11) | collective-permute-done | bytes 131104 | tf_op jit(solution)/shard_map/ppermute | solution.py:430
  82.2 0.7 copy-done.7
  82.9 1.9 %shard_map.72 = bf16[128,2048]{1,0:T(8,128)(2,1)} custom-call(bf16[128,1024]{1,0:T(8,128)(2,1)} %copy-done.6, bf16[128,512]{1,0:T(8,128)(2,1)} %copy-done.8, bf16[128,1024]{1,0:T(8,128)(2,1)} %copy-done.7, bf16[128,512]{1,0:T(8,128)(2,1)} %copy-done.9), custom_call_target="tpu_custom_call" | custom-call | bytes 1048576 | tf_op jit(solution)/shard_map/pallas_call | solution.py:412
  (30 shorter events, 4.4 us)
Async XLA Ops:
  0.0 58.8 %collective-permute-start.4 = (bf16[1024,512]{1,0:T(8,128)(2,1)}, bf16[1024,512]{1,0:T(8,128)(2,1)S(1)}, u32[]{:S(2)}, u32[]{:S(2)}) collective-permute-start(bf16[1024,512]{1,0:T(8,128)(2,1)} %bitcast.12), channel_id=1, source_target_pairs={{0,1},{1,2},{2,3},{4,5},{5,6},{6,7},{8,9},{9,10},{10,11},{12,13},{... | collective-permute-start | bytes 3145736 | tf_op jit(solution)/shard_map/ppermute | solution.py:425
  3.5 55.3 %collective-permute-start.5 = (bf16[1024,512]{1,0:T(8,128)(2,1)}, bf16[1024,512]{1,0:T(8,128)(2,1)S(1)}, u32[]{:S(2)}, u32[]{:S(2)}) collective-permute-start(bf16[1024,512]{1,0:T(8,128)(2,1)} %bitcast.13), channel_id=1, source_target_pairs={{1,0},{2,1},{3,2},{5,4},{6,5},{7,6},{9,8},{10,9},{11,10},{13,12},{... | collective-permute-start | bytes 3145736 | tf_op jit(solution)/shard_map/ppermute | solution.py:425
  6.8 21.0 %collective-permute-start = (bf16[3,5120]{1,0:T(4,128)(2,1)S(1)}, bf16[3,5120]{1,0:T(4,128)(2,1)S(1)}, u32[]{:S(2)}, u32[]{:S(2)}) collective-permute-start(bf16[3,5120]{1,0:T(4,128)(2,1)S(1)} %slice_bitcast_fusion), channel_id=1, source_target_pairs={{0,1},{1,2},{2,3},{4,5},{5,6},{6,7},{8,9},{9,10},{10,11},{12,13},{... | collective-permute-start | bytes 92168 | tf_op jit(solution)/shard_map/ppermute | solution.py:425
  10.3 1.3 %copy-start.2 = (bf16[1,128,5120]{2,1,0:T(8,128)(2,1)S(1)}, bf16[1,128,5120]{2,1,0:T(8,128)(2,1)}, u32[]{:S(2)}) copy-start(bf16[1,128,5120]{2,1,0:T(8,128)(2,1)} %param.6) | copy-start | bytes 3932164
  11.6 0.8 copy-start.3
  12.4 0.7 copy-start.4
  13.1 0.7 copy-start.5
  35.7 9.1 %collective-permute-start.1 = (bf16[8,128,128]{2,1,0:T(8,128)(2,1)S(1)}, bf16[8,128,128]{2,1,0:T(8,128)(2,1)S(1)}, u32[]{:S(2)}, u32[]{:S(2)}) collective-permute-start(bf16[8,128,128]{2,1,0:T(8,128)(2,1)S(1)} %get-tuple-element.24), channel_id=1, source_target_pairs={{0,1},{4,5},{8,9},{12,13},{16,17},{20,21},{24,25},{28,29}} | collective-permute-start | bytes 786440 | tf_op jit(solution)/shard_map/ppermute | solution.py:425
  44.8 6.6 %copy-start.1 = (f32[1,1024]{1,0:T(1,128)S(1)}, f32[1,1024]{1,0:T(1,128)}, u32[]{:S(2)}) copy-start(f32[1,1024]{1,0:T(1,128)} %gain_ref.3) | copy-start | bytes 12292
  45.1 5.3 %collective-permute-start.2 = (bf16[8,128,128]{2,1,0:T(8,128)(2,1)S(1)}, bf16[8,128,128]{2,1,0:T(8,128)(2,1)S(1)}, u32[]{:S(2)}, u32[]{:S(2)}) collective-permute-start(bf16[8,128,128]{2,1,0:T(8,128)(2,1)S(1)} %shard_map.66), channel_id=1, source_target_pairs={{1,2},{5,6},{9,10},{13,14},{17,18},{21,22},{25,26},{29,30}} | collective-permute-start | bytes 786440 | tf_op jit(solution)/shard_map/ppermute | solution.py:425
  50.7 6.3 %collective-permute-start.3 = (bf16[8,128,128]{2,1,0:T(8,128)(2,1)S(1)}, bf16[8,128,128]{2,1,0:T(8,128)(2,1)S(1)}, u32[]{:S(2)}, u32[]{:S(2)}) collective-permute-start(bf16[8,128,128]{2,1,0:T(8,128)(2,1)S(1)} %shard_map.67), channel_id=1, source_target_pairs={{2,3},{6,7},{10,11},{14,15},{18,19},{22,23},{26,27},{30,31}} | collective-permute-start | bytes 786440 | tf_op jit(solution)/shard_map/ppermute | solution.py:425
  51.9 6.9 %copy-start = (bf16[1,1024,512]{2,1,0:T(8,128)(2,1)S(1)}, bf16[1,1024,512]{2,1,0:T(8,128)(2,1)}, u32[]{:S(2)}) copy-start(bf16[1,1024,512]{2,1,0:T(8,128)(2,1)} %param.11) | copy-start | bytes 3145732
  51.9 15.1 %collective-permute-start.9 = (bf16[128,1024]{1,0:T(8,128)(2,1)S(1)}, bf16[128,1024]{1,0:T(8,128)(2,1)S(1)}, u32[]{:S(2)}, u32[]{:S(2)}) collective-permute-start(bf16[128,1024]{1,0:T(8,128)(2,1)S(1)} %shard_map.70), channel_id=1, source_target_pairs={{1,2},{2,1},{5,6},{6,5},{9,10},{10,9},{13,14},{14,13},{17,18},{18,... | collective-permute-start | bytes 786440 | tf_op jit(solution)/shard_map/ppermute | solution.py:425
  57.4 9.5 %collective-permute-start.8 = (bf16[128,1024]{1,0:T(8,128)(2,1)S(1)}, bf16[128,1024]{1,0:T(8,128)(2,1)S(1)}, u32[]{:S(2)}, u32[]{:S(2)}) collective-permute-start(bf16[128,1024]{1,0:T(8,128)(2,1)S(1)} %shard_map.68.rows_ref), channel_id=1, source_target_pairs={{0,2},{3,1},{4,6},{7,5},{8,10},{11,9},{12,14},{15,13},{16,18},{19,... | collective-permute-start | bytes 786440 | tf_op jit(solution)/shard_map/ppermute | solution.py:425
  59.5 21.9 %collective-permute-start.6 = (bf16[128,1024]{1,0:T(8,128)(2,1)S(1)}, bf16[128,1024]{1,0:T(8,128)(2,1)S(1)}, u32[]{:S(2)}, u32[]{:S(2)}) collective-permute-start(bf16[128,1024]{1,0:T(8,128)(2,1)S(1)} %get-tuple-element.27), channel_id=1, source_target_pairs={{0,4},{1,5},{2,6},{3,7},{4,8},{5,9},{6,10},{7,11},{8,12},{9,13},{1... | collective-permute-start | bytes 786440 | tf_op jit(solution)/shard_map/ppermute | solution.py:430
  67.8 13.7 %collective-permute-start.10 = (bf16[128,1024]{1,0:T(8,128)(2,1)S(1)}, bf16[128,1024]{1,0:T(8,128)(2,1)S(1)}, u32[]{:S(2)}, u32[]{:S(2)}) collective-permute-start(bf16[128,1024]{1,0:T(8,128)(2,1)S(1)} %get-tuple-element.29), channel_id=1, source_target_pairs={{1,7},{2,4},{5,11},{6,8},{9,15},{10,12},{13,19},{14,16},{17,23},{1... | collective-permute-start | bytes 786440 | tf_op jit(solution)/shard_map/ppermute | solution.py:430
  69.1 7.2 %collective-permute-start.7 = (bf16[128,512]{1,0:T(8,128)(2,1)S(1)}, bf16[128,512]{1,0:T(8,128)(2,1)S(1)}, u32[]{:S(2)}, u32[]{:S(2)}) collective-permute-start(bf16[128,512]{1,0:T(8,128)(2,1)S(1)} %get-tuple-element.28), channel_id=1, source_target_pairs={{1,5},{2,6},{5,9},{6,10},{9,13},{10,14},{13,17},{14,18},{17,21},{1... | collective-permute-start | bytes 393224 | tf_op jit(solution)/shard_map/ppermute | solution.py:430
  71.9 9.5 %collective-permute-start.11 = (bf16[128,512]{1,0:T(8,128)(2,1)S(1)}, bf16[128,512]{1,0:T(8,128)(2,1)S(1)}, u32[]{:S(2)}, u32[]{:S(2)}) collective-permute-start(bf16[128,512]{1,0:T(8,128)(2,1)S(1)} %get-tuple-element.30), channel_id=1, source_target_pairs={{1,6},{2,5},{5,10},{6,9},{9,14},{10,13},{13,18},{14,17},{17,22},{1... | collective-permute-start | bytes 393224 | tf_op jit(solution)/shard_map/ppermute | solution.py:430
  76.3 5.2 %copy-start.8 = (bf16[128,512]{1,0:T(8,128)(2,1)}, bf16[128,512]{1,0:T(8,128)(2,1)S(1)}, u32[]{:S(2)}) copy-start(bf16[128,512]{1,0:T(8,128)(2,1)S(1)} %collective-permute-done.7.own_one) | copy-start | bytes 393220
  81.4 0.6 copy-start.9
  81.4 0.8 copy-start.6
  82.2 0.7 copy-start.7

commit v3 on v2

--- a/solution.py
+++ b/solution.py
@@ -144,44 +144,53 @@
     return acts
 
 
-def later_kernel(x_ref, taps_ref, beta_ref, gate_ref, map_ref, add_ref, direct_ref, reach_ref, ext):
+def terms_kernel(
+    x_hbm, rim_ref, taps_hbm, beta_hbm, gate_hbm,
+    map_ref, add_ref, sent_ref, direct_ref, reach_ref, both_ref,
+    x_ref, taps_ref, beta_ref, gate_ref, ext, sems,
+):
+    copies = [
+        pltpu.make_async_copy(source, target, sems.at[index])
+        for index, (source, target) in enumerate(
+            ((x_hbm, x_ref), (taps_hbm, taps_ref), (beta_hbm, beta_ref), (gate_hbm, gate_ref))
+        )
+    ]
+    for copy in copies:
+        copy.start()
+    for copy in copies:
+        copy.wait()
     heads, toks = gate_ref.shape
     half = toks // 2
-    ext[...] = x_ref[half - 16 :].astype(f32)[8:]
-    acts = activations(ext, taps_ref, half, heads)
-    found = half_terms(1, heads, half, acts, beta_ref[...], gate_ref[...])
-    for head, (map2, add2, direct2, reach2) in enumerate(found):
+    ext[0] = x_ref[half - 16 :].astype(f32)[8:]
+    ext[1, 8 - (CONV - 1) : 8] = rim_ref[...].astype(f32)
+    ext[1, 8:] = x_ref[:half].astype(f32)
+    later, earlier = (
+        half_terms(
+            u, heads, half, activations(ext.at[1 - u], taps_ref, half, heads), beta_ref[...], gate_ref[...]
+        )
+        for u in (1, 0)
+    )
+    for head in range(heads):
         lanes = slice(head * HK, (head + 1) * HK)
-        map_ref[head] = map2
-        add_ref[head] = add2
-        direct_ref[:, lanes] = direct2
-        reach_ref[:, lanes] = reach2
-
-
-def earlier_kernel(
-    x_ref, rim_ref, taps_ref, beta_ref, gate_ref, map2_ref, add2_ref, direct2_ref, reach2_ref,
-    map_ref, add_ref, sent_ref, direct_ref, reach_ref, ext,
-):
-    heads, toks = gate_ref.shape
-    half = toks // 2
-    ext[8 - (CONV - 1) : 8] = rim_ref[...].astype(f32)
-    ext[8:] = x_ref[:half].astype(f32)
-    acts = activations(ext, taps_ref, half, heads)
-    found = half_terms(0, heads, half, acts, beta_ref[...], gate_ref[...])
-    for head, (map1, add1, direct1, reach1) in enumerate(found):
-        lanes = slice(head * HK, (head + 1) * HK)
+        map1, add1, direct1, reach1 = earlier[head]
+        map2, add2, direct2, reach2 = later[head]
         joined = dot3(
-            jnp.concatenate([map2_ref[head], reach2_ref[:, lanes]], axis=0),
-            jnp.concatenate([map1, add1], axis=1),
-        )
-        total = joined[:HK, HK:] + add2_ref[head]
+            jnp.concatenate([map2, reach2], axis=0), jnp.concatenate([map1, add1], axis=1)
+        )
+        total = joined[:HK, HK:] + add2
+        direct2 = joined[HK:, HK:] + direct2
+        reach2 = joined[HK:, :HK]
         map_ref[head] = joined[:HK, :HK]
         add_ref[head] = total
         sent_ref[head] = total.astype(bf16)
-        direct_ref[:half, lanes] = direct1
-        direct_ref[half:, lanes] = joined[HK:, HK:] + direct2_ref[:, lanes]
-        reach_ref[:half, lanes] = reach1
-        reach_ref[half:, lanes] = joined[HK:, :HK]
+        for rows, direct, reach in (
+            (slice(0, half), direct1, reach1),
+            (slice(half, toks), direct2, reach2),
+        ):
+            direct_ref[rows, lanes] = direct
+            reach_ref[rows, lanes] = reach
+            both_ref[0, rows, lanes] = direct.astype(bf16)
+            both_ref[1, rows, lanes] = reach.astype(bf16)
 
 
 def shard_terms(streams, rim, conv_weight, beta_t, gate_t):
@@ -189,31 +198,34 @@
     heads = gate_t.shape[0]
     half = toks // 2
     vmem = pl.BlockSpec(memory_space=pltpu.VMEM)
+    hbm = pl.BlockSpec(memory_space=pl.ANY)
     shape = jax.ShapeDtypeStruct
-    square = (heads, HK, HK)
-    params = dict(
-        scratch_shapes=[pltpu.VMEM((8 + half, channels), f32)],
-        compiler_params=pltpu.CompilerParams(vmem_limit_bytes=40 * 2**20),
+    square, rows = (heads, HK, HK), (toks, heads * HK)
+    return pl.pallas_call(
+        terms_kernel,
+        in_specs=[hbm, vmem, hbm, hbm, hbm],
+        out_specs=[vmem] * 6,
+        out_shape=[
+            shape(square, f32),
+            shape(square, f32),
+            shape(square, bf16),
+            shape(rows, f32),
+            shape(rows, f32),
+            shape((2,) + rows, bf16),
+        ],
+        scratch_shapes=[
+            pltpu.VMEM(streams.shape, bf16),
+            pltpu.VMEM(conv_weight.shape, bf16),
+            pltpu.VMEM(beta_t.shape, f32),
+            pltpu.VMEM(gate_t.shape, f32),
+            pltpu.VMEM((2, 8 + half, channels), f32),
+            pltpu.SemaphoreType.DMA((4,)),
+        ],
+        compiler_params=pltpu.CompilerParams(vmem_limit_bytes=44 * 2**20),
         cost_estimate=pl.CostEstimate(
-            flops=30 * heads * HK**3 * 2, bytes_accessed=4 * 2**20, transcendentals=0
+            flops=60 * heads * HK**3 * 2, bytes_accessed=4 * 2**20, transcendentals=0
         ),
-    )
-    later = pl.pallas_call(
-        later_kernel,
-        in_specs=[vmem] * 4,
-        out_specs=[vmem] * 4,
-        out_shape=[shape(square, f32)] * 2 + [shape((half, heads * HK), f32)] * 2,
-        **params,
-    )(streams, conv_weight, beta_t, gate_t)
-    return pl.pallas_call(
-        earlier_kernel,
-        in_specs=[vmem] * 9,
-        out_specs=[vmem] * 5,
-        out_shape=[shape(square, f32)] * 2
-        + [shape(square, bf16)]
-        + [shape((toks, heads * HK), f32)] * 2,
-        **params,
-    )(streams, rim, conv_weight, beta_t, gate_t, *later)
+    )(streams, rim, conv_weight, beta_t, gate_t)
 
 
 def hand_on_kernel(map_ref, add_ref, state_ref, out_ref):
@@ -299,106 +311,126 @@
     )(*states, direct, reach, gain, own, *rights, *lefts)
 
 
-def norm_kernel(direct_ref, reach_ref, gain_ref, *refs):
-    states, out_ref = refs[:-1], refs[-1]
-    for head in range(states[0].shape[0]):
+def normed_rows(direct, reach, state, gain):
+    out = direct + dot(reach, state)
+    return (out * lax.rsqrt(jnp.mean(out * out, axis=-1, keepdims=True) + 1e-05) * gain).astype(bf16)
+
+
+def normed_kernel(
+    map_ref, add_ref, direct_ref, reach_ref, gain_ref, both_ref, first_ref, second_ref,
+    own_ref, next_ref, sent_ref,
+):
+    mine = lax.axis_index("ctx")
+    for head in range(map_ref.shape[0]):
         lanes = slice(head * HK, (head + 1) * HK)
-        state = states[0][head]
-        for other in states[1:]:
-            state = state + other[head]
-        high, low = split(reach_ref[:, lanes])
-        out = direct_ref[:, lanes] + dot(
-            jnp.concatenate([high, low], axis=1), jnp.concatenate([state, state], axis=0)
-        )
-        inverse = lax.rsqrt(jnp.mean(out * out, axis=-1, keepdims=True) + 1e-05)
-        out_ref[:, lanes] = (out * inverse * gain_ref[:, lanes]).astype(bf16)
-
-
-def normalize(direct, reach, gain, states):
+        gain = gain_ref[:, lanes]
+        state = first_ref[head] + second_ref[head]
+        twice = jnp.concatenate([state, state], axis=0)
+        halves = lambda x: jnp.concatenate(split(x), axis=1)
+        own_ref[:, lanes] = normed_rows(direct_ref[:, lanes], halves(reach_ref[:, lanes]), twice, gain)
+        left = (dot(halves(map_ref[head]), twice) + add_ref[head]).astype(bf16)
+        next_ref[:, lanes] = normed_rows(both_ref[0, :, lanes].astype(f32), both_ref[1, :, lanes], left, gain)
+
+    @pl.when(mine == 2)
+    def _():
+        sent_ref[...] = next_ref[...]
+
+    @pl.when(mine != 2)
+    def _():
+        sent_ref[...] = own_ref[...]
+
+
+def normed(*operands):
     vmem = pl.BlockSpec(memory_space=pltpu.VMEM)
+    direct = operands[2]
     return pl.pallas_call(
-        norm_kernel,
-        in_specs=[vmem] * (3 + len(states)),
-        out_specs=vmem,
-        out_shape=jax.ShapeDtypeStruct(direct.shape, bf16),
+        normed_kernel,
+        in_specs=[vmem] * 8,
+        out_specs=[vmem] * 3,
+        out_shape=[jax.ShapeDtypeStruct(direct.shape, bf16)] * 3,
         compiler_params=pltpu.CompilerParams(vmem_limit_bytes=16 * 2**20),
         cost_estimate=pl.CostEstimate(
-            flops=4 * direct.size * HK, bytes_accessed=10 * direct.size, transcendentals=0
+            flops=10 * direct.size * HK, bytes_accessed=16 * direct.size, transcendentals=0
         ),
-    )(direct, reach, gain, *states)
-
-
-def own_columns_kernel(rows_ref, own_ref, left_ref, right_ref, two_ref, one_ref):
-    mine = lax.axis_index("ctx")
-    rows = rows_ref[...]
-    cols = own_ref.shape[1]
-    two_ref[:, :cols] = dot(rows, own_ref[...]).astype(bf16)
-
-    @pl.when(mine < 2)
-    def _():
-        two_ref[:, cols:] = dot(rows, right_ref[...]).astype(bf16)
-        one_ref[...] = dot(rows, left_ref[...]).astype(bf16)
-
-    @pl.when(mine >= 2)
-    def _():
-        two_ref[:, cols:] = dot(rows, left_ref[...]).astype(bf16)
-        one_ref[...] = dot(rows, right_ref[...]).astype(bf16)
-
-
-def others_columns_kernel(far_ref, near_ref, own_ref, left_ref, right_ref, two_ref, one_ref):
+    )(*operands)
+
+
+def near_columns_kernel(
+    own_rows, next_rows, own_ref, left_ref, right_ref, own_two, next_two, one_ref
+):
     mine = lax.axis_index("ctx")
     cols = own_ref.shape[1]
-    far = far_ref[...]
-    two_ref[:, :cols] = dot(far, own_ref[...]).astype(bf16)
-
-    @pl.when(mine < 2)
-    def _():
-        two_ref[:, cols:] = dot(far, left_ref[...]).astype(bf16)
-        one_ref[...] = dot(near_ref[...], left_ref[...]).astype(bf16)
-
-    @pl.when(mine >= 2)
-    def _():
-        two_ref[:, cols:] = dot(far, right_ref[...]).astype(bf16)
-        one_ref[...] = dot(near_ref[...], right_ref[...]).astype(bf16)
-
-
-def columns(kernel, rows, own, left, right):
+    first, second = slice(0, cols), slice(cols, 2 * cols)
+
+    def put(out_ref, where, rows, weight):
+        out_ref[:, where] = dot(rows[...], weight[...]).astype(bf16)
+
+    @pl.when(mine < 3)
+    def _():
+        put(own_two, first, own_rows, own_ref)
+        put(own_two, second, own_rows, right_ref)
+
+    @pl.when(mine == 1)
+    def _():
+        put(next_two, first, next_rows, left_ref)
+        put(next_two, second, next_rows, own_ref)
+        put(one_ref, first, own_rows, left_ref)
+
+    @pl.when(mine == 2)
+    def _():
+        put(next_two, first, next_rows, own_ref)
+        put(next_two, second, next_rows, right_ref)
+        put(one_ref, first, next_rows, left_ref)
+
+
+def far_columns_kernel(rows_ref, own_ref, left_ref, right_ref, one_ref, last_ref):
+    mine = lax.axis_index("ctx")
+
+    @pl.when(mine == 2)
+    def _():
+        one_ref[...] = dot(rows_ref[...], right_ref[...]).astype(bf16)
+
+    @pl.when(mine != 2)
+    def _():
+        one_ref[...] = dot(rows_ref[...], left_ref[...]).astype(bf16)
+
+    @pl.when(mine == 3)
+    def _():
+        last_ref[...] = dot(rows_ref[...], own_ref[...]).astype(bf16)
+
+
+def columns(kernel, rows, widths, own, left, right):
     vmem = pl.BlockSpec(memory_space=pltpu.VMEM)
     toks, cols = rows[0].shape[0], own.shape[1]
     return pl.pallas_call(
         kernel,
         in_specs=[vmem] * (len(rows) + 3),
-        out_specs=[vmem] * 2,
-        out_shape=[
-            jax.ShapeDtypeStruct((toks, 2 * cols), bf16),
-            jax.ShapeDtypeStruct((toks, cols), bf16),
-        ],
+        out_specs=[vmem] * len(widths),
+        out_shape=[jax.ShapeDtypeStruct((toks, width * cols), bf16) for width in widths],
         compiler_params=pltpu.CompilerParams(vmem_limit_bytes=32 * 2**20),
         cost_estimate=pl.CostEstimate(
-            flops=6 * own.size * toks, bytes_accessed=8 * own.size, transcendentals=0
+            flops=2 * sum(widths) * own.size * toks, bytes_accessed=6 * own.size, transcendentals=0
         ),
     )(*rows, own, left, right)
 
 
-def assemble_kernel(own_two, own_one, far_two, near_one, out_ref, sems):
+def assemble_kernel(own_two, next_two, one, far_one, far_last, out_ref, sems):
     mine = lax.axis_index("ctx")
-    cols = own_one.shape[1]
-    first, second = pl.ds(0, cols), pl.ds(cols, cols)
+    cols = one.shape[1]
+    block = lambda ref, index: ref.at[:, pl.ds(index * cols, cols)]
     sources = (
-        (own_two.at[:, first], own_two.at[:, second], far_two.at[:, first], far_two.at[:, second]),
-        (own_one, own_two.at[:, first], own_two.at[:, second], near_one),
-        (near_one, own_two.at[:, second], own_two.at[:, first], own_one),
-        (far_two.at[:, second], far_two.at[:, first], own_two.at[:, second], own_two.at[:, first]),
+        (block(own_two, 0), block(own_two, 1), far_one, far_last),
+        (one, block(own_two, 0), block(own_two, 1), far_one),
+        (block(next_two, 0), block(next_two, 1), block(own_two, 0), block(own_two, 1)),
+        (far_one, one, block(next_two, 0), block(next_two, 1)),
     )
     for place, blocks in enumerate(sources):
 
         @pl.when(mine == place)
         def _():
             copies = [
-                pltpu.make_async_copy(
-                    block, out_ref.at[:, pl.ds(index * cols, cols)], sems.at[index]
-                )
-                for index, block in enumerate(blocks)
+                pltpu.make_async_copy(source, block(out_ref, index), sems.at[index])
+                for index, source in enumerate(blocks)
             ]
             for copy in copies:
                 copy.start()
@@ -406,13 +438,13 @@
                 copy.wait()
 
 
-def assemble(parts):
-    vmem = pl.BlockSpec(memory_space=pltpu.VMEM)
-    toks, cols = parts[1].shape
+def assemble(*parts):
+    hbm = pl.BlockSpec(memory_space=pl.ANY)
+    toks, cols = parts[-1].shape
     return pl.pallas_call(
         assemble_kernel,
-        in_specs=[vmem] * 4,
-        out_specs=pl.BlockSpec(memory_space=pl.ANY),
+        in_specs=[hbm] * len(parts),
+        out_specs=hbm,
         out_shape=jax.ShapeDtypeStruct((toks, 4 * cols), bf16),
         scratch_shapes=[pltpu.SemaphoreType.DMA((4,))],
         cost_estimate=pl.CostEstimate(
@@ -442,35 +474,38 @@
     count = lax.axis_size("ctx")
     toks = streams.shape[1]
     rim = moved(streams[0, toks - (CONV - 1) :], [(c, c + 1) for c in range(count - 1)])
-    own = w_out[0]
+    rim, own = lax.optimization_barrier((rim, w_out[0]))
     rights = [moved(own, [(c, c + 1) for c in range(count - 1)])]
     lefts = [moved(own, [(c, c - 1) for c in range(1, count)])]
     if count != 4:
         for turn in range(2, count):
             rights.append(moved(rights[-1], [(c, c + 1) for c in range(turn - 1, count - 1)]))
             lefts.append(moved(lefts[-1], [(c, c - 1) for c in range(1, count - turn + 1)]))
-    total_map, total_add, sent, direct, reach = shard_terms(
+    total_map, total_add, sent, direct, reach, both = shard_terms(
         streams[0], rim, conv_weight[0], beta_logit[0].T, gate_log[0].T
     )
-    states = [moved(sent, [(0, 1)])]
-    for turn in range(1, count - 1):
-        states.append(moved(hand_on(total_map, total_add, states[-1]), [(turn, turn + 1)]))
     if count != 4:
+        states = [moved(sent, [(0, 1)])]
+        for turn in range(1, count - 1):
+            states.append(moved(hand_on(total_map, total_add, states[-1]), [(turn, turn + 1)]))
         mixed = project(states, direct, reach, norm_gain, own, rights, lefts)
         return handed(mixed, [(c, c) for c in range(count)])[None]
-    early = normalize(direct, reach, norm_gain, states[:-1])
-    near = moved(early, [(1, 2), (2, 1)])
-    normed = normalize(direct, reach, norm_gain, states)
-    far = moved(normed, [(0, 2), (3, 1)])
-    own_two, own_one = columns(own_columns_kernel, [normed], own, rights[0], lefts[0])
-    far_two, near_one = columns(others_columns_kernel, [far, near], own, rights[0], lefts[0])
+    weights = (own, rights[0], lefts[0])
+    first = moved(sent, [(0, 1)])
+    both = moved(both, [(3, 2), (2, 1)])
+    second = moved(hand_on(total_map, total_add, first), [(1, 2)])
+    own_rows, next_rows, sent_rows = normed(
+        total_map, total_add, direct, reach, norm_gain, both, first, second
+    )
+    far_rows = moved(sent_rows, [(0, 3), (1, 2), (2, 1)])
+    own_two, next_two, one = columns(near_columns_kernel, [own_rows, next_rows], (2, 2, 1), *weights)
+    far_one, far_last = columns(far_columns_kernel, [far_rows], (1, 1), *weights)
     return assemble(
-        [
-            handed(own_two, [(c, c) for c in range(4)]),
-            handed(own_one, [(1, 1), (2, 2)]),
-            handed(far_two, [(1, 3), (2, 0)]),
-            handed(near_one, [(1, 2), (2, 1)]),
-        ]
+        handed(own_two, [(0, 0), (1, 1), (2, 2)]),
+        handed(next_two, [(1, 2), (2, 3)]),
+        handed(one, [(1, 1), (2, 3)]),
+        handed(far_one, [(3, 0), (2, 1), (1, 3)]),
+        handed(far_last, [(3, 0)]),
     )[None]
 
 

time: 85.5 us -> 94 us (1.099)
  the two profiles are of different devices: /device:TPU:8 before, /device:TPU:24 now
where the time goes in v3:
time: 94 us; the launch traced here: 93.4 us
  waiting for transfers between devices  34.5 us (37%)
  Pallas kernels  33.9 us (36%)
  starting transfers between devices  18.8 us (20%)
  local copies, waits for them, and re-layouts  5.82 us (6%)
    ppermute x7, waiting for transfers between devices, moved(): return lax.ppermute(value, 'ctx', pairs)  21.7 us
    pallas_call x1, Pallas kernels, assemble(): pl.pallas_call(assemble_kernel, in_specs=[hbm] * len(parts), out_specs=hb...  17 us
    pallas_call x1, Pallas kernels, shard_terms(): pl.pallas_call(terms_kernel, in_specs=[hbm, vmem, hbm, hbm, hbm], out_spe...  14.3 us
    ppermute x5, waiting for transfers between devices, handed(): lax.ppermute(value, ('section', 'ctx'), [(s * count + a, (s + 1) % sectio...  12.8 us
    ppermute x7, starting transfers between devices, moved(): return lax.ppermute(value, 'ctx', pairs)  12.3 us
    ppermute x5, starting transfers between devices, handed(): lax.ppermute(value, ('section', 'ctx'), [(s * count + a, (s + 1) % sectio...  6.48 us
    unnamed x22, local copies, waits for them, and re-layouts  4.91 us
  transfers between devices with their start and end apart: 12, of which 5 were waited for; matrix products, arithmetic and copies ran while one was open for 0% of the time, Pallas kernels for 18%

profile of v3, /device:TPU:24, one launch (start us, length us, event | category | flops | bytes accessed | tf_op | source)
XLA Modules:
  0.0 93.4 jit_solution(13210751509287462460)
XLA Ops:
  0.0 0.9 slice_bitcast_fusion
  0.9 1.3 %collective-permute-start = (bf16[3,5120]{1,0:T(4,128)(2,1)S(1)}, bf16[3,5120]{1,0:T(4,128)(2,1)S(1)}, u32[]{:S(2)}, u32[]{:S(2)}) collective-permute-start(bf16[3,5120]{1,0:T(4,128)(2,1)S(1)} %slice_bitcast_fusion), channel_id=1, source_target_pairs={{0,1},{1,2},{2,3},{4,5},{5,6},{6,7},{8,9},{9,10},{10,11},{12,13},{... | collective-permute-start | bytes 92168 | tf_op jit(solution)/shard_map/ppermute | solution.py:457
  2.2 4.6 %collective-permute-done.rim_ref = bf16[3,5120]{1,0:T(4,128)(2,1)S(1)} collective-permute-done((bf16[3,5120]{1,0:T(4,128)(2,1)S(1)}, bf16[3,5120]{1,0:T(4,128)(2,1)S(1)}, u32[]{:S(2)}, u32[]{:S(2)}) %collective-permute-start) | collective-permute-done | bytes 30752 | tf_op jit(solution)/shard_map/ppermute | solution.py:457
  6.8 1.3 %collective-permute-start.4 = (bf16[1024,512]{1,0:T(8,128)(2,1)}, bf16[1024,512]{1,0:T(8,128)(2,1)S(1)}, u32[]{:S(2)}, u32[]{:S(2)}) collective-permute-start(bf16[1024,512]{1,0:T(8,128)(2,1)} %bitcast.12), channel_id=1, source_target_pairs={{0,1},{1,2},{2,3},{4,5},{5,6},{6,7},{8,9},{9,10},{10,11},{12,13},{... | collective-permute-start | bytes 3145736 | tf_op jit(solution)/shard_map/ppermute | solution.py:457
  8.1 4.6 %collective-permute-start.5 = (bf16[1024,512]{1,0:T(8,128)(2,1)}, bf16[1024,512]{1,0:T(8,128)(2,1)S(1)}, u32[]{:S(2)}, u32[]{:S(2)}) collective-permute-start(bf16[1024,512]{1,0:T(8,128)(2,1)} %bitcast.13), channel_id=1, source_target_pairs={{1,0},{2,1},{3,2},{5,4},{6,5},{7,6},{9,8},{10,9},{11,10},{13,12},{... | collective-permute-start | bytes 3145736 | tf_op jit(solution)/shard_map/ppermute | solution.py:457
  12.7 1.3 %copy-done.2 = bf16[1,128,5120]{2,1,0:T(8,128)(2,1)S(1)} copy-done((bf16[1,128,5120]{2,1,0:T(8,128)(2,1)S(1)}, bf16[1,128,5120]{2,1,0:T(8,128)(2,1)}, u32[]{:S(2)}) %copy-start.2) | copy-done | bytes 1310744
  14.0 0.8 copy-done.3
  14.8 0.7 copy-done.4
  15.5 0.7 copy-done.5
  16.2 14.3 %shard_map.64 = (f32[8,128,128]{2,1,0:T(8,128)S(1)}, f32[8,128,128]{2,1,0:T(8,128)S(1)}, bf16[8,128,128]{2,1,0:T(8,128)(2,1)S(1)}, f32[128,1024]{1,0:T(8,128)S(1...) custom-call(bf16[128,5120]{1,0:T(8,128)(2,1)S(1)} %bitcast.16, ...), custom_call_target="tpu_custom_call" | custom-call | flops 2013265920 | bytes 4194304 | tf_op jit(solution)/shard_map/pallas_call | solution.py:204
  30.5 0.7 collective-permute-start.2
  31.2 2.5 %collective-permute-start.1 = (bf16[2,128,1024]{2,1,0:T(8,128)(2,1)S(1)}, bf16[2,128,1024]{2,1,0:T(8,128)(2,1)S(1)}, u32[]{:S(2)}, u32[]{:S(2)}) collective-permute-start(bf16[2,128,1024]{2,1,0:T(8,128)(2,1)S(1)} %get-tuple-element.26), channel_id=1, source_target_pairs={{3,2},{2,1},{7,6},{6,5},{11,10},{10,9},{15,14},{14,13},{19,18},{18... | collective-permute-start | bytes 1572872 | tf_op jit(solution)/shard_map/ppermute | solution.py:457
  34.7 10.3 %collective-permute-done.1.both_ref = bf16[2,128,1024]{2,1,0:T(8,128)(2,1)S(1)} collective-permute-done((bf16[2,128,1024]{2,1,0:T(8,128)(2,1)S(1)}, bf16[2,128,1024]{2,1,0:T(8,128)(2,1)S(1)}, u32[]{:S(2)}, u32[]{:S(2)}) %collective-permute-start.1) | collective-permute-done | bytes 524320 | tf_op jit(solution)/shard_map/ppermute | solution.py:457
  45.1 1.6 %shard_map.66 = (bf16[128,1024]{1,0:T(8,128)(2,1)S(1)}, bf16[128,1024]{1,0:T(8,128)(2,1)S(1)}, bf16[128,1024]{1,0:T(8,128)(2,1)S(1)}) custom-call(f32[8,128,128]{2,1,0:T(8,128)S(1)} %get-tuple-element.22.map_ref, f32[8,128,128]{2,1,0:T(8,128)S(1)} %get-tuple-element.23.add_ref, f32[128,1024]{1,0:T(8,128)S(1)} %get-tuple-element.24.direct_ref, ...), custom_call_target="tpu_custom_call" | custom-call | flops 167772160 | bytes 2097152 | tf_op jit(solution)/shard_map/pallas_call | solution.py:346
  46.7 1.3 %collective-permute-start.9 = (bf16[128,1024]{1,0:T(8,128)(2,1)S(1)}, bf16[128,1024]{1,0:T(8,128)(2,1)S(1)}, u32[]{:S(2)}, u32[]{:S(2)}) collective-permute-start(bf16[128,1024]{1,0:T(8,128)(2,1)S(1)} %get-tuple-element.34), channel_id=1, source_target_pairs={{0,3},{1,2},{2,1},{4,7},{5,6},{6,5},{8,11},{9,10},{10,9},{12,15},{... | collective-permute-start | bytes 786440 | tf_op jit(solution)/shard_map/ppermute | solution.py:457
  48.8 1.3 %collective-permute-start.7 = (bf16[128,1024]{1,0:T(8,128)(2,1)S(1)}, bf16[128,1024]{1,0:T(8,128)(2,1)S(1)}, u32[]{:S(2)}, u32[]{:S(2)}) collective-permute-start(bf16[128,1024]{1,0:T(8,128)(2,1)S(1)} %get-tuple-element.32), channel_id=1, source_target_pairs={{1,6},{2,7},{5,10},{6,11},{9,14},{10,15},{13,18},{14,19},{17,22},{... | collective-permute-start | bytes 786440 | tf_op jit(solution)/shard_map/ppermute | solution.py:462
  50.1 6.8 %collective-permute-done.9.rows_ref = bf16[128,1024]{1,0:T(8,128)(2,1)S(1)} collective-permute-done((bf16[128,1024]{1,0:T(8,128)(2,1)S(1)}, bf16[128,1024]{1,0:T(8,128)(2,1)S(1)}, u32[]{:S(2)}, u32[]{:S(2)}) %collective-permute-start.9) | collective-permute-done | bytes 262176 | tf_op jit(solution)/shard_map/ppermute | solution.py:457
  57.5 1.9 %collective-permute-start.10 = (bf16[128,512]{1,0:T(8,128)(2,1)S(1)}, bf16[128,512]{1,0:T(8,128)(2,1)S(1)}, u32[]{:S(2)}, u32[]{:S(2)}) collective-permute-start(bf16[128,512]{1,0:T(8,128)(2,1)S(1)} %get-tuple-element.35), channel_id=1, source_target_pairs={{3,4},{2,5},{1,7},{7,8},{6,9},{5,11},{11,12},{10,13},{9,15},{15,16... | collective-permute-start | bytes 393224 | tf_op jit(solution)/shard_map/ppermute | solution.py:462
  59.4 1.3 %collective-permute-start.11 = (bf16[128,512]{1,0:T(8,128)(2,1)S(1)}, bf16[128,512]{1,0:T(8,128)(2,1)S(1)}, u32[]{:S(2)}, u32[]{:S(2)}) collective-permute-start(bf16[128,512]{1,0:T(8,128)(2,1)S(1)} %get-tuple-element.36), channel_id=1, source_target_pairs={{3,4},{7,8},{11,12},{15,16},{19,20},{23,24},{27,28},{31,0}} | collective-permute-start | bytes 393224 | tf_op jit(solution)/shard_map/ppermute | solution.py:462
  60.7 1.3 %collective-permute-start.8 = (bf16[128,512]{1,0:T(8,128)(2,1)S(1)}, bf16[128,512]{1,0:T(8,128)(2,1)S(1)}, u32[]{:S(2)}, u32[]{:S(2)}) collective-permute-start(bf16[128,512]{1,0:T(8,128)(2,1)S(1)} %get-tuple-element.33), channel_id=1, source_target_pairs={{1,5},{2,7},{5,9},{6,11},{9,13},{10,15},{13,17},{14,19},{17,21},{1... | collective-permute-start | bytes 393224 | tf_op jit(solution)/shard_map/ppermute | solution.py:462
  62.0 10.6 %collective-permute-done.10.far_one = bf16[128,512]{1,0:T(8,128)(2,1)S(1)} collective-permute-done((bf16[128,512]{1,0:T(8,128)(2,1)S(1)}, bf16[128,512]{1,0:T(8,128)(2,1)S(1)}, u32[]{:S(2)}, u32[]{:S(2)}) %collective-permute-start.10) | collective-permute-done | bytes 131104 | tf_op jit(solution)/shard_map/ppermute | solution.py:462
  72.6 2.2 %collective-permute-done.8.one = bf16[128,512]{1,0:T(8,128)(2,1)S(1)} collective-permute-done((bf16[128,512]{1,0:T(8,128)(2,1)S(1)}, bf16[128,512]{1,0:T(8,128)(2,1)S(1)}, u32[]{:S(2)}, u32[]{:S(2)}) %collective-permute-start.8) | collective-permute-done | bytes 131104 | tf_op jit(solution)/shard_map/ppermute | solution.py:462
  75.5 0.7 copy-done.7
  76.2 17.0 %shard_map.69 = bf16[128,2048]{1,0:T(8,128)(2,1)} custom-call(bf16[128,1024]{1,0:T(8,128)(2,1)} %copy-done.6, bf16[128,1024]{1,0:T(8,128)(2,1)} %copy-done.7, bf16[128,512]{1,0:T(8,128)(2,1)} %copy-done.10, bf16[128,512]{1,0:T(8,128)(2,1)} %copy-done.8, bf16[128,512]{1,0:T(8,128)(2,1)} %copy-done.9), custom_call_target="tpu_custom_call" | custom-call | bytes 1048576 | tf_op jit(solution)/shard_map/pallas_call | solution.py:444
  (29 shorter events, 3.1 us)
Async XLA Ops:
  0.9 5.9 %collective-permute-start = (bf16[3,5120]{1,0:T(4,128)(2,1)S(1)}, bf16[3,5120]{1,0:T(4,128)(2,1)S(1)}, u32[]{:S(2)}, u32[]{:S(2)}) collective-permute-start(bf16[3,5120]{1,0:T(4,128)(2,1)S(1)} %slice_bitcast_fusion), channel_id=1, source_target_pairs={{0,1},{1,2},{2,3},{4,5},{5,6},{6,7},{8,9},{9,10},{10,11},{12,13},{... | collective-permute-start | bytes 92168 | tf_op jit(solution)/shard_map/ppermute | solution.py:457
  6.8 41.2 %collective-permute-start.4 = (bf16[1024,512]{1,0:T(8,128)(2,1)}, bf16[1024,512]{1,0:T(8,128)(2,1)S(1)}, u32[]{:S(2)}, u32[]{:S(2)}) collective-permute-start(bf16[1024,512]{1,0:T(8,128)(2,1)} %bitcast.12), channel_id=1, source_target_pairs={{0,1},{1,2},{2,3},{4,5},{5,6},{6,7},{8,9},{9,10},{10,11},{12,13},{... | collective-permute-start | bytes 3145736 | tf_op jit(solution)/shard_map/ppermute | solution.py:457
  8.1 39.9 %collective-permute-start.5 = (bf16[1024,512]{1,0:T(8,128)(2,1)}, bf16[1024,512]{1,0:T(8,128)(2,1)S(1)}, u32[]{:S(2)}, u32[]{:S(2)}) collective-permute-start(bf16[1024,512]{1,0:T(8,128)(2,1)} %bitcast.13), channel_id=1, source_target_pairs={{1,0},{2,1},{3,2},{5,4},{6,5},{7,6},{9,8},{10,9},{11,10},{13,12},{... | collective-permute-start | bytes 3145736 | tf_op jit(solution)/shard_map/ppermute | solution.py:457
  12.7 1.3 %copy-start.2 = (bf16[1,128,5120]{2,1,0:T(8,128)(2,1)S(1)}, bf16[1,128,5120]{2,1,0:T(8,128)(2,1)}, u32[]{:S(2)}) copy-start(bf16[1,128,5120]{2,1,0:T(8,128)(2,1)} %param.6) | copy-start | bytes 3932164
  14.0 0.8 copy-start.3
  14.8 0.7 copy-start.4
  15.5 0.7 copy-start.5
  30.5 14.6 %copy-start.1 = (f32[1,1024]{1,0:T(1,128)S(1)}, f32[1,1024]{1,0:T(1,128)}, u32[]{:S(2)}) copy-start(f32[1,1024]{1,0:T(1,128)} %gain_ref.1) | copy-start | bytes 12292
  30.5 3.2 %collective-permute-start.2 = (bf16[8,128,128]{2,1,0:T(8,128)(2,1)S(1)}, bf16[8,128,128]{2,1,0:T(8,128)(2,1)S(1)}, u32[]{:S(2)}, u32[]{:S(2)}) collective-permute-start(bf16[8,128,128]{2,1,0:T(8,128)(2,1)S(1)} %get-tuple-element.27), channel_id=1, source_target_pairs={{0,1},{4,5},{8,9},{12,13},{16,17},{20,21},{24,25},{28,29}} | collective-permute-start | bytes 786440 | tf_op jit(solution)/shard_map/ppermute | solution.py:457
  31.2 13.9 %collective-permute-start.1 = (bf16[2,128,1024]{2,1,0:T(8,128)(2,1)S(1)}, bf16[2,128,1024]{2,1,0:T(8,128)(2,1)S(1)}, u32[]{:S(2)}, u32[]{:S(2)}) collective-permute-start(bf16[2,128,1024]{2,1,0:T(8,128)(2,1)S(1)} %get-tuple-element.26), channel_id=1, source_target_pairs={{3,2},{2,1},{7,6},{6,5},{11,10},{10,9},{15,14},{14,13},{19,18},{18... | collective-permute-start | bytes 1572872 | tf_op jit(solution)/shard_map/ppermute | solution.py:457
  34.0 0.7 collective-permute-start.3
  45.1 3.0 %copy-start = (bf16[1,1024,512]{2,1,0:T(8,128)(2,1)S(1)}, bf16[1,1024,512]{2,1,0:T(8,128)(2,1)}, u32[]{:S(2)}) copy-start(bf16[1,1024,512]{2,1,0:T(8,128)(2,1)} %param.11) | copy-start | bytes 3145732
  46.7 10.1 %collective-permute-start.9 = (bf16[128,1024]{1,0:T(8,128)(2,1)S(1)}, bf16[128,1024]{1,0:T(8,128)(2,1)S(1)}, u32[]{:S(2)}, u32[]{:S(2)}) collective-permute-start(bf16[128,1024]{1,0:T(8,128)(2,1)S(1)} %get-tuple-element.34), channel_id=1, source_target_pairs={{0,3},{1,2},{2,1},{4,7},{5,6},{6,5},{8,11},{9,10},{10,9},{12,15},{... | collective-permute-start | bytes 786440 | tf_op jit(solution)/shard_map/ppermute | solution.py:457
  48.1 26.7 %collective-permute-start.6 = (bf16[128,1024]{1,0:T(8,128)(2,1)S(1)}, bf16[128,1024]{1,0:T(8,128)(2,1)S(1)}, u32[]{:S(2)}, u32[]{:S(2)}) collective-permute-start(bf16[128,1024]{1,0:T(8,128)(2,1)S(1)} %get-tuple-element.31), channel_id=1, source_target_pairs={{0,4},{1,5},{2,6},{4,8},{5,9},{6,10},{8,12},{9,13},{10,14},{12,16}... | collective-permute-start | bytes 786440 | tf_op jit(solution)/shard_map/ppermute | solution.py:462
  48.8 26.0 %collective-permute-start.7 = (bf16[128,1024]{1,0:T(8,128)(2,1)S(1)}, bf16[128,1024]{1,0:T(8,128)(2,1)S(1)}, u32[]{:S(2)}, u32[]{:S(2)}) collective-permute-start(bf16[128,1024]{1,0:T(8,128)(2,1)S(1)} %get-tuple-element.32), channel_id=1, source_target_pairs={{1,6},{2,7},{5,10},{6,11},{9,14},{10,15},{13,18},{14,19},{17,22},{... | collective-permute-start | bytes 786440 | tf_op jit(solution)/shard_map/ppermute | solution.py:462
  57.5 15.1 %collective-permute-start.10 = (bf16[128,512]{1,0:T(8,128)(2,1)S(1)}, bf16[128,512]{1,0:T(8,128)(2,1)S(1)}, u32[]{:S(2)}, u32[]{:S(2)}) collective-permute-start(bf16[128,512]{1,0:T(8,128)(2,1)S(1)} %get-tuple-element.35), channel_id=1, source_target_pairs={{3,4},{2,5},{1,7},{7,8},{6,9},{5,11},{11,12},{10,13},{9,15},{15,16... | collective-permute-start | bytes 393224 | tf_op jit(solution)/shard_map/ppermute | solution.py:462
  59.4 13.2 %collective-permute-start.11 = (bf16[128,512]{1,0:T(8,128)(2,1)S(1)}, bf16[128,512]{1,0:T(8,128)(2,1)S(1)}, u32[]{:S(2)}, u32[]{:S(2)}) collective-permute-start(bf16[128,512]{1,0:T(8,128)(2,1)S(1)} %get-tuple-element.36), channel_id=1, source_target_pairs={{3,4},{7,8},{11,12},{15,16},{19,20},{23,24},{27,28},{31,0}} | collective-permute-start | bytes 393224 | tf_op jit(solution)/shard_map/ppermute | solution.py:462
  60.7 14.1 %collective-permute-start.8 = (bf16[128,512]{1,0:T(8,128)(2,1)S(1)}, bf16[128,512]{1,0:T(8,128)(2,1)S(1)}, u32[]{:S(2)}, u32[]{:S(2)}) collective-permute-start(bf16[128,512]{1,0:T(8,128)(2,1)S(1)} %get-tuple-element.33), channel_id=1, source_target_pairs={{1,5},{2,7},{5,9},{6,11},{9,13},{10,15},{13,17},{14,19},{17,21},{1... | collective-permute-start | bytes 393224 | tf_op jit(solution)/shard_map/ppermute | solution.py:462
  72.6 2.2 %copy-start.8 = (bf16[128,512]{1,0:T(8,128)(2,1)}, bf16[128,512]{1,0:T(8,128)(2,1)S(1)}, u32[]{:S(2)}) copy-start(bf16[128,512]{1,0:T(8,128)(2,1)S(1)} %collective-permute-done.10.far_one) | copy-start | bytes 393220
  72.6 2.2 %copy-start.9 = (bf16[128,512]{1,0:T(8,128)(2,1)}, bf16[128,512]{1,0:T(8,128)(2,1)S(1)}, u32[]{:S(2)}) copy-start(bf16[128,512]{1,0:T(8,128)(2,1)S(1)} %collective-permute-done.11.far_last) | copy-start | bytes 393220
  74.8 0.7 copy-start.10
  74.8 0.8 copy-start.6
  75.5 0.7 copy-start.7

commit v4 on v2

--- a/solution.py
+++ b/solution.py
@@ -144,12 +144,33 @@
     return acts
 
 
-def later_kernel(x_ref, taps_ref, beta_ref, gate_ref, map_ref, add_ref, direct_ref, reach_ref, ext):
+def load_kernel(*refs):
+    sources, targets, edge_ref, sems = refs[:4], refs[4:8], refs[8], refs[9]
+    copies = [
+        pltpu.make_async_copy(source, target, sems.at[index])
+        for index, (source, target) in enumerate(zip(sources, targets))
+    ]
+    for copy in copies:
+        copy.start()
+    for copy in copies:
+        copy.wait()
+    toks = targets[0].shape[0]
+    edge_ref[...] = targets[0][toks - 16 :].astype(f32)[16 - (CONV - 1) :].astype(bf16)
+
+
+def conv_kernel(x_ref, taps_ref, out_ref, ext):
+    half, channels = out_ref.shape
+    ext[...] = x_ref[half - 16 :].astype(f32)[8:]
+    width = channels // 5
+    for part, act in enumerate(activations(ext, taps_ref, half, width // HK)):
+        out_ref[:, part * width : (part + 1) * width] = act
+
+
+def later_kernel(act_ref, beta_ref, gate_ref, map_ref, add_ref, direct_ref, reach_ref):
     heads, toks = gate_ref.shape
-    half = toks // 2
-    ext[...] = x_ref[half - 16 :].astype(f32)[8:]
-    acts = activations(ext, taps_ref, half, heads)
-    found = half_terms(1, heads, half, acts, beta_ref[...], gate_ref[...])
+    width = heads * HK
+    acts = [act_ref[:, part * width : (part + 1) * width] for part in range(5)]
+    found = half_terms(1, heads, toks // 2, acts, beta_ref[...], gate_ref[...])
     for head, (map2, add2, direct2, reach2) in enumerate(found):
         lanes = slice(head * HK, (head + 1) * HK)
         map_ref[head] = map2
@@ -159,8 +180,8 @@
 
 
 def earlier_kernel(
-    x_ref, rim_ref, taps_ref, beta_ref, gate_ref, map2_ref, add2_ref, direct2_ref, reach2_ref,
-    map_ref, add_ref, sent_ref, direct_ref, reach_ref, ext,
+    rim_ref, x_ref, taps_ref, beta_ref, gate_ref, map2_ref, add2_ref, direct2_ref, reach2_ref,
+    map_ref, add_ref, sent_ref, direct_ref, reach_ref, both_ref, ext,
 ):
     heads, toks = gate_ref.shape
     half = toks // 2
@@ -178,42 +199,71 @@
         map_ref[head] = joined[:HK, :HK]
         add_ref[head] = total
         sent_ref[head] = total.astype(bf16)
-        direct_ref[:half, lanes] = direct1
-        direct_ref[half:, lanes] = joined[HK:, HK:] + direct2_ref[:, lanes]
-        reach_ref[:half, lanes] = reach1
-        reach_ref[half:, lanes] = joined[HK:, :HK]
-
-
-def shard_terms(streams, rim, conv_weight, beta_t, gate_t):
-    toks, channels = streams.shape
+        for rows, direct, reach in (
+            (slice(0, half), direct1, reach1),
+            (slice(half, toks), joined[HK:, HK:] + direct2_ref[:, lanes], joined[HK:, :HK]),
+        ):
+            direct_ref[rows, lanes] = direct
+            reach_ref[rows, lanes] = reach
+            both_ref[0, rows, lanes] = direct.astype(bf16)
+            both_ref[1, rows, lanes] = reach.astype(bf16)
+
+
+def kernel_call(kernel, operands, out_shapes, limit=16, scratch=(), cost=2**16, space=pltpu.VMEM):
+    return pl.pallas_call(
+        kernel,
+        in_specs=[pl.BlockSpec(memory_space=space)] * len(operands),
+        out_specs=[pl.BlockSpec(memory_space=pltpu.VMEM)] * len(out_shapes),
+        out_shape=[jax.ShapeDtypeStruct(*shape) for shape in out_shapes],
+        scratch_shapes=scratch,
+        compiler_params=pltpu.CompilerParams(vmem_limit_bytes=limit * 2**20),
+        cost_estimate=pl.CostEstimate(flops=2**20, bytes_accessed=cost, transcendentals=0),
+    )(*operands)
+
+
+def load(*sources):
+    sources = [pltpu.with_memory_space_constraint(x, pltpu.HBM) for x in sources]
+    edge = ((CONV - 1, sources[0].shape[1]), bf16)
+    return pl.pallas_call(
+        load_kernel,
+        in_specs=[pl.BlockSpec(memory_space=pltpu.HBM)] * len(sources),
+        out_specs=[pl.BlockSpec(memory_space=pltpu.VMEM)] * (len(sources) + 1),
+        out_shape=[pltpu.VMEM(x.shape, x.dtype) for x in sources] + [pltpu.VMEM(*edge)],
+        scratch_shapes=[pltpu.SemaphoreType.DMA((len(sources),))],
+        compiler_params=pltpu.CompilerParams(vmem_limit_bytes=2**22),
+    )(*sources)
+
+
+def later_activations(x, taps):
+    toks, channels = x.shape
+    half = toks // 2
+    return kernel_call(
+        conv_kernel,
+        (x, taps),
+        [((half, channels), f32)],
+        scratch=[pltpu.VMEM((8 + half, channels), f32)],
+        cost=2**27,
+    )[0]
+
+
+def shard_terms(later_acts, rim, x, taps, beta_t, gate_t):
+    toks, channels = x.shape
     heads = gate_t.shape[0]
     half = toks // 2
-    vmem = pl.BlockSpec(memory_space=pltpu.VMEM)
-    shape = jax.ShapeDtypeStruct
-    square = (heads, HK, HK)
-    params = dict(
-        scratch_shapes=[pltpu.VMEM((8 + half, channels), f32)],
-        compiler_params=pltpu.CompilerParams(vmem_limit_bytes=40 * 2**20),
-        cost_estimate=pl.CostEstimate(
-            flops=30 * heads * HK**3 * 2, bytes_accessed=4 * 2**20, transcendentals=0
-        ),
-    )
-    later = pl.pallas_call(
+    square, rows, half_rows = (heads, HK, HK), (toks, heads * HK), (half, heads * HK)
+    later = kernel_call(
         later_kernel,
-        in_specs=[vmem] * 4,
-        out_specs=[vmem] * 4,
-        out_shape=[shape(square, f32)] * 2 + [shape((half, heads * HK), f32)] * 2,
-        **params,
-    )(streams, conv_weight, beta_t, gate_t)
-    return pl.pallas_call(
+        (later_acts, beta_t, gate_t),
+        [(square, f32)] * 2 + [(half_rows, f32)] * 2,
+        limit=32,
+    )
+    return kernel_call(
         earlier_kernel,
-        in_specs=[vmem] * 9,
-        out_specs=[vmem] * 5,
-        out_shape=[shape(square, f32)] * 2
-        + [shape(square, bf16)]
-        + [shape((toks, heads * HK), f32)] * 2,
-        **params,
-    )(streams, rim, conv_weight, beta_t, gate_t, *later)
+        (rim, x, taps, beta_t, gate_t, *later),
+        [(square, f32)] * 2 + [(square, bf16)] + [(rows, f32)] * 2 + [((2,) + rows, bf16)],
+        limit=32,
+        scratch=[pltpu.VMEM((8 + half, channels), f32)],
+    )
 
 
 def hand_on_kernel(map_ref, add_ref, state_ref, out_ref):
@@ -299,126 +349,138 @@
     )(*states, direct, reach, gain, own, *rights, *lefts)
 
 
-def norm_kernel(direct_ref, reach_ref, gain_ref, *refs):
-    states, out_ref = refs[:-1], refs[-1]
-    for head in range(states[0].shape[0]):
-        lanes = slice(head * HK, (head + 1) * HK)
-        state = states[0][head]
-        for other in states[1:]:
-            state = state + other[head]
-        high, low = split(reach_ref[:, lanes])
+def on_shard(place):
+    return pl.when(lax.axis_index("ctx") == place)
+
+
+def head_lanes(heads):
+    return [(head, slice(head * HK, (head + 1) * HK)) for head in range(heads)]
+
+
+def normed_rows(out, gain):
+    return (out * lax.rsqrt(jnp.mean(out * out, axis=-1, keepdims=True) + 1e-05) * gain).astype(bf16)
+
+
+def project_to(out_ref, rows, *weights):
+    cols = weights[0].shape[1]
+    for index, weight in enumerate(weights):
+        out_ref[:, index * cols : (index + 1) * cols] = dot(rows, weight[...]).astype(bf16)
+
+
+def rows_with_state(direct_ref, reach_ref, gain_ref, state_ref, out_ref):
+    for head, lanes in head_lanes(state_ref.shape[0]):
+        state = state_ref[head]
         out = direct_ref[:, lanes] + dot(
-            jnp.concatenate([high, low], axis=1), jnp.concatenate([state, state], axis=0)
-        )
-        inverse = lax.rsqrt(jnp.mean(out * out, axis=-1, keepdims=True) + 1e-05)
-        out_ref[:, lanes] = (out * inverse * gain_ref[:, lanes]).astype(bf16)
-
-
-def normalize(direct, reach, gain, states):
+            jnp.concatenate(split(reach_ref[:, lanes]), axis=1), jnp.concatenate([state, state], axis=0)
+        )
+        out_ref[:, lanes] = normed_rows(out, gain_ref[:, lanes])
+
+
+def rows_of_next(both_ref, gain_ref, head, lanes, state):
+    out = both_ref[0, :, lanes].astype(f32) + dot(both_ref[1, :, lanes], state)
+    return normed_rows(out, gain_ref[:, lanes])
+
+
+def first_rows_kernel(direct_ref, gain_ref, out_ref):
+    @on_shard(0)
+    def _():
+        for head, lanes in head_lanes(direct_ref.shape[1] // HK):
+            out_ref[:, lanes] = normed_rows(direct_ref[:, lanes], gain_ref[:, lanes])
+
+
+def second_rows_kernel(direct_ref, reach_ref, gain_ref, state_ref, out_ref):
+    @on_shard(1)
+    def _():
+        rows_with_state(direct_ref, reach_ref, gain_ref, state_ref, out_ref)
+
+
+def third_columns_kernel(both_ref, gain_ref, state_ref, left_ref, out_ref, rows_ref):
+    @on_shard(1)
+    def _():
+        for head, lanes in head_lanes(state_ref.shape[0]):
+            rows_ref[:, lanes] = rows_of_next(both_ref, gain_ref, head, lanes, state_ref[head])
+        project_to(out_ref, rows_ref[...], left_ref)
+
+
+def fourth_rows_kernel(map_ref, add_ref, both_ref, gain_ref, state_ref, out_ref):
+    @on_shard(2)
+    def _():
+        for head, lanes in head_lanes(state_ref.shape[0]):
+            state = state_ref[head]
+            left = add_ref[head] + dot(
+                jnp.concatenate(split(map_ref[head]), axis=1), jnp.concatenate([state, state], axis=0)
+            )
+            out_ref[:, lanes] = rows_of_next(both_ref, gain_ref, head, lanes, left.astype(bf16))
+
+
+def near_columns_kernel(
+    direct_ref, reach_ref, gain_ref, state_ref, rows0_ref, rows1_ref, rows3_ref, own_ref, left_ref, right_ref,
+    own_three, next_three, rows_ref,
+):
+    weights = (own_ref, right_ref, left_ref)
+
+    @on_shard(0)
+    def _():
+        project_to(own_three, rows0_ref[...], *weights[:2])
+
+    @on_shard(1)
+    def _():
+        project_to(own_three, rows1_ref[...], *weights)
+
+    @on_shard(2)
+    def _():
+        project_to(next_three, rows3_ref[...], *weights)
+        rows_with_state(direct_ref, reach_ref, gain_ref, state_ref, rows_ref)
+        project_to(own_three, rows_ref[...], *weights)
+
+
+def first_columns_kernel(rows_ref, own_ref, left_ref, out_ref):
+    @on_shard(3)
+    def _():
+        project_to(out_ref, rows_ref[...], left_ref, own_ref)
+
+
+def far_columns_kernel(rows1_ref, rows3_ref, left_ref, right_ref, out_ref):
+    @on_shard(1)
+    def _():
+        project_to(out_ref, rows3_ref[...], left_ref)
+
+    @on_shard(2)
+    def _():
+        project_to(out_ref, rows1_ref[...], right_ref)
+
+
+def call(kernel, operands, out_shapes, scratch=()):
     vmem = pl.BlockSpec(memory_space=pltpu.VMEM)
-    return pl.pallas_call(
-        norm_kernel,
-        in_specs=[vmem] * (3 + len(states)),
-        out_specs=vmem,
-        out_shape=jax.ShapeDtypeStruct(direct.shape, bf16),
+    shapes = [jax.ShapeDtypeStruct(shape, bf16) for shape in out_shapes]
+    found = pl.pallas_call(
+        kernel,
+        in_specs=[vmem] * len(operands),
+        out_specs=[vmem] * len(shapes),
+        out_shape=shapes,
+        scratch_shapes=[pltpu.VMEM(shape, bf16) for shape in scratch],
         compiler_params=pltpu.CompilerParams(vmem_limit_bytes=16 * 2**20),
-        cost_estimate=pl.CostEstimate(
-            flops=4 * direct.size * HK, bytes_accessed=10 * direct.size, transcendentals=0
-        ),
-    )(direct, reach, gain, *states)
-
-
-def own_columns_kernel(rows_ref, own_ref, left_ref, right_ref, two_ref, one_ref):
-    mine = lax.axis_index("ctx")
-    rows = rows_ref[...]
-    cols = own_ref.shape[1]
-    two_ref[:, :cols] = dot(rows, own_ref[...]).astype(bf16)
-
-    @pl.when(mine < 2)
-    def _():
-        two_ref[:, cols:] = dot(rows, right_ref[...]).astype(bf16)
-        one_ref[...] = dot(rows, left_ref[...]).astype(bf16)
-
-    @pl.when(mine >= 2)
-    def _():
-        two_ref[:, cols:] = dot(rows, left_ref[...]).astype(bf16)
-        one_ref[...] = dot(rows, right_ref[...]).astype(bf16)
-
-
-def others_columns_kernel(far_ref, near_ref, own_ref, left_ref, right_ref, two_ref, one_ref):
-    mine = lax.axis_index("ctx")
-    cols = own_ref.shape[1]
-    far = far_ref[...]
-    two_ref[:, :cols] = dot(far, own_ref[...]).astype(bf16)
-
-    @pl.when(mine < 2)
-    def _():
-        two_ref[:, cols:] = dot(far, left_ref[...]).astype(bf16)
-        one_ref[...] = dot(near_ref[...], left_ref[...]).astype(bf16)
-
-    @pl.when(mine >= 2)
-    def _():
-        two_ref[:, cols:] = dot(far, right_ref[...]).astype(bf16)
-        one_ref[...] = dot(near_ref[...], right_ref[...]).astype(bf16)
-
-
-def columns(kernel, rows, own, left, right):
-    vmem = pl.BlockSpec(memory_space=pltpu.VMEM)
-    toks, cols = rows[0].shape[0], own.shape[1]
-    return pl.pallas_call(
-        kernel,
-        in_specs=[vmem] * (len(rows) + 3),
-        out_specs=[vmem] * 2,
-        out_shape=[
-            jax.ShapeDtypeStruct((toks, 2 * cols), bf16),
-            jax.ShapeDtypeStruct((toks, cols), bf16),
-        ],
-        compiler_params=pltpu.CompilerParams(vmem_limit_bytes=32 * 2**20),
-        cost_estimate=pl.CostEstimate(
-            flops=6 * own.size * toks, bytes_accessed=8 * own.size, transcendentals=0
-        ),
-    )(*rows, own, left, right)
-
-
-def assemble_kernel(own_two, own_one, far_two, near_one, out_ref, sems):
-    mine = lax.axis_index("ctx")
-    cols = own_one.shape[1]
-    first, second = pl.ds(0, cols), pl.ds(cols, cols)
+        cost_estimate=pl.CostEstimate(flops=2**20, bytes_accessed=2**16, transcendentals=0),
+    )(*operands)
+    return found if len(shapes) > 1 else found[0]
+
+
+def assemble_kernel(own_three, next_three, third_one, first_two, far_one, out_ref):
+    cols = far_one.shape[1]
+    own = [(own_three, index) for index in range(3)]
+    after = [(next_three, index) for index in range(3)]
     sources = (
-        (own_two.at[:, first], own_two.at[:, second], far_two.at[:, first], far_two.at[:, second]),
-        (own_one, own_two.at[:, first], own_two.at[:, second], near_one),
-        (near_one, own_two.at[:, second], own_two.at[:, first], own_one),
-        (far_two.at[:, second], far_two.at[:, first], own_two.at[:, second], own_two.at[:, first]),
+        (own[0], own[1], (first_two, 0), (first_two, 1)),
+        (own[2], own[0], own[1], (far_one, 0)),
+        ((third_one, 0), own[2], own[0], own[1]),
+        ((far_one, 0), after[2], after[0], after[1]),
     )
     for place, blocks in enumerate(sources):
 
-        @pl.when(mine == place)
+        @on_shard(place)
         def _():
-            copies = [
-                pltpu.make_async_copy(
-                    block, out_ref.at[:, pl.ds(index * cols, cols)], sems.at[index]
-                )
-                for index, block in enumerate(blocks)
-            ]
-            for copy in copies:
-                copy.start()
-            for copy in copies:
-                copy.wait()
-
-
-def assemble(parts):
-    vmem = pl.BlockSpec(memory_space=pltpu.VMEM)
-    toks, cols = parts[1].shape
-    return pl.pallas_call(
-        assemble_kernel,
-        in_specs=[vmem] * 4,
-        out_specs=pl.BlockSpec(memory_space=pl.ANY),
-        out_shape=jax.ShapeDtypeStruct((toks, 4 * cols), bf16),
-        scratch_shapes=[pltpu.SemaphoreType.DMA((4,))],
-        cost_estimate=pl.CostEstimate(
-            flops=0, bytes_accessed=16 * toks * cols, transcendentals=0
-        ),
-    )(*parts)
+            for index, (ref, block) in enumerate(blocks):
+                out_ref[:, index * cols : (index + 1) * cols] = ref[:, block * cols : (block + 1) * cols]
 
 
 def moved(value, pairs):
@@ -440,37 +502,65 @@
 
 def on_device(streams, conv_weight, beta_logit, gate_log, norm_gain, w_out):
     count = lax.axis_size("ctx")
-    toks = streams.shape[1]
-    rim = moved(streams[0, toks - (CONV - 1) :], [(c, c + 1) for c in range(count - 1)])
-    own = w_out[0]
+    toks, width = streams.shape[1], norm_gain.shape[1]
+    x, taps, beta_t, gate_t, edge = load(
+        streams[0], conv_weight[0], beta_logit[0].T, gate_log[0].T
+    )
+    rim = moved(edge, [(c, c + 1) for c in range(count - 1)])
+    later_acts = later_activations(x, taps)
+    rim, later_acts, own = lax.optimization_barrier((rim, later_acts, w_out[0]))
     rights = [moved(own, [(c, c + 1) for c in range(count - 1)])]
     lefts = [moved(own, [(c, c - 1) for c in range(1, count)])]
     if count != 4:
         for turn in range(2, count):
             rights.append(moved(rights[-1], [(c, c + 1) for c in range(turn - 1, count - 1)]))
             lefts.append(moved(lefts[-1], [(c, c - 1) for c in range(1, count - turn + 1)]))
-    total_map, total_add, sent, direct, reach = shard_terms(
-        streams[0], rim, conv_weight[0], beta_logit[0].T, gate_log[0].T
-    )
-    states = [moved(sent, [(0, 1)])]
-    for turn in range(1, count - 1):
-        states.append(moved(hand_on(total_map, total_add, states[-1]), [(turn, turn + 1)]))
+    total_map, total_add, sent, direct, reach, both = shard_terms(
+        later_acts, rim, x, taps, beta_t, gate_t
+    )
     if count != 4:
+        states = [moved(sent, [(0, 1)])]
+        for turn in range(1, count - 1):
+            states.append(moved(hand_on(total_map, total_add, states[-1]), [(turn, turn + 1)]))
         mixed = project(states, direct, reach, norm_gain, own, rights, lefts)
         return handed(mixed, [(c, c) for c in range(count)])[None]
-    early = normalize(direct, reach, norm_gain, states[:-1])
-    near = moved(early, [(1, 2), (2, 1)])
-    normed = normalize(direct, reach, norm_gain, states)
-    far = moved(normed, [(0, 2), (3, 1)])
-    own_two, own_one = columns(own_columns_kernel, [normed], own, rights[0], lefts[0])
-    far_two, near_one = columns(others_columns_kernel, [far, near], own, rights[0], lefts[0])
-    return assemble(
+
+    left, right = rights[0], lefts[0]
+    cols = own.shape[1]
+    rows = (toks, width)
+    one, two, three = ((toks, blocks * cols) for blocks in (1, 2, 3))
+    first = moved(sent, [(0, 1)])
+    both = moved(both, [(3, 2), (2, 1)])
+    rows0 = call(first_rows_kernel, [direct, norm_gain], [rows])
+    far0 = moved(rows0, [(0, 3)])
+    first, far0 = lax.optimization_barrier((first, far0))
+    out1 = hand_on(total_map, total_add, first)
+    second = moved(out1, [(1, 2)])
+    rows1 = call(second_rows_kernel, [direct, reach, norm_gain, first], [rows])
+    far1 = moved(rows1, [(1, 2)])
+    third_one = call(third_columns_kernel, [both, norm_gain, out1, left], [one], [rows])
+    first_two = call(first_columns_kernel, [far0, own, left], [two])
+    third_one, first_two, rows1 = lax.optimization_barrier((third_one, first_two, rows1))
+    third_one, first_two = handed(third_one, [(1, 2)]), handed(first_two, [(3, 0)])
+    rows3 = call(fourth_rows_kernel, [total_map, total_add, both, norm_gain, second], [rows])
+    far3 = moved(rows3, [(2, 1)])
+    own_three, next_three = call(
+        near_columns_kernel,
+        [direct, reach, norm_gain, second, rows0, rows1, rows3, own, left, right],
+        [three, three],
+        [rows],
+    )
+    far_one = call(far_columns_kernel, [far1, far3, left, right], [one])
+    return call(
+        assemble_kernel,
         [
-            handed(own_two, [(c, c) for c in range(4)]),
-            handed(own_one, [(1, 1), (2, 2)]),
-            handed(far_two, [(1, 3), (2, 0)]),
-            handed(near_one, [(1, 2), (2, 1)]),
-        ]
+            handed(own_three, [(0, 0), (1, 1), (2, 2)]),
+            handed(next_three, [(2, 3)]),
+            third_one,
+            first_two,
+            handed(far_one, [(2, 1), (1, 3)]),
+        ],
+        [(toks, 4 * cols)],
     )[None]
 
 

time: 85.5 us -> 73.9 us (0.86)
  the two profiles are of different devices: /device:TPU:8 before, /device:TPU:24 now
where the time goes in v4:
time: 73.9 us; the launch traced here: 73.3 us
  waiting for transfers between devices  33.9 us (46%)
  starting transfers between devices  20.1 us (27%)
  Pallas kernels  19 us (26%)
    ppermute x5, waiting for transfers between devices, handed(): lax.ppermute(value, ('section', 'ctx'), [(s * count + a, (s + 1) % sectio...  18.1 us
    ppermute x9, waiting for transfers between devices, moved(): return lax.ppermute(value, 'ctx', pairs)  15.8 us
    pallas_call x3, Pallas kernels, kernel_call(): pl.pallas_call(kernel, in_specs=[pl.BlockSpec(memory_space=space)] * len(...  15.8 us
    ppermute x9, starting transfers between devices, moved(): return lax.ppermute(value, 'ctx', pairs)  12.9 us
    ppermute x5, starting transfers between devices, handed(): lax.ppermute(value, ('section', 'ctx'), [(s * count + a, (s + 1) % sectio...  7.17 us
    pallas_call x8, Pallas kernels, call(): pl.pallas_call(kernel, in_specs=[vmem] * len(operands), out_specs=[vmem]...  1.56 us
  transfers between devices with their start and end apart: 14, of which 4 were waited for; matrix products, arithmetic and copies ran while one was open for 0% of the time, Pallas kernels for 23%

profile of v4, /device:TPU:24, one launch (start us, length us, event | category | flops | bytes accessed | tf_op | source)
XLA Modules:
  0.0 73.3 jit_solution(9759900853199764407)
XLA Ops:
  0.0 1.4 %shard_map.64 = (bf16[128,5120]{1,0:T(8,128)(2,1)S(1)}, bf16[4,5120]{1,0:T(4,128)(2,1)S(1)}, f32[16,128]{1,0:T(8,128)S(1)}, f32[8,128]{1,0:T(8,128)S(1)}, bf16[3,5120]{1,0:T(4,128)(2,1)S(1)}) custom-call(bf16[128,5120]{1,0:T(8,128)(2,1)} %bitcast.14, bf16[4,5120]{1,0:T(4,128)(2,1)} %bitcast.15, f32[16,128]{1,0:T(8,128)} %bitcast.16, f32[8,128]{1,0:T(8,128)} %bitcast.17), custom_call_target="tpu_custom_call" | custom-call | tf_op jit(solution)/shard_map/pallas_call | solution.py:227
  1.4 1.3 %collective-permute-start = (bf16[3,5120]{1,0:T(4,128)(2,1)S(1)}, bf16[3,5120]{1,0:T(4,128)(2,1)S(1)}, u32[]{:S(2)}, u32[]{:S(2)}) collective-permute-start(bf16[3,5120]{1,0:T(4,128)(2,1)S(1)} %get-tuple-element.30), channel_id=1, source_target_pairs={{0,1},{1,2},{2,3},{4,5},{5,6},{6,7},{8,9},{9,10},{10,11},{12,13},{... | collective-permute-start | bytes 92168 | tf_op jit(solution)/shard_map/ppermute | solution.py:487
  2.7 1.4 %shard_map.65.act_ref = f32[64,5120]{1,0:T(8,128)S(1)} custom-call(bf16[128,5120]{1,0:T(8,128)(2,1)S(1)} %get-tuple-element.31.x_ref, bf16[4,5120]{1,0:T(4,128)(2,1)S(1)} %get-tuple-element.32.taps_ref), custom_call_target="tpu_custom_call" | custom-call | flops 1048576 | bytes 134217728 | tf_op jit(solution)/shard_map/pallas_call | solution.py:213
  4.1 3.1 %collective-permute-done.rim_ref = bf16[3,5120]{1,0:T(4,128)(2,1)S(1)} collective-permute-done((bf16[3,5120]{1,0:T(4,128)(2,1)S(1)}, bf16[3,5120]{1,0:T(4,128)(2,1)S(1)}, u32[]{:S(2)}, u32[]{:S(2)}) %collective-permute-start) | collective-permute-done | bytes 30752 | tf_op jit(solution)/shard_map/ppermute | solution.py:487
  7.3 1.3 %collective-permute-start.5 = (bf16[1024,512]{1,0:T(8,128)(2,1)S(1)}, bf16[1024,512]{1,0:T(8,128)(2,1)S(1)}, u32[]{:S(2)}, u32[]{:S(2)}) collective-permute-start(bf16[1024,512]{1,0:T(8,128)(2,1)S(1)} %bitcast.10), channel_id=1, source_target_pairs={{0,1},{1,2},{2,3},{4,5},{5,6},{6,7},{8,9},{9,10},{10,11},{12,13},{... | collective-permute-start | bytes 3145736 | tf_op jit(solution)/shard_map/ppermute | solution.py:487
  8.6 4.6 %collective-permute-start.6 = (bf16[1024,512]{1,0:T(8,128)(2,1)S(1)}, bf16[1024,512]{1,0:T(8,128)(2,1)S(1)}, u32[]{:S(2)}, u32[]{:S(2)}) collective-permute-start(bf16[1024,512]{1,0:T(8,128)(2,1)S(1)} %bitcast.11), channel_id=1, source_target_pairs={{1,0},{2,1},{3,2},{5,4},{6,5},{7,6},{9,8},{10,9},{11,10},{13,12},{... | collective-permute-start | bytes 3145736 | tf_op jit(solution)/shard_map/ppermute | solution.py:487
  13.2 6.5 %shard_map.66 = (f32[8,128,128]{2,1,0:T(8,128)S(1)}, f32[8,128,128]{2,1,0:T(8,128)S(1)}, f32[64,1024]{1,0:T(8,128)S(1)}, f32[64,1024]{1,0:T(8,128)S(1)}) custom-call(f32[64,5120]{1,0:T(8,128)S(1)} %shard_map.65.act_ref, f32[16,128]{1,0:T(8,128)S(1)} %get-tuple-element.34.beta_ref, f32[8,128]{1,0:T(8,128)S(1)} %get-tuple-element.35.gate_ref), custom_call_target="tpu_custom_call" | custom-call | flops 1048576 | bytes 65536 | tf_op jit(solution)/shard_map/pallas_call | solution.py:213
  19.7 7.9 %shard_map.67 = (f32[8,128,128]{2,1,0:T(8,128)S(1)}, f32[8,128,128]{2,1,0:T(8,128)S(1)}, bf16[8,128,128]{2,1,0:T(8,128)(2,1)S(1)}, f32[128,1024]{1,0:T(8,128)S(1...) custom-call(bf16[3,5120]{1,0:T(4,128)(2,1)S(1)} %collective-permute-done.rim_ref, ...), custom_call_target="tpu_custom_call" | custom-call | flops 1048576 | bytes 65536 | tf_op jit(solution)/shard_map/pallas_call | solution.py:213
  27.6 0.7 collective-permute-start.1
  28.3 1.3 %collective-permute-start.2 = (bf16[128,1024]{1,0:T(8,128)(2,1)S(1)}, bf16[128,1024]{1,0:T(8,128)(2,1)S(1)}, u32[]{:S(2)}, u32[]{:S(2)}) collective-permute-start(bf16[128,1024]{1,0:T(8,128)(2,1)S(1)} %shard_map.68.rows0_ref), channel_id=1, source_target_pairs={{0,3},{4,7},{8,11},{12,15},{16,19},{20,23},{24,27},{28,31}} | collective-permute-start | bytes 786440 | tf_op jit(solution)/shard_map/ppermute | solution.py:487
  29.6 1.7 %collective-permute-start.4 = (bf16[2,128,1024]{2,1,0:T(8,128)(2,1)S(1)}, bf16[2,128,1024]{2,1,0:T(8,128)(2,1)S(1)}, u32[]{:S(2)}, u32[]{:S(2)}) collective-permute-start(bf16[2,128,1024]{2,1,0:T(8,128)(2,1)S(1)} %get-tuple-element.47), channel_id=1, source_target_pairs={{3,2},{2,1},{7,6},{6,5},{11,10},{10,9},{15,14},{14,13},{19,18},{18... | collective-permute-start | bytes 1572872 | tf_op jit(solution)/shard_map/ppermute | solution.py:487
  31.3 12.7 %collective-permute-done.2.rows_ref = bf16[128,1024]{1,0:T(8,128)(2,1)S(1)} collective-permute-done((bf16[128,1024]{1,0:T(8,128)(2,1)S(1)}, bf16[128,1024]{1,0:T(8,128)(2,1)S(1)}, u32[]{:S(2)}, u32[]{:S(2)}) %collective-permute-start.2) | collective-permute-done | bytes 262176 | tf_op jit(solution)/shard_map/ppermute | solution.py:487
  44.3 0.7 collective-permute-start.3
  45.0 0.7 collective-permute-start.11
  45.9 0.7 collective-permute-start.12
  46.7 0.4 shard_map.71
  47.2 0.7 collective-permute-start.7
  47.8 1.3 %collective-permute-start.8 = (bf16[128,1536]{1,0:T(8,128)(2,1)S(1)}, bf16[128,1536]{1,0:T(8,128)(2,1)S(1)}, u32[]{:S(2)}, u32[]{:S(2)}) collective-permute-start(bf16[128,1536]{1,0:T(8,128)(2,1)S(1)} %get-tuple-element.52), channel_id=1, source_target_pairs={{2,7},{6,11},{10,15},{14,19},{18,23},{22,27},{26,31},{30,3}} | collective-permute-start | bytes 1179656 | tf_op jit(solution)/shard_map/ppermute | solution.py:492
  49.1 3.2 %collective-permute-start.10 = (bf16[128,1024]{1,0:T(8,128)(2,1)S(1)}, bf16[128,1024]{1,0:T(8,128)(2,1)S(1)}, u32[]{:S(2)}, u32[]{:S(2)}) collective-permute-start(bf16[128,1024]{1,0:T(8,128)(2,1)S(1)} %shard_map.71), channel_id=1, source_target_pairs={{3,4},{7,8},{11,12},{15,16},{19,20},{23,24},{27,28},{31,0}} | collective-permute-start | bytes 786440 | tf_op jit(solution)/shard_map/ppermute | solution.py:492
  52.4 0.7 collective-permute-start.9
  53.1 1.3 %collective-permute-start.13 = (bf16[128,512]{1,0:T(8,128)(2,1)S(1)}, bf16[128,512]{1,0:T(8,128)(2,1)S(1)}, u32[]{:S(2)}, u32[]{:S(2)}) collective-permute-start(bf16[128,512]{1,0:T(8,128)(2,1)S(1)} %shard_map.75), channel_id=1, source_target_pairs={{2,5},{1,7},{6,9},{5,11},{10,13},{9,15},{14,17},{13,19},{18,21},{1... | collective-permute-start | bytes 393224 | tf_op jit(solution)/shard_map/ppermute | solution.py:492
  54.4 14.9 %collective-permute-done.13.far_one = bf16[128,512]{1,0:T(8,128)(2,1)S(1)} collective-permute-done((bf16[128,512]{1,0:T(8,128)(2,1)S(1)}, bf16[128,512]{1,0:T(8,128)(2,1)S(1)}, u32[]{:S(2)}, u32[]{:S(2)}) %collective-permute-start.13) | collective-permute-done | bytes 131104 | tf_op jit(solution)/shard_map/ppermute | solution.py:492
  69.4 3.2 %collective-permute-done.8.next_three = bf16[128,1536]{1,0:T(8,128)(2,1)S(1)} collective-permute-done((bf16[128,1536]{1,0:T(8,128)(2,1)S(1)}, bf16[128,1536]{1,0:T(8,128)(2,1)S(1)}, u32[]{:S(2)}, u32[]{:S(2)}) %collective-permute-start.8) | collective-permute-done | bytes 393248 | tf_op jit(solution)/shard_map/ppermute | solution.py:492
  72.5 0.8 %shard_map.76 = bf16[128,2048]{1,0:T(8,128)(2,1)} custom-call(bf16[128,1536]{1,0:T(8,128)(2,1)S(1)} %collective-permute-done.7.own_three, bf16[128,1536]{1,0:T(8,128)(2,1)S(1)} %collective-permute-done.8.next_three, bf16[128,512]{1,0:T(8,128)(2,1)S(1)} %collective-permute-done.9.third_one, bf16[128,1024]{1,0:T(8,128)(2,1)S(1)} %collective-permute-done.10.first_two, ...), custom_call_target="tpu_custom_call" | custom-call | flops 1048576 | bytes 65536 | tf_op jit(solution)/shard_map/pallas_call | solution.py:456
  (21 shorter events, 0.6 us)
Async XLA Ops:
  1.4 5.9 %collective-permute-start = (bf16[3,5120]{1,0:T(4,128)(2,1)S(1)}, bf16[3,5120]{1,0:T(4,128)(2,1)S(1)}, u32[]{:S(2)}, u32[]{:S(2)}) collective-permute-start(bf16[3,5120]{1,0:T(4,128)(2,1)S(1)} %get-tuple-element.30), channel_id=1, source_target_pairs={{0,1},{1,2},{2,3},{4,5},{5,6},{6,7},{8,9},{9,10},{10,11},{12,13},{... | collective-permute-start | bytes 92168 | tf_op jit(solution)/shard_map/ppermute | solution.py:487
  2.7 4.6 %copy-start = (bf16[1,1024,512]{2,1,0:T(8,128)(2,1)S(1)}, bf16[1,1024,512]{2,1,0:T(8,128)(2,1)}, u32[]{:S(2)}) copy-start(bf16[1,1024,512]{2,1,0:T(8,128)(2,1)} %param.11) | copy-start | bytes 3145732
  7.3 39.3 %collective-permute-start.5 = (bf16[1024,512]{1,0:T(8,128)(2,1)S(1)}, bf16[1024,512]{1,0:T(8,128)(2,1)S(1)}, u32[]{:S(2)}, u32[]{:S(2)}) collective-permute-start(bf16[1024,512]{1,0:T(8,128)(2,1)S(1)} %bitcast.10), channel_id=1, source_target_pairs={{0,1},{1,2},{2,3},{4,5},{5,6},{6,7},{8,9},{9,10},{10,11},{12,13},{... | collective-permute-start | bytes 3145736 | tf_op jit(solution)/shard_map/ppermute | solution.py:487
  8.6 38.5 %collective-permute-start.6 = (bf16[1024,512]{1,0:T(8,128)(2,1)S(1)}, bf16[1024,512]{1,0:T(8,128)(2,1)S(1)}, u32[]{:S(2)}, u32[]{:S(2)}) collective-permute-start(bf16[1024,512]{1,0:T(8,128)(2,1)S(1)} %bitcast.11), channel_id=1, source_target_pairs={{1,0},{2,1},{3,2},{5,4},{6,5},{7,6},{9,8},{10,9},{11,10},{13,12},{... | collective-permute-start | bytes 3145736 | tf_op jit(solution)/shard_map/ppermute | solution.py:487
  19.7 8.6 %copy-start.1 = (f32[1,1024]{1,0:T(1,128)S(1)}, f32[1,1024]{1,0:T(1,128)}, u32[]{:S(2)}) copy-start(f32[1,1024]{1,0:T(1,128)} %gain_ref.9) | copy-start | bytes 12292
  27.6 3.7 %collective-permute-start.1 = (bf16[8,128,128]{2,1,0:T(8,128)(2,1)S(1)}, bf16[8,128,128]{2,1,0:T(8,128)(2,1)S(1)}, u32[]{:S(2)}, u32[]{:S(2)}) collective-permute-start(bf16[8,128,128]{2,1,0:T(8,128)(2,1)S(1)} %get-tuple-element.45), channel_id=1, source_target_pairs={{0,1},{4,5},{8,9},{12,13},{16,17},{20,21},{24,25},{28,29}} | collective-permute-start | bytes 786440 | tf_op jit(solution)/shard_map/ppermute | solution.py:487
  28.3 15.7 %collective-permute-start.2 = (bf16[128,1024]{1,0:T(8,128)(2,1)S(1)}, bf16[128,1024]{1,0:T(8,128)(2,1)S(1)}, u32[]{:S(2)}, u32[]{:S(2)}) collective-permute-start(bf16[128,1024]{1,0:T(8,128)(2,1)S(1)} %shard_map.68.rows0_ref), channel_id=1, source_target_pairs={{0,3},{4,7},{8,11},{12,15},{16,19},{20,23},{24,27},{28,31}} | collective-permute-start | bytes 786440 | tf_op jit(solution)/shard_map/ppermute | solution.py:487
  29.6 16.1 %collective-permute-start.4 = (bf16[2,128,1024]{2,1,0:T(8,128)(2,1)S(1)}, bf16[2,128,1024]{2,1,0:T(8,128)(2,1)S(1)}, u32[]{:S(2)}, u32[]{:S(2)}) collective-permute-start(bf16[2,128,1024]{2,1,0:T(8,128)(2,1)S(1)} %get-tuple-element.47), channel_id=1, source_target_pairs={{3,2},{2,1},{7,6},{6,5},{11,10},{10,9},{15,14},{14,13},{19,18},{18... | collective-permute-start | bytes 1572872 | tf_op jit(solution)/shard_map/ppermute | solution.py:487
  44.3 1.4 %collective-permute-start.3 = (bf16[8,128,128]{2,1,0:T(8,128)(2,1)S(1)}, bf16[8,128,128]{2,1,0:T(8,128)(2,1)S(1)}, u32[]{:S(2)}, u32[]{:S(2)}) collective-permute-start(bf16[8,128,128]{2,1,0:T(8,128)(2,1)S(1)} %shard_map.69.state_ref), channel_id=1, source_target_pairs={{1,2},{5,6},{9,10},{13,14},{17,18},{21,22},{25,26},{29,30}} | collective-permute-start | bytes 786440 | tf_op jit(solution)/shard_map/ppermute | solution.py:487
  45.0 7.4 %collective-permute-start.11 = (bf16[128,1024]{1,0:T(8,128)(2,1)S(1)}, bf16[128,1024]{1,0:T(8,128)(2,1)S(1)}, u32[]{:S(2)}, u32[]{:S(2)}) collective-permute-start(bf16[128,1024]{1,0:T(8,128)(2,1)S(1)} %shard_map.72.rows1_ref), channel_id=1, source_target_pairs={{1,2},{5,6},{9,10},{13,14},{17,18},{21,22},{25,26},{29,30}} | collective-permute-start | bytes 786440 | tf_op jit(solution)/shard_map/ppermute | solution.py:487
  45.9 7.1 %collective-permute-start.12 = (bf16[128,1024]{1,0:T(8,128)(2,1)S(1)}, bf16[128,1024]{1,0:T(8,128)(2,1)S(1)}, u32[]{:S(2)}, u32[]{:S(2)}) collective-permute-start(bf16[128,1024]{1,0:T(8,128)(2,1)S(1)} %shard_map.73.rows3_ref), channel_id=1, source_target_pairs={{2,1},{6,5},{10,9},{14,13},{18,17},{22,21},{26,25},{30,29}} | collective-permute-start | bytes 786440 | tf_op jit(solution)/shard_map/ppermute | solution.py:487
  47.2 22.2 %collective-permute-start.7 = (bf16[128,1536]{1,0:T(8,128)(2,1)S(1)}, bf16[128,1536]{1,0:T(8,128)(2,1)S(1)}, u32[]{:S(2)}, u32[]{:S(2)}) collective-permute-start(bf16[128,1536]{1,0:T(8,128)(2,1)S(1)} %get-tuple-element.51), channel_id=1, source_target_pairs={{0,4},{1,5},{2,6},{4,8},{5,9},{6,10},{8,12},{9,13},{10,14},{12,16}... | collective-permute-start | bytes 1179656 | tf_op jit(solution)/shard_map/ppermute | solution.py:492
  47.8 24.7 %collective-permute-start.8 = (bf16[128,1536]{1,0:T(8,128)(2,1)S(1)}, bf16[128,1536]{1,0:T(8,128)(2,1)S(1)}, u32[]{:S(2)}, u32[]{:S(2)}) collective-permute-start(bf16[128,1536]{1,0:T(8,128)(2,1)S(1)} %get-tuple-element.52), channel_id=1, source_target_pairs={{2,7},{6,11},{10,15},{14,19},{18,23},{22,27},{26,31},{30,3}} | collective-permute-start | bytes 1179656 | tf_op jit(solution)/shard_map/ppermute | solution.py:492
  49.1 20.2 %collective-permute-start.10 = (bf16[128,1024]{1,0:T(8,128)(2,1)S(1)}, bf16[128,1024]{1,0:T(8,128)(2,1)S(1)}, u32[]{:S(2)}, u32[]{:S(2)}) collective-permute-start(bf16[128,1024]{1,0:T(8,128)(2,1)S(1)} %shard_map.71), channel_id=1, source_target_pairs={{3,4},{7,8},{11,12},{15,16},{19,20},{23,24},{27,28},{31,0}} | collective-permute-start | bytes 786440 | tf_op jit(solution)/shard_map/ppermute | solution.py:492
  52.4 2.0 %collective-permute-start.9 = (bf16[128,512]{1,0:T(8,128)(2,1)S(1)}, bf16[128,512]{1,0:T(8,128)(2,1)S(1)}, u32[]{:S(2)}, u32[]{:S(2)}) collective-permute-start(bf16[128,512]{1,0:T(8,128)(2,1)S(1)} %shard_map.70), channel_id=1, source_target_pairs={{1,6},{5,10},{9,14},{13,18},{17,22},{21,26},{25,30},{29,2}} | collective-permute-start | bytes 393224 | tf_op jit(solution)/shard_map/ppermute | solution.py:492
  53.1 16.2 %collective-permute-start.13 = (bf16[128,512]{1,0:T(8,128)(2,1)S(1)}, bf16[128,512]{1,0:T(8,128)(2,1)S(1)}, u32[]{:S(2)}, u32[]{:S(2)}) collective-permute-start(bf16[128,512]{1,0:T(8,128)(2,1)S(1)} %shard_map.75), channel_id=1, source_target_pairs={{2,5},{1,7},{6,9},{5,11},{10,13},{9,15},{14,17},{13,19},{18,21},{1... | collective-permute-start | bytes 393224 | tf_op jit(solution)/shard_map/ppermute | solution.py:492

commit v5 on v4

--- a/solution.py
+++ b/solution.py
@@ -394,12 +394,12 @@
         rows_with_state(direct_ref, reach_ref, gain_ref, state_ref, out_ref)
 
 
-def third_columns_kernel(both_ref, gain_ref, state_ref, left_ref, out_ref, rows_ref):
+def third_columns_kernel(both_ref, gain_ref, state_ref, pair_ref, out_ref, rows_ref):
     @on_shard(1)
     def _():
         for head, lanes in head_lanes(state_ref.shape[0]):
             rows_ref[:, lanes] = rows_of_next(both_ref, gain_ref, head, lanes, state_ref[head])
-        project_to(out_ref, rows_ref[...], left_ref)
+        project_to(out_ref, rows_ref[...], pair_ref.at[0])
 
 
 def fourth_rows_kernel(map_ref, add_ref, both_ref, gain_ref, state_ref, out_ref):
@@ -414,40 +414,41 @@
 
 
 def near_columns_kernel(
-    direct_ref, reach_ref, gain_ref, state_ref, rows0_ref, rows1_ref, rows3_ref, own_ref, left_ref, right_ref,
+    direct_ref, reach_ref, gain_ref, state_ref, rows0_ref, rows1_ref, rows3_ref, pair_ref, middle_ref,
     own_three, next_three, rows_ref,
 ):
-    weights = (own_ref, right_ref, left_ref)
+    low, high = pair_ref.at[0], pair_ref.at[1]
 
     @on_shard(0)
     def _():
-        project_to(own_three, rows0_ref[...], *weights[:2])
+        project_to(own_three, rows0_ref[...], low, high)
 
     @on_shard(1)
     def _():
-        project_to(own_three, rows1_ref[...], *weights)
+        project_to(own_three, rows1_ref[...], high, middle_ref, low)
 
     @on_shard(2)
     def _():
+        weights = (low, high, middle_ref)
         project_to(next_three, rows3_ref[...], *weights)
         rows_with_state(direct_ref, reach_ref, gain_ref, state_ref, rows_ref)
         project_to(own_three, rows_ref[...], *weights)
 
 
-def first_columns_kernel(rows_ref, own_ref, left_ref, out_ref):
+def first_columns_kernel(rows_ref, pair_ref, out_ref):
     @on_shard(3)
     def _():
-        project_to(out_ref, rows_ref[...], left_ref, own_ref)
-
-
-def far_columns_kernel(rows1_ref, rows3_ref, left_ref, right_ref, out_ref):
+        project_to(out_ref, rows_ref[...], pair_ref.at[0], pair_ref.at[1])
+
+
+def far_columns_kernel(rows1_ref, rows3_ref, pair_ref, out_ref):
     @on_shard(1)
     def _():
-        project_to(out_ref, rows3_ref[...], left_ref)
+        project_to(out_ref, rows3_ref[...], pair_ref.at[0])
 
     @on_shard(2)
     def _():
-        project_to(out_ref, rows1_ref[...], right_ref)
+        project_to(out_ref, rows1_ref[...], pair_ref.at[1])
 
 
 def call(kernel, operands, out_shapes, scratch=()):
@@ -508,11 +509,14 @@
     )
     rim = moved(edge, [(c, c + 1) for c in range(count - 1)])
     later_acts = later_activations(x, taps)
-    rim, later_acts, own = lax.optimization_barrier((rim, later_acts, w_out[0]))
-    rights = [moved(own, [(c, c + 1) for c in range(count - 1)])]
-    lefts = [moved(own, [(c, c - 1) for c in range(1, count)])]
-    if count != 4:
-        for turn in range(2, count):
+    own = w_out[0]
+    if count == 4:
+        pair = lax.all_gather(own, "ctx", axis_index_groups=[[0, 1], [2, 3]])
+        rim, later_acts, own = lax.optimization_barrier((rim, later_acts, own))
+        middle = moved(own, [(1, 2), (2, 1)])
+    else:
+        rights, lefts = [own], [own]
+        for turn in range(1, count):
             rights.append(moved(rights[-1], [(c, c + 1) for c in range(turn - 1, count - 1)]))
             lefts.append(moved(lefts[-1], [(c, c - 1) for c in range(1, count - turn + 1)]))
     total_map, total_add, sent, direct, reach, both = shard_terms(
@@ -522,10 +526,9 @@
         states = [moved(sent, [(0, 1)])]
         for turn in range(1, count - 1):
             states.append(moved(hand_on(total_map, total_add, states[-1]), [(turn, turn + 1)]))
-        mixed = project(states, direct, reach, norm_gain, own, rights, lefts)
+        mixed = project(states, direct, reach, norm_gain, own, rights[1:], lefts[1:])
         return handed(mixed, [(c, c) for c in range(count)])[None]
 
-    left, right = rights[0], lefts[0]
     cols = own.shape[1]
     rows = (toks, width)
     one, two, three = ((toks, blocks * cols) for blocks in (1, 2, 3))
@@ -533,31 +536,29 @@
     both = moved(both, [(3, 2), (2, 1)])
     rows0 = call(first_rows_kernel, [direct, norm_gain], [rows])
     far0 = moved(rows0, [(0, 3)])
-    first, far0 = lax.optimization_barrier((first, far0))
     out1 = hand_on(total_map, total_add, first)
     second = moved(out1, [(1, 2)])
     rows1 = call(second_rows_kernel, [direct, reach, norm_gain, first], [rows])
     far1 = moved(rows1, [(1, 2)])
-    third_one = call(third_columns_kernel, [both, norm_gain, out1, left], [one], [rows])
-    first_two = call(first_columns_kernel, [far0, own, left], [two])
-    third_one, first_two, rows1 = lax.optimization_barrier((third_one, first_two, rows1))
-    third_one, first_two = handed(third_one, [(1, 2)]), handed(first_two, [(3, 0)])
+    third_one = call(third_columns_kernel, [both, norm_gain, out1, pair], [one], [rows])
+    first_two = call(first_columns_kernel, [far0, pair], [two])
     rows3 = call(fourth_rows_kernel, [total_map, total_add, both, norm_gain, second], [rows])
     far3 = moved(rows3, [(2, 1)])
     own_three, next_three = call(
         near_columns_kernel,
-        [direct, reach, norm_gain, second, rows0, rows1, rows3, own, left, right],
+        [direct, reach, norm_gain, second, rows0, rows1, rows3, pair, middle],
         [three, three],
         [rows],
     )
-    far_one = call(far_columns_kernel, [far1, far3, left, right], [one])
+    far_one = call(far_columns_kernel, [far1, far3, pair], [one])
+    far_one, third_one, first_two = lax.optimization_barrier((far_one, third_one, first_two))
     return call(
         assemble_kernel,
         [
             handed(own_three, [(0, 0), (1, 1), (2, 2)]),
             handed(next_three, [(2, 3)]),
-            third_one,
-            first_two,
+            handed(third_one, [(1, 2)]),
+            handed(first_two, [(3, 0)]),
             handed(far_one, [(2, 1), (1, 3)]),
         ],
         [(toks, 4 * cols)],

time: 73.9 us -> 98 us (1.33)
  between operations: 0.29 us -> 13.6 us
  waiting for transfers between devices: 33.9 us -> 39.3 us
  Pallas kernels: 19 us -> 22.6 us
  local copies, waits for them, and re-layouts: 0.01 us -> 2.62 us
  starting transfers between devices: 20.1 us -> 18.6 us
    pallas_call x8, Pallas kernels: 1.56 us -> 5.14 us  [call(): pl.pallas_call(kernel, in_specs=[vmem] * len(operands), out_specs=[vmem]...]
    ppermute x5, waiting for transfers between devices: 18.1 us -> 21.4 us  [handed(): lax.ppermute(value, ('section', 'ctx'), [(s * count + a, (s + 1) % sectio...]
    unnamed x4 -> x12, local copies, waits for them, and re-layouts: 0.01 us -> 2.62 us
    ppermute x9 -> x8, starting transfers between devices: 12.9 us -> 11.4 us  [moved(): return lax.ppermute(value, 'ctx', pairs)]
    ppermute x9 -> x8, waiting for transfers between devices: 15.8 us -> 17.2 us  [moved(): return lax.ppermute(value, 'ctx', pairs)]
  transfers between devices with their start and end apart: 14 -> 14, of which waited for: 4 -> 3; matrix products, arithmetic and copies ran while one was open for 0% -> 0% of each run, Pallas kernels for 23% -> 22%
where the time goes in v5:
time: 98 us; the launch traced here: 96.8 us
  waiting for transfers between devices  39.3 us (40%)
  Pallas kernels  22.6 us (23%)
  starting transfers between devices  18.6 us (19%)
  between operations  13.6 us (14%)
  local copies, waits for them, and re-layouts  2.62 us (3%)
    ppermute x5, waiting for transfers between devices, handed(): lax.ppermute(value, ('section', 'ctx'), [(s * count + a, (s + 1) % sectio...  21.4 us
    ppermute x8, waiting for transfers between devices, moved(): return lax.ppermute(value, 'ctx', pairs)  17.2 us
    pallas_call x3, Pallas kernels, kernel_call(): pl.pallas_call(kernel, in_specs=[pl.BlockSpec(memory_space=space)] * len(...  15.8 us
    ppermute x8, starting transfers between devices, moved(): return lax.ppermute(value, 'ctx', pairs)  11.4 us
    ppermute x5, starting transfers between devices, handed(): lax.ppermute(value, ('section', 'ctx'), [(s * count + a, (s + 1) % sectio...  7.19 us
    pallas_call x8, Pallas kernels, call(): pl.pallas_call(kernel, in_specs=[vmem] * len(operands), out_specs=[vmem]...  5.14 us
    unnamed x12, local copies, waits for them, and re-layouts  2.62 us
  transfers between devices with their start and end apart: 14, of which 3 were waited for; matrix products, arithmetic and copies ran while one was open for 0% of the time, Pallas kernels for 22%

profile of v5, /device:TPU:24, one launch (start us, length us, event | category | flops | bytes accessed | tf_op | source)
XLA Modules:
  0.0 96.8 jit_solution(7423343436774457790)
XLA Ops:
  6.5 0.7 all-gather.2.cloned.1.call-update
  7.3 1.4 %shard_map.64 = (bf16[128,5120]{1,0:T(8,128)(2,1)S(1)}, bf16[4,5120]{1,0:T(4,128)(2,1)S(1)}, f32[16,128]{1,0:T(8,128)S(1)}, f32[8,128]{1,0:T(8,128)S(1)}, bf16[3,5120]{1,0:T(4,128)(2,1)S(1)}) custom-call(bf16[128,5120]{1,0:T(8,128)(2,1)} %bitcast.10, bf16[4,5120]{1,0:T(4,128)(2,1)} %bitcast.12, f32[16,128]{1,0:T(8,128)} %bitcast.13, f32[8,128]{1,0:T(8,128)} %bitcast.14), custom_call_target="tpu_custom_call" | custom-call | tf_op jit(solution)/shard_map/pallas_call | solution.py:227
  8.6 1.3 %collective-permute-start = (bf16[3,5120]{1,0:T(4,128)(2,1)S(1)}, bf16[3,5120]{1,0:T(4,128)(2,1)S(1)}, u32[]{:S(2)}, u32[]{:S(2)}) collective-permute-start(bf16[3,5120]{1,0:T(4,128)(2,1)S(1)} %get-tuple-element.28), channel_id=1, source_target_pairs={{0,1},{1,2},{2,3},{4,5},{5,6},{6,7},{8,9},{9,10},{10,11},{12,13},{... | collective-permute-start | bytes 92168 | tf_op jit(solution)/shard_map/ppermute | solution.py:488
  10.0 1.4 %shard_map.65.act_ref = f32[64,5120]{1,0:T(8,128)S(1)} custom-call(bf16[128,5120]{1,0:T(8,128)(2,1)S(1)} %get-tuple-element.29.x_ref, bf16[4,5120]{1,0:T(4,128)(2,1)S(1)} %get-tuple-element.30.taps_ref), custom_call_target="tpu_custom_call" | custom-call | flops 1048576 | bytes 134217728 | tf_op jit(solution)/shard_map/pallas_call | solution.py:213
  11.4 3.1 %collective-permute-done.rim_ref = bf16[3,5120]{1,0:T(4,128)(2,1)S(1)} collective-permute-done((bf16[3,5120]{1,0:T(4,128)(2,1)S(1)}, bf16[3,5120]{1,0:T(4,128)(2,1)S(1)}, u32[]{:S(2)}, u32[]{:S(2)}) %collective-permute-start) | collective-permute-done | bytes 30752 | tf_op jit(solution)/shard_map/ppermute | solution.py:488
  14.5 0.7 collective-permute-start.4
  15.3 6.5 %shard_map.66 = (f32[8,128,128]{2,1,0:T(8,128)S(1)}, f32[8,128,128]{2,1,0:T(8,128)S(1)}, f32[64,1024]{1,0:T(8,128)S(1)}, f32[64,1024]{1,0:T(8,128)S(1)}) custom-call(f32[64,5120]{1,0:T(8,128)S(1)} %shard_map.65.act_ref, f32[16,128]{1,0:T(8,128)S(1)} %get-tuple-element.32.beta_ref, f32[8,128]{1,0:T(8,128)S(1)} %get-tuple-element.33.gate_ref), custom_call_target="tpu_custom_call" | custom-call | flops 1048576 | bytes 65536 | tf_op jit(solution)/shard_map/pallas_call | solution.py:213
  21.8 7.9 %shard_map.67 = (f32[8,128,128]{2,1,0:T(8,128)S(1)}, f32[8,128,128]{2,1,0:T(8,128)S(1)}, bf16[8,128,128]{2,1,0:T(8,128)(2,1)S(1)}, f32[128,1024]{1,0:T(8,128)S(1...) custom-call(bf16[3,5120]{1,0:T(4,128)(2,1)S(1)} %collective-permute-done.rim_ref, ...), custom_call_target="tpu_custom_call" | custom-call | flops 1048576 | bytes 65536 | tf_op jit(solution)/shard_map/pallas_call | solution.py:213
  30.3 4.0 %collective-permute-start.3 = (bf16[2,128,1024]{2,1,0:T(8,128)(2,1)S(1)}, bf16[2,128,1024]{2,1,0:T(8,128)(2,1)S(1)}, u32[]{:S(2)}, u32[]{:S(2)}) collective-permute-start(bf16[2,128,1024]{2,1,0:T(8,128)(2,1)S(1)} %get-tuple-element.44), channel_id=1, source_target_pairs={{3,2},{2,1},{7,6},{6,5},{11,10},{10,9},{15,14},{14,13},{19,18},{18... | collective-permute-start | bytes 1572872 | tf_op jit(solution)/shard_map/ppermute | solution.py:488
  35.4 1.3 %collective-permute-start.9 = (bf16[128,1024]{1,0:T(8,128)(2,1)S(1)}, bf16[128,1024]{1,0:T(8,128)(2,1)}, u32[]{:S(2)}, u32[]{:S(2)}) collective-permute-start(bf16[128,1024]{1,0:T(8,128)(2,1)S(1)} %shard_map.69.rows0_ref), channel_id=1, source_target_pairs={{0,3},{4,7},{8,11},{12,15},{16,19},{20,23},{24,27},{28,31}} | collective-permute-start | bytes 786440 | tf_op jit(solution)/shard_map/ppermute | solution.py:488
  36.7 1.4 %collective-permute-start.7 = (bf16[128,1024]{1,0:T(8,128)(2,1)S(1)}, bf16[128,1024]{1,0:T(8,128)(2,1)}, u32[]{:S(2)}, u32[]{:S(2)}) collective-permute-start(bf16[128,1024]{1,0:T(8,128)(2,1)S(1)} %shard_map.70.rows1_ref), channel_id=1, source_target_pairs={{1,2},{5,6},{9,10},{13,14},{17,18},{21,22},{25,26},{29,30}} | collective-permute-start | bytes 786440 | tf_op jit(solution)/shard_map/ppermute | solution.py:488
  38.1 14.0 %collective-permute-done.3.both_ref = bf16[2,128,1024]{2,1,0:T(8,128)(2,1)S(1)} collective-permute-done((bf16[2,128,1024]{2,1,0:T(8,128)(2,1)S(1)}, bf16[2,128,1024]{2,1,0:T(8,128)(2,1)S(1)}, u32[]{:S(2)}, u32[]{:S(2)}) %collective-permute-start.3) | collective-permute-done | bytes 524320 | tf_op jit(solution)/shard_map/ppermute | solution.py:488
  52.1 0.7 shard_map.71.rows3_ref
  52.9 1.4 %collective-permute-start.8 = (bf16[128,1024]{1,0:T(8,128)(2,1)}, bf16[128,1024]{1,0:T(8,128)(2,1)}, u32[]{:S(2)}, u32[]{:S(2)}) collective-permute-start(bf16[128,1024]{1,0:T(8,128)(2,1)} %shard_map.71.rows3_ref), channel_id=1, source_target_pairs={{2,1},{6,5},{10,9},{14,13},{18,17},{22,21},{26,25},{30,29}} | collective-permute-start | bytes 786440 | tf_op jit(solution)/shard_map/ppermute | solution.py:488
  54.3 1.6 %copy-done = bf16[2,1024,512]{2,1,0:T(8,128)(2,1)S(1)} copy-done((bf16[2,1024,512]{2,1,0:T(8,128)(2,1)S(1)}, bf16[2,1024,512]{2,1,0:T(8,128)(2,1)}, u32[]{:S(2)}) %copy-start) | copy-done | bytes 2097176
  55.9 0.9 copy-done.3
  56.8 1.1 %shard_map.72 = (bf16[128,1536]{1,0:T(8,128)(2,1)S(1)}, bf16[128,1536]{1,0:T(8,128)(2,1)S(1)}) custom-call(f32[128,1024]{1,0:T(8,128)S(1)} %get-tuple-element.39.direct_ref, f32[128,1024]{1,0:T(8,128)S(1)} %get-tuple-element.40.reach_ref, f32[1,1024]{1,0:T(1,128)S(1)} %copy-done.4, bf16[8,128,128]{2,1,0:T(8,128)(2,1)S(1)} %copy-done.3, ...), custom_call_target="tpu_custom_call" | custom-call | flops 1048576 | bytes 65536 | tf_op jit(solution)/shard_map/pallas_call | solution.py:457
  58.6 1.3 %collective-permute-start.6 = (bf16[128,1536]{1,0:T(8,128)(2,1)S(1)}, bf16[128,1536]{1,0:T(8,128)(2,1)S(1)}, u32[]{:S(2)}, u32[]{:S(2)}) collective-permute-start(bf16[128,1536]{1,0:T(8,128)(2,1)S(1)} %get-tuple-element.47), channel_id=1, source_target_pairs={{2,7},{6,11},{10,15},{14,19},{18,23},{22,27},{26,31},{30,3}} | collective-permute-start | bytes 1179656 | tf_op jit(solution)/shard_map/ppermute | solution.py:493
  60.0 1.4 %shard_map.75 = bf16[128,1024]{1,0:T(8,128)(2,1)S(1)} custom-call(bf16[128,1024]{1,0:T(8,128)(2,1)} %collective-permute-done.9.rows_ref, bf16[2,1024,512]{2,1,0:T(8,128)(2,1)S(1)} %copy-done.1), custom_call_target="tpu_custom_call" | custom-call | flops 1048576 | bytes 65536 | tf_op jit(solution)/shard_map/pallas_call | solution.py:457
  61.4 1.0 %shard_map.73 = bf16[128,512]{1,0:T(8,128)(2,1)S(1)} custom-call(bf16[128,1024]{1,0:T(8,128)(2,1)} %collective-permute-done.7.rows1_ref, bf16[128,1024]{1,0:T(8,128)(2,1)} %collective-permute-done.8.rows3_ref, bf16[2,1024,512]{2,1,0:T(8,128)(2,1)S(1)} %copy-done.1), custom_call_target="tpu_custom_call" | custom-call | flops 1048576 | bytes 65536 | tf_op jit(solution)/shard_map/pallas_call | solution.py:457
  62.4 3.3 %collective-permute-start.11 = (bf16[128,1024]{1,0:T(8,128)(2,1)S(1)}, bf16[128,1024]{1,0:T(8,128)(2,1)S(1)}, u32[]{:S(2)}, u32[]{:S(2)}) collective-permute-start(bf16[128,1024]{1,0:T(8,128)(2,1)S(1)} %shard_map.75), channel_id=1, source_target_pairs={{3,4},{7,8},{11,12},{15,16},{19,20},{23,24},{27,28},{31,0}} | collective-permute-start | bytes 786440 | tf_op jit(solution)/shard_map/ppermute | solution.py:493
  66.4 1.3 %collective-permute-start.12 = (bf16[128,512]{1,0:T(8,128)(2,1)S(1)}, bf16[128,512]{1,0:T(8,128)(2,1)S(1)}, u32[]{:S(2)}, u32[]{:S(2)}) collective-permute-start(bf16[128,512]{1,0:T(8,128)(2,1)S(1)} %shard_map.73), channel_id=1, source_target_pairs={{2,5},{1,7},{6,9},{5,11},{10,13},{9,15},{14,17},{13,19},{18,21},{1... | collective-permute-start | bytes 393224 | tf_op jit(solution)/shard_map/ppermute | solution.py:493
  67.7 21.4 %collective-permute-done.12.far_one = bf16[128,512]{1,0:T(8,128)(2,1)S(1)} collective-permute-done((bf16[128,512]{1,0:T(8,128)(2,1)S(1)}, bf16[128,512]{1,0:T(8,128)(2,1)S(1)}, u32[]{:S(2)}, u32[]{:S(2)}) %collective-permute-start.12) | collective-permute-done | bytes 131104 | tf_op jit(solution)/shard_map/ppermute | solution.py:493
  89.1 0.9 shard_map.76
  (30 shorter events, 3.1 us)
Async XLA Ops:
  6.5 47.8 %all-gather.2.cloned.1.call-start = ((), (), s32[]{:S(2)}) async-start(), calls=%async_computation | async-start | bytes 3145728 | tf_op jit(solution)/shard_map/all_gather | solution.py:514
  8.6 5.9 %collective-permute-start = (bf16[3,5120]{1,0:T(4,128)(2,1)S(1)}, bf16[3,5120]{1,0:T(4,128)(2,1)S(1)}, u32[]{:S(2)}, u32[]{:S(2)}) collective-permute-start(bf16[3,5120]{1,0:T(4,128)(2,1)S(1)} %get-tuple-element.28), channel_id=1, source_target_pairs={{0,1},{1,2},{2,3},{4,5},{5,6},{6,7},{8,9},{9,10},{10,11},{12,13},{... | collective-permute-start | bytes 92168 | tf_op jit(solution)/shard_map/ppermute | solution.py:488
  9.9 4.6 %copy-start.5 = (bf16[1,1024,512]{2,1,0:T(8,128)(2,1)S(1)}, bf16[1,1024,512]{2,1,0:T(8,128)(2,1)}, u32[]{:S(2)}) copy-start(bf16[1,1024,512]{2,1,0:T(8,128)(2,1)} %param.11) | copy-start | bytes 3145732
  14.5 39.8 %collective-permute-start.4 = (bf16[1024,512]{1,0:T(8,128)(2,1)S(1)}, bf16[1024,512]{1,0:T(8,128)(2,1)S(1)}, u32[]{:S(2)}, u32[]{:S(2)}) collective-permute-start(bf16[1024,512]{1,0:T(8,128)(2,1)S(1)} %bitcast.11), channel_id=1, source_target_pairs={{1,2},{2,1},{5,6},{6,5},{9,10},{10,9},{13,14},{14,13},{17,18},{18,... | collective-permute-start | bytes 3145736 | tf_op jit(solution)/shard_map/ppermute | solution.py:488
  29.6 5.7 %copy-start.4 = (f32[1,1024]{1,0:T(1,128)S(1)}, f32[1,1024]{1,0:T(1,128)}, u32[]{:S(2)}) copy-start(f32[1,1024]{1,0:T(1,128)} %gain_ref.9) | copy-start | bytes 12292
  29.7 4.7 %collective-permute-start.1 = (bf16[8,128,128]{2,1,0:T(8,128)(2,1)S(1)}, bf16[8,128,128]{2,1,0:T(8,128)(2,1)S(1)}, u32[]{:S(2)}, u32[]{:S(2)}) collective-permute-start(bf16[8,128,128]{2,1,0:T(8,128)(2,1)S(1)} %get-tuple-element.43), channel_id=1, source_target_pairs={{0,1},{4,5},{8,9},{12,13},{16,17},{20,21},{24,25},{28,29}} | collective-permute-start | bytes 786440 | tf_op jit(solution)/shard_map/ppermute | solution.py:488
  30.3 21.8 %collective-permute-start.3 = (bf16[2,128,1024]{2,1,0:T(8,128)(2,1)S(1)}, bf16[2,128,1024]{2,1,0:T(8,128)(2,1)S(1)}, u32[]{:S(2)}, u32[]{:S(2)}) collective-permute-start(bf16[2,128,1024]{2,1,0:T(8,128)(2,1)S(1)} %get-tuple-element.44), channel_id=1, source_target_pairs={{3,2},{2,1},{7,6},{6,5},{11,10},{10,9},{15,14},{14,13},{19,18},{18... | collective-permute-start | bytes 1572872 | tf_op jit(solution)/shard_map/ppermute | solution.py:488
  34.7 17.4 %collective-permute-start.2 = (bf16[8,128,128]{2,1,0:T(8,128)(2,1)S(1)}, bf16[8,128,128]{2,1,0:T(8,128)(2,1)S(1)}, u32[]{:S(2)}, u32[]{:S(2)}) collective-permute-start(bf16[8,128,128]{2,1,0:T(8,128)(2,1)S(1)} %shard_map.68.state_ref), channel_id=1, source_target_pairs={{1,2},{5,6},{9,10},{13,14},{17,18},{21,22},{25,26},{29,30}} | collective-permute-start | bytes 786440 | tf_op jit(solution)/shard_map/ppermute | solution.py:488
  35.4 24.6 %collective-permute-start.9 = (bf16[128,1024]{1,0:T(8,128)(2,1)S(1)}, bf16[128,1024]{1,0:T(8,128)(2,1)}, u32[]{:S(2)}, u32[]{:S(2)}) collective-permute-start(bf16[128,1024]{1,0:T(8,128)(2,1)S(1)} %shard_map.69.rows0_ref), channel_id=1, source_target_pairs={{0,3},{4,7},{8,11},{12,15},{16,19},{20,23},{24,27},{28,31}} | collective-permute-start | bytes 786440 | tf_op jit(solution)/shard_map/ppermute | solution.py:488
  36.7 24.6 %collective-permute-start.7 = (bf16[128,1024]{1,0:T(8,128)(2,1)S(1)}, bf16[128,1024]{1,0:T(8,128)(2,1)}, u32[]{:S(2)}, u32[]{:S(2)}) collective-permute-start(bf16[128,1024]{1,0:T(8,128)(2,1)S(1)} %shard_map.70.rows1_ref), channel_id=1, source_target_pairs={{1,2},{5,6},{9,10},{13,14},{17,18},{21,22},{25,26},{29,30}} | collective-permute-start | bytes 786440 | tf_op jit(solution)/shard_map/ppermute | solution.py:488
  52.1 0.8 copy-start.2
  52.9 8.5 %collective-permute-start.8 = (bf16[128,1024]{1,0:T(8,128)(2,1)}, bf16[128,1024]{1,0:T(8,128)(2,1)}, u32[]{:S(2)}, u32[]{:S(2)}) collective-permute-start(bf16[128,1024]{1,0:T(8,128)(2,1)} %shard_map.71.rows3_ref), channel_id=1, source_target_pairs={{2,1},{6,5},{10,9},{14,13},{18,17},{22,21},{26,25},{30,29}} | collective-permute-start | bytes 786440 | tf_op jit(solution)/shard_map/ppermute | solution.py:488
  54.3 1.6 %copy-start = (bf16[2,1024,512]{2,1,0:T(8,128)(2,1)S(1)}, bf16[2,1024,512]{2,1,0:T(8,128)(2,1)}, u32[]{:S(2)}) copy-start(bf16[2,1024,512]{2,1,0:T(8,128)(2,1)} %all-gather.2.cloned.1.call-done.pair_ref) | copy-start | bytes 6291460
  55.9 0.9 copy-start.3
  56.8 3.1 %copy-start.1 = (bf16[2,1024,512]{2,1,0:T(8,128)(2,1)S(1)}, bf16[2,1024,512]{2,1,0:T(8,128)(2,1)}, u32[]{:S(2)}) copy-start(bf16[2,1024,512]{2,1,0:T(8,128)(2,1)} %all-gather.2.cloned.1.call-done.pair_ref) | copy-start | bytes 6291460
  57.9 31.2 %collective-permute-start.5 = (bf16[128,1536]{1,0:T(8,128)(2,1)S(1)}, bf16[128,1536]{1,0:T(8,128)(2,1)S(1)}, u32[]{:S(2)}, u32[]{:S(2)}) collective-permute-start(bf16[128,1536]{1,0:T(8,128)(2,1)S(1)} %get-tuple-element.46), channel_id=1, source_target_pairs={{0,4},{1,5},{2,6},{4,8},{5,9},{6,10},{8,12},{9,13},{10,14},{12,16}... | collective-permute-start | bytes 1179656 | tf_op jit(solution)/shard_map/ppermute | solution.py:493
  58.6 30.5 %collective-permute-start.6 = (bf16[128,1536]{1,0:T(8,128)(2,1)S(1)}, bf16[128,1536]{1,0:T(8,128)(2,1)S(1)}, u32[]{:S(2)}, u32[]{:S(2)}) collective-permute-start(bf16[128,1536]{1,0:T(8,128)(2,1)S(1)} %get-tuple-element.47), channel_id=1, source_target_pairs={{2,7},{6,11},{10,15},{14,19},{18,23},{22,27},{26,31},{30,3}} | collective-permute-start | bytes 1179656 | tf_op jit(solution)/shard_map/ppermute | solution.py:493
  62.4 26.7 %collective-permute-start.11 = (bf16[128,1024]{1,0:T(8,128)(2,1)S(1)}, bf16[128,1024]{1,0:T(8,128)(2,1)S(1)}, u32[]{:S(2)}, u32[]{:S(2)}) collective-permute-start(bf16[128,1024]{1,0:T(8,128)(2,1)S(1)} %shard_map.75), channel_id=1, source_target_pairs={{3,4},{7,8},{11,12},{15,16},{19,20},{23,24},{27,28},{31,0}} | collective-permute-start | bytes 786440 | tf_op jit(solution)/shard_map/ppermute | solution.py:493
  65.7 2.0 %collective-permute-start.10 = (bf16[128,512]{1,0:T(8,128)(2,1)S(1)}, bf16[128,512]{1,0:T(8,128)(2,1)S(1)}, u32[]{:S(2)}, u32[]{:S(2)}) collective-permute-start(bf16[128,512]{1,0:T(8,128)(2,1)S(1)} %shard_map.74), channel_id=1, source_target_pairs={{1,6},{5,10},{9,14},{13,18},{17,22},{21,26},{25,30},{29,2}} | collective-permute-start | bytes 393224 | tf_op jit(solution)/shard_map/ppermute | solution.py:493
  66.4 22.7 %collective-permute-start.12 = (bf16[128,512]{1,0:T(8,128)(2,1)S(1)}, bf16[128,512]{1,0:T(8,128)(2,1)S(1)}, u32[]{:S(2)}, u32[]{:S(2)}) collective-permute-start(bf16[128,512]{1,0:T(8,128)(2,1)S(1)} %shard_map.73), channel_id=1, source_target_pairs={{2,5},{1,7},{6,9},{5,11},{10,13},{9,15},{14,17},{13,19},{18,21},{1... | collective-permute-start | bytes 393224 | tf_op jit(solution)/shard_map/ppermute | solution.py:493
Sparse Core Ops, SparseCore 0:
  8.9 39.4 all-gather.1

commit v6 on v4

--- a/solution.py
+++ b/solution.py
@@ -242,7 +242,6 @@
         (x, taps),
         [((half, channels), f32)],
         scratch=[pltpu.VMEM((8 + half, channels), f32)],
-        cost=2**27,
     )[0]
 
 
@@ -362,9 +361,12 @@
 
 
 def project_to(out_ref, rows, *weights):
-    cols = weights[0].shape[1]
+    cols = out_ref.shape[1] // len(weights)
     for index, weight in enumerate(weights):
-        out_ref[:, index * cols : (index + 1) * cols] = dot(rows, weight[...]).astype(bf16)
+        parts = weight if isinstance(weight, tuple) else (weight,)
+        depth = rows.shape[1] // len(parts)
+        found = sum(dot(rows[:, i * depth : (i + 1) * depth], part[...]) for i, part in enumerate(parts))
+        out_ref[:, index * cols : (index + 1) * cols] = found.astype(bf16)
 
 
 def rows_with_state(direct_ref, reach_ref, gain_ref, state_ref, out_ref):
@@ -394,12 +396,12 @@
         rows_with_state(direct_ref, reach_ref, gain_ref, state_ref, out_ref)
 
 
-def third_columns_kernel(both_ref, gain_ref, state_ref, left_ref, out_ref, rows_ref):
+def third_columns_kernel(both_ref, gain_ref, state_ref, left_a, left_b, out_ref, rows_ref):
     @on_shard(1)
     def _():
         for head, lanes in head_lanes(state_ref.shape[0]):
             rows_ref[:, lanes] = rows_of_next(both_ref, gain_ref, head, lanes, state_ref[head])
-        project_to(out_ref, rows_ref[...], left_ref)
+        project_to(out_ref, rows_ref[...], (left_a, left_b))
 
 
 def fourth_rows_kernel(map_ref, add_ref, both_ref, gain_ref, state_ref, out_ref):
@@ -414,21 +416,20 @@
 
 
 def near_columns_kernel(
-    direct_ref, reach_ref, gain_ref, state_ref, rows0_ref, rows1_ref, rows3_ref, own_ref, left_ref, right_ref,
+    direct_ref, reach_ref, gain_ref, state_ref, rows0_ref, rows1_ref, rows3_ref, own_ref, left_ref, left_a, left_b, right_ref,
     own_three, next_three, rows_ref,
 ):
-    weights = (own_ref, right_ref, left_ref)
-
     @on_shard(0)
     def _():
-        project_to(own_three, rows0_ref[...], *weights[:2])
+        project_to(own_three.at[:, : 2 * own_ref.shape[1]], rows0_ref[...], own_ref, right_ref)
 
     @on_shard(1)
     def _():
-        project_to(own_three, rows1_ref[...], *weights)
+        project_to(own_three, rows1_ref[...], own_ref, right_ref, (left_a, left_b))
 
     @on_shard(2)
     def _():
+        weights = (own_ref, right_ref, left_ref)
         project_to(next_three, rows3_ref[...], *weights)
         rows_with_state(direct_ref, reach_ref, gain_ref, state_ref, rows_ref)
         project_to(own_three, rows_ref[...], *weights)
@@ -440,10 +441,10 @@
         project_to(out_ref, rows_ref[...], left_ref, own_ref)
 
 
-def far_columns_kernel(rows1_ref, rows3_ref, left_ref, right_ref, out_ref):
+def far_columns_kernel(rows1_ref, rows3_ref, left_a, left_b, right_ref, out_ref):
     @on_shard(1)
     def _():
-        project_to(out_ref, rows3_ref[...], left_ref)
+        project_to(out_ref, rows3_ref[...], (left_a, left_b))
 
     @on_shard(2)
     def _():
@@ -508,10 +509,15 @@
     )
     rim = moved(edge, [(c, c + 1) for c in range(count - 1)])
     later_acts = later_activations(x, taps)
-    rim, later_acts, own = lax.optimization_barrier((rim, later_acts, w_out[0]))
-    rights = [moved(own, [(c, c + 1) for c in range(count - 1)])]
+    whole = own = w_out[0]
     lefts = [moved(own, [(c, c - 1) for c in range(1, count)])]
-    if count != 4:
+    if count == 4:
+        top, rest = own[: width // 2], own[width // 2 :]
+        rim, later_acts, own, top = lax.optimization_barrier((rim, later_acts, own, top))
+        left = moved(own, [(1, 2), (2, 3)])
+        top = moved(top, [(0, 1)])
+    else:
+        rights = [moved(own, [(c, c + 1) for c in range(count - 1)])]
         for turn in range(2, count):
             rights.append(moved(rights[-1], [(c, c + 1) for c in range(turn - 1, count - 1)]))
             lefts.append(moved(lefts[-1], [(c, c - 1) for c in range(1, count - turn + 1)]))
@@ -525,39 +531,41 @@
         mixed = project(states, direct, reach, norm_gain, own, rights, lefts)
         return handed(mixed, [(c, c) for c in range(count)])[None]
 
-    left, right = rights[0], lefts[0]
+    right = lefts[0]
     cols = own.shape[1]
     rows = (toks, width)
     one, two, three = ((toks, blocks * cols) for blocks in (1, 2, 3))
+    sent, top, right = lax.optimization_barrier((sent, top, lefts[0]))
     first = moved(sent, [(0, 1)])
     both = moved(both, [(3, 2), (2, 1)])
+    out1 = hand_on(total_map, total_add, first)
+    second = moved(out1, [(1, 2)])
     rows0 = call(first_rows_kernel, [direct, norm_gain], [rows])
     far0 = moved(rows0, [(0, 3)])
-    first, far0 = lax.optimization_barrier((first, far0))
-    out1 = hand_on(total_map, total_add, first)
-    second = moved(out1, [(1, 2)])
     rows1 = call(second_rows_kernel, [direct, reach, norm_gain, first], [rows])
+    rows1, rest = lax.optimization_barrier((rows1, rest))
     far1 = moved(rows1, [(1, 2)])
-    third_one = call(third_columns_kernel, [both, norm_gain, out1, left], [one], [rows])
-    first_two = call(first_columns_kernel, [far0, own, left], [two])
-    third_one, first_two, rows1 = lax.optimization_barrier((third_one, first_two, rows1))
-    third_one, first_two = handed(third_one, [(1, 2)]), handed(first_two, [(3, 0)])
+    rest = moved(rest, [(0, 1)])
+    both, second = lax.optimization_barrier((both, second))
     rows3 = call(fourth_rows_kernel, [total_map, total_add, both, norm_gain, second], [rows])
     far3 = moved(rows3, [(2, 1)])
     own_three, next_three = call(
         near_columns_kernel,
-        [direct, reach, norm_gain, second, rows0, rows1, rows3, own, left, right],
+        [direct, reach, norm_gain, second, rows0, rows1, rows3, whole, left, top, rest, right],
         [three, three],
         [rows],
     )
-    far_one = call(far_columns_kernel, [far1, far3, left, right], [one])
+    third_one = call(third_columns_kernel, [both, norm_gain, out1, top, rest], [one], [rows])
+    first_two = call(first_columns_kernel, [far0, whole, left], [two])
+    far_one = call(far_columns_kernel, [far1, far3, top, rest, right], [one])
+    far_one, third_one = lax.optimization_barrier((far_one, third_one))
     return call(
         assemble_kernel,
         [
             handed(own_three, [(0, 0), (1, 1), (2, 2)]),
             handed(next_three, [(2, 3)]),
-            third_one,
-            first_two,
+            handed(third_one, [(1, 2)]),
+            handed(first_two, [(3, 0)]),
             handed(far_one, [(2, 1), (1, 3)]),
         ],
         [(toks, 4 * cols)],

time: 73.9 us -> 72.7 us (0.984)
  the two profiles are of different devices: /device:TPU:24 before, /device:TPU:8 now
where the time goes in v6:
time: 72.7 us; the launch traced here: 72.3 us
  starting transfers between devices  29 us (40%)
  waiting for transfers between devices  22.4 us (31%)
  Pallas kernels  20.4 us (28%)
    ppermute x11, starting transfers between devices, moved(): return lax.ppermute(value, 'ctx', pairs)  20.4 us
    pallas_call x3, Pallas kernels, kernel_call(): pl.pallas_call(kernel, in_specs=[pl.BlockSpec(memory_space=space)] * len(...  15.8 us
    ppermute x11, waiting for transfers between devices, moved(): return lax.ppermute(value, 'ctx', pairs)  14.7 us
    ppermute x5, starting transfers between devices, handed(): lax.ppermute(value, ('section', 'ctx'), [(s * count + a, (s + 1) % sectio...  8.61 us
    ppermute x5, waiting for transfers between devices, handed(): lax.ppermute(value, ('section', 'ctx'), [(s * count + a, (s + 1) % sectio...  7.75 us
    pallas_call x8, Pallas kernels, call(): pl.pallas_call(kernel, in_specs=[vmem] * len(operands), out_specs=[vmem]...  2.97 us
  transfers between devices with their start and end apart: 16, of which 5 were waited for; matrix products, arithmetic and copies ran while one was open for 0% of the time, Pallas kernels for 27%

profile of v6, /device:TPU:8, one launch (start us, length us, event | category | flops | bytes accessed | tf_op | source)
XLA Modules:
  0.0 72.3 jit_solution(15868882831745572798)
XLA Ops:
  0.0 2.0 %collective-permute-start.3 = (bf16[1024,512]{1,0:T(8,128)(2,1)}, bf16[1024,512]{1,0:T(8,128)(2,1)S(1)}, u32[]{:S(2)}, u32[]{:S(2)}) collective-permute-start(bf16[1024,512]{1,0:T(8,128)(2,1)} %bitcast.14), channel_id=1, source_target_pairs={{1,0},{2,1},{3,2},{5,4},{6,5},{7,6},{9,8},{10,9},{11,10},{13,12},{... | collective-permute-start | bytes 3145736 | tf_op jit(solution)/shard_map/ppermute | solution.py:488
  2.0 1.4 %shard_map.64 = (bf16[128,5120]{1,0:T(8,128)(2,1)S(1)}, bf16[4,5120]{1,0:T(4,128)(2,1)S(1)}, f32[16,128]{1,0:T(8,128)S(1)}, f32[8,128]{1,0:T(8,128)S(1)}, bf16[3,5120]{1,0:T(4,128)(2,1)S(1)}) custom-call(bf16[128,5120]{1,0:T(8,128)(2,1)} %bitcast.18, bf16[4,5120]{1,0:T(4,128)(2,1)} %bitcast.19, f32[16,128]{1,0:T(8,128)} %bitcast.20, f32[8,128]{1,0:T(8,128)} %bitcast.21), custom_call_target="tpu_custom_call" | custom-call | tf_op jit(solution)/shard_map/pallas_call | solution.py:227
  3.4 3.9 %collective-permute-start = (bf16[3,5120]{1,0:T(4,128)(2,1)S(1)}, bf16[3,5120]{1,0:T(4,128)(2,1)S(1)}, u32[]{:S(2)}, u32[]{:S(2)}) collective-permute-start(bf16[3,5120]{1,0:T(4,128)(2,1)S(1)} %get-tuple-element.35), channel_id=1, source_target_pairs={{0,1},{1,2},{2,3},{4,5},{5,6},{6,7},{8,9},{9,10},{10,11},{12,13},{... | collective-permute-start | bytes 92168 | tf_op jit(solution)/shard_map/ppermute | solution.py:488
  7.5 1.4 %shard_map.65.act_ref = f32[64,5120]{1,0:T(8,128)S(1)} custom-call(bf16[128,5120]{1,0:T(8,128)(2,1)S(1)} %get-tuple-element.36.x_ref, bf16[4,5120]{1,0:T(4,128)(2,1)S(1)} %get-tuple-element.37.taps_ref), custom_call_target="tpu_custom_call" | custom-call | flops 1048576 | bytes 65536 | tf_op jit(solution)/shard_map/pallas_call | solution.py:213
  9.3 1.3 %collective-permute-start.2 = (bf16[512,512]{1,0:T(8,128)(2,1)S(1)}, bf16[512,512]{1,0:T(8,128)(2,1)S(1)}, u32[]{:S(2)}, u32[]{:S(2)}) collective-permute-start(bf16[512,512]{1,0:T(8,128)(2,1)S(1)} %get-tuple-element.52), channel_id=1, source_target_pairs={{0,1},{4,5},{8,9},{12,13},{16,17},{20,21},{24,25},{28,29}} | collective-permute-start | bytes 1572872 | tf_op jit(solution)/shard_map/ppermute | solution.py:488
  10.6 3.4 %collective-permute-start.6 = (bf16[1024,512]{1,0:T(8,128)(2,1)S(1)}, bf16[1024,512]{1,0:T(8,128)(2,1)S(1)}, u32[]{:S(2)}, u32[]{:S(2)}) collective-permute-start(bf16[1024,512]{1,0:T(8,128)(2,1)S(1)} %bitcast.15), channel_id=1, source_target_pairs={{1,2},{2,3},{5,6},{6,7},{9,10},{10,11},{13,14},{14,15},{17,18},{18... | collective-permute-start | bytes 3145736 | tf_op jit(solution)/shard_map/ppermute | solution.py:488
  14.0 6.5 %shard_map.66 = (f32[8,128,128]{2,1,0:T(8,128)S(1)}, f32[8,128,128]{2,1,0:T(8,128)S(1)}, f32[64,1024]{1,0:T(8,128)S(1)}, f32[64,1024]{1,0:T(8,128)S(1)}) custom-call(f32[64,5120]{1,0:T(8,128)S(1)} %shard_map.65.act_ref, f32[16,128]{1,0:T(8,128)S(1)} %get-tuple-element.39.beta_ref, f32[8,128]{1,0:T(8,128)S(1)} %get-tuple-element.40.gate_ref), custom_call_target="tpu_custom_call" | custom-call | flops 1048576 | bytes 65536 | tf_op jit(solution)/shard_map/pallas_call | solution.py:213
  20.5 7.9 %shard_map.67 = (f32[8,128,128]{2,1,0:T(8,128)S(1)}, f32[8,128,128]{2,1,0:T(8,128)S(1)}, bf16[8,128,128]{2,1,0:T(8,128)(2,1)S(1)}, f32[128,1024]{1,0:T(8,128)S(1...) custom-call(bf16[3,5120]{1,0:T(4,128)(2,1)S(1)} %collective-permute-done.rim_ref, ...), custom_call_target="tpu_custom_call" | custom-call | flops 1048576 | bytes 65536 | tf_op jit(solution)/shard_map/pallas_call | solution.py:213
  28.4 1.3 %collective-permute-start.4 = (bf16[8,128,128]{2,1,0:T(8,128)(2,1)S(1)}, bf16[8,128,128]{2,1,0:T(8,128)(2,1)S(1)}, u32[]{:S(2)}, u32[]{:S(2)}) collective-permute-start(bf16[8,128,128]{2,1,0:T(8,128)(2,1)S(1)} %get-tuple-element.53), channel_id=1, source_target_pairs={{0,1},{4,5},{8,9},{12,13},{16,17},{20,21},{24,25},{28,29}} | collective-permute-start | bytes 786440 | tf_op jit(solution)/shard_map/ppermute | solution.py:488
  29.7 1.3 %collective-permute-start.1 = (bf16[2,128,1024]{2,1,0:T(8,128)(2,1)S(1)}, bf16[2,128,1024]{2,1,0:T(8,128)(2,1)S(1)}, u32[]{:S(2)}, u32[]{:S(2)}) collective-permute-start(bf16[2,128,1024]{2,1,0:T(8,128)(2,1)S(1)} %get-tuple-element.48), channel_id=1, source_target_pairs={{3,2},{2,1},{7,6},{6,5},{11,10},{10,9},{15,14},{14,13},{19,18},{18... | collective-permute-start | bytes 1572872 | tf_op jit(solution)/shard_map/ppermute | solution.py:488
  31.0 5.9 %collective-permute-done.4.state_ref = bf16[8,128,128]{2,1,0:T(8,128)(2,1)S(1)} collective-permute-done((bf16[8,128,128]{2,1,0:T(8,128)(2,1)S(1)}, bf16[8,128,128]{2,1,0:T(8,128)(2,1)S(1)}, u32[]{:S(2)}, u32[]{:S(2)}) %collective-permute-start.4) | collective-permute-done | bytes 262176 | tf_op jit(solution)/shard_map/ppermute | solution.py:488
  37.4 1.3 %collective-permute-start.7 = (bf16[512,512]{1,0:T(8,128)(2,1)S(1)}, bf16[512,512]{1,0:T(8,128)(2,1)S(1)}, u32[]{:S(2)}, u32[]{:S(2)}) collective-permute-start(bf16[512,512]{1,0:T(8,128)(2,1)S(1)} %get-tuple-element.59), channel_id=1, source_target_pairs={{0,1},{4,5},{8,9},{12,13},{16,17},{20,21},{24,25},{28,29}} | collective-permute-start | bytes 1572872 | tf_op jit(solution)/shard_map/ppermute | solution.py:488
  39.0 1.3 %collective-permute-start.5 = (bf16[8,128,128]{2,1,0:T(8,128)(2,1)S(1)}, bf16[8,128,128]{2,1,0:T(8,128)(2,1)S(1)}, u32[]{:S(2)}, u32[]{:S(2)}) collective-permute-start(bf16[8,128,128]{2,1,0:T(8,128)(2,1)S(1)} %shard_map.68.state_ref), channel_id=1, source_target_pairs={{1,2},{5,6},{9,10},{13,14},{17,18},{21,22},{25,26},{29,30}} | collective-permute-start | bytes 786440 | tf_op jit(solution)/shard_map/ppermute | solution.py:488
  41.0 2.9 %collective-permute-done.1.both_ref = bf16[2,128,1024]{2,1,0:T(8,128)(2,1)S(1)} collective-permute-done((bf16[2,128,1024]{2,1,0:T(8,128)(2,1)S(1)}, bf16[2,128,1024]{2,1,0:T(8,128)(2,1)S(1)}, u32[]{:S(2)}, u32[]{:S(2)}) %collective-permute-start.1) | collective-permute-done | bytes 524320 | tf_op jit(solution)/shard_map/ppermute | solution.py:488
  43.9 2.6 %collective-permute-start.10 = (bf16[128,1024]{1,0:T(8,128)(2,1)S(1)}, bf16[128,1024]{1,0:T(8,128)(2,1)S(1)}, u32[]{:S(2)}, u32[]{:S(2)}) collective-permute-start(bf16[128,1024]{1,0:T(8,128)(2,1)S(1)} %shard_map.70.rows1_ref), channel_id=1, source_target_pairs={{1,2},{5,6},{9,10},{13,14},{17,18},{21,22},{25,26},{29,30}} | collective-permute-start | bytes 786440 | tf_op jit(solution)/shard_map/ppermute | solution.py:488
  46.7 1.3 %collective-permute-start.11 = (bf16[128,1024]{1,0:T(8,128)(2,1)S(1)}, bf16[128,1024]{1,0:T(8,128)(2,1)S(1)}, u32[]{:S(2)}, u32[]{:S(2)}) collective-permute-start(bf16[128,1024]{1,0:T(8,128)(2,1)S(1)} %shard_map.71.rows3_ref), channel_id=1, source_target_pairs={{2,1},{6,5},{10,9},{14,13},{18,17},{22,21},{26,25},{30,29}} | collective-permute-start | bytes 786440 | tf_op jit(solution)/shard_map/ppermute | solution.py:488
  48.0 5.4 %collective-permute-done.7.left_b = bf16[512,512]{1,0:T(8,128)(2,1)S(1)} collective-permute-done((bf16[512,512]{1,0:T(8,128)(2,1)S(1)}, bf16[512,512]{1,0:T(8,128)(2,1)S(1)}, u32[]{:S(2)}, u32[]{:S(2)}) %collective-permute-start.7) | collective-permute-done | bytes 524320 | tf_op jit(solution)/shard_map/ppermute | solution.py:488
  54.0 1.9 %collective-permute-start.8 = (bf16[128,1536]{1,0:T(8,128)(2,1)S(1)}, bf16[128,1536]{1,0:T(8,128)(2,1)S(1)}, u32[]{:S(2)}, u32[]{:S(2)}) collective-permute-start(bf16[128,1536]{1,0:T(8,128)(2,1)S(1)} %get-tuple-element.61), channel_id=1, source_target_pairs={{0,4},{1,5},{2,6},{4,8},{5,9},{6,10},{8,12},{9,13},{10,14},{12,16}... | collective-permute-start | bytes 1179656 | tf_op jit(solution)/shard_map/ppermute | solution.py:493
  55.9 0.7 collective-permute-start.9
  56.6 0.7 collective-permute-start.14
  58.3 1.3 %collective-permute-start.12 = (bf16[128,512]{1,0:T(8,128)(2,1)S(1)}, bf16[128,512]{1,0:T(8,128)(2,1)S(1)}, u32[]{:S(2)}, u32[]{:S(2)}) collective-permute-start(bf16[128,512]{1,0:T(8,128)(2,1)S(1)} %shard_map.74), channel_id=1, source_target_pairs={{1,6},{5,10},{9,14},{13,18},{17,22},{21,26},{25,30},{29,2}} | collective-permute-start | bytes 393224 | tf_op jit(solution)/shard_map/ppermute | solution.py:493
  59.6 4.0 %collective-permute-start.15 = (bf16[128,512]{1,0:T(8,128)(2,1)S(1)}, bf16[128,512]{1,0:T(8,128)(2,1)S(1)}, u32[]{:S(2)}, u32[]{:S(2)}) collective-permute-start(bf16[128,512]{1,0:T(8,128)(2,1)S(1)} %shard_map.73), channel_id=1, source_target_pairs={{2,5},{1,7},{6,9},{5,11},{10,13},{9,15},{14,17},{13,19},{18,21},{1... | collective-permute-start | bytes 393224 | tf_op jit(solution)/shard_map/ppermute | solution.py:493
  63.7 7.7 %collective-permute-done.15.far_one = bf16[128,512]{1,0:T(8,128)(2,1)S(1)} collective-permute-done((bf16[128,512]{1,0:T(8,128)(2,1)S(1)}, bf16[128,512]{1,0:T(8,128)(2,1)S(1)}, u32[]{:S(2)}, u32[]{:S(2)}) %collective-permute-start.15) | collective-permute-done | bytes 131104 | tf_op jit(solution)/shard_map/ppermute | solution.py:493
  71.4 0.8 %shard_map.76 = bf16[128,2048]{1,0:T(8,128)(2,1)} custom-call(bf16[128,1536]{1,0:T(8,128)(2,1)S(1)} %collective-permute-done.8.own_three, bf16[128,1536]{1,0:T(8,128)(2,1)S(1)} %collective-permute-done.9.next_three, bf16[128,512]{1,0:T(8,128)(2,1)S(1)} %collective-permute-done.12.third_one, bf16[128,1024]{1,0:T(8,128)(2,1)S(1)} %collective-permute-done.14.first_two, ...), custom_call_target="tpu_custom_call" | custom-call | flops 1048576 | bytes 65536 | tf_op jit(solution)/shard_map/pallas_call | solution.py:457
  (26 shorter events, 3.6 us)
Async XLA Ops:
  0.0 7.4 %copy-start = (bf16[1,1024,512]{2,1,0:T(8,128)(2,1)S(1)}, bf16[1,1024,512]{2,1,0:T(8,128)(2,1)}, u32[]{:S(2)}) copy-start(bf16[1,1024,512]{2,1,0:T(8,128)(2,1)} %param.11) | copy-start | bytes 3145732
  0.0 28.4 %collective-permute-start.3 = (bf16[1024,512]{1,0:T(8,128)(2,1)}, bf16[1024,512]{1,0:T(8,128)(2,1)S(1)}, u32[]{:S(2)}, u32[]{:S(2)}) collective-permute-start(bf16[1024,512]{1,0:T(8,128)(2,1)} %bitcast.14), channel_id=1, source_target_pairs={{1,0},{2,1},{3,2},{5,4},{6,5},{7,6},{9,8},{10,9},{11,10},{13,12},{... | collective-permute-start | bytes 3145736 | tf_op jit(solution)/shard_map/ppermute | solution.py:488
  3.4 5.9 %collective-permute-start = (bf16[3,5120]{1,0:T(4,128)(2,1)S(1)}, bf16[3,5120]{1,0:T(4,128)(2,1)S(1)}, u32[]{:S(2)}, u32[]{:S(2)}) collective-permute-start(bf16[3,5120]{1,0:T(4,128)(2,1)S(1)} %get-tuple-element.35), channel_id=1, source_target_pairs={{0,1},{1,2},{2,3},{4,5},{5,6},{6,7},{8,9},{9,10},{10,11},{12,13},{... | collective-permute-start | bytes 92168 | tf_op jit(solution)/shard_map/ppermute | solution.py:488
  9.3 19.1 %collective-permute-start.2 = (bf16[512,512]{1,0:T(8,128)(2,1)S(1)}, bf16[512,512]{1,0:T(8,128)(2,1)S(1)}, u32[]{:S(2)}, u32[]{:S(2)}) collective-permute-start(bf16[512,512]{1,0:T(8,128)(2,1)S(1)} %get-tuple-element.52), channel_id=1, source_target_pairs={{0,1},{4,5},{8,9},{12,13},{16,17},{20,21},{24,25},{28,29}} | collective-permute-start | bytes 1572872 | tf_op jit(solution)/shard_map/ppermute | solution.py:488
  10.6 37.4 %collective-permute-start.6 = (bf16[1024,512]{1,0:T(8,128)(2,1)S(1)}, bf16[1024,512]{1,0:T(8,128)(2,1)S(1)}, u32[]{:S(2)}, u32[]{:S(2)}) collective-permute-start(bf16[1024,512]{1,0:T(8,128)(2,1)S(1)} %bitcast.15), channel_id=1, source_target_pairs={{1,2},{2,3},{5,6},{6,7},{9,10},{10,11},{13,14},{14,15},{17,18},{18... | collective-permute-start | bytes 3145736 | tf_op jit(solution)/shard_map/ppermute | solution.py:488
  20.5 16.5 %copy-start.1 = (f32[1,1024]{1,0:T(1,128)S(1)}, f32[1,1024]{1,0:T(1,128)}, u32[]{:S(2)}) copy-start(f32[1,1024]{1,0:T(1,128)} %gain_ref.9) | copy-start | bytes 12292
  28.4 8.5 %collective-permute-start.4 = (bf16[8,128,128]{2,1,0:T(8,128)(2,1)S(1)}, bf16[8,128,128]{2,1,0:T(8,128)(2,1)S(1)}, u32[]{:S(2)}, u32[]{:S(2)}) collective-permute-start(bf16[8,128,128]{2,1,0:T(8,128)(2,1)S(1)} %get-tuple-element.53), channel_id=1, source_target_pairs={{0,1},{4,5},{8,9},{12,13},{16,17},{20,21},{24,25},{28,29}} | collective-permute-start | bytes 786440 | tf_op jit(solution)/shard_map/ppermute | solution.py:488
  29.7 14.1 %collective-permute-start.1 = (bf16[2,128,1024]{2,1,0:T(8,128)(2,1)S(1)}, bf16[2,128,1024]{2,1,0:T(8,128)(2,1)S(1)}, u32[]{:S(2)}, u32[]{:S(2)}) collective-permute-start(bf16[2,128,1024]{2,1,0:T(8,128)(2,1)S(1)} %get-tuple-element.48), channel_id=1, source_target_pairs={{3,2},{2,1},{7,6},{6,5},{11,10},{10,9},{15,14},{14,13},{19,18},{18... | collective-permute-start | bytes 1572872 | tf_op jit(solution)/shard_map/ppermute | solution.py:488
  37.4 16.0 %collective-permute-start.7 = (bf16[512,512]{1,0:T(8,128)(2,1)S(1)}, bf16[512,512]{1,0:T(8,128)(2,1)S(1)}, u32[]{:S(2)}, u32[]{:S(2)}) collective-permute-start(bf16[512,512]{1,0:T(8,128)(2,1)S(1)} %get-tuple-element.59), channel_id=1, source_target_pairs={{0,1},{4,5},{8,9},{12,13},{16,17},{20,21},{24,25},{28,29}} | collective-permute-start | bytes 1572872 | tf_op jit(solution)/shard_map/ppermute | solution.py:488
  39.0 7.5 %collective-permute-start.5 = (bf16[8,128,128]{2,1,0:T(8,128)(2,1)S(1)}, bf16[8,128,128]{2,1,0:T(8,128)(2,1)S(1)}, u32[]{:S(2)}, u32[]{:S(2)}) collective-permute-start(bf16[8,128,128]{2,1,0:T(8,128)(2,1)S(1)} %shard_map.68.state_ref), channel_id=1, source_target_pairs={{1,2},{5,6},{9,10},{13,14},{17,18},{21,22},{25,26},{29,30}} | collective-permute-start | bytes 786440 | tf_op jit(solution)/shard_map/ppermute | solution.py:488
  40.3 16.3 %collective-permute-start.13 = (bf16[128,1024]{1,0:T(8,128)(2,1)S(1)}, bf16[128,1024]{1,0:T(8,128)(2,1)S(1)}, u32[]{:S(2)}, u32[]{:S(2)}) collective-permute-start(bf16[128,1024]{1,0:T(8,128)(2,1)S(1)} %shard_map.69.rows0_ref), channel_id=1, source_target_pairs={{0,3},{4,7},{8,11},{12,15},{16,19},{20,23},{24,27},{28,31}} | collective-permute-start | bytes 786440 | tf_op jit(solution)/shard_map/ppermute | solution.py:488
  43.9 14.1 %collective-permute-start.10 = (bf16[128,1024]{1,0:T(8,128)(2,1)S(1)}, bf16[128,1024]{1,0:T(8,128)(2,1)S(1)}, u32[]{:S(2)}, u32[]{:S(2)}) collective-permute-start(bf16[128,1024]{1,0:T(8,128)(2,1)S(1)} %shard_map.70.rows1_ref), channel_id=1, source_target_pairs={{1,2},{5,6},{9,10},{13,14},{17,18},{21,22},{25,26},{29,30}} | collective-permute-start | bytes 786440 | tf_op jit(solution)/shard_map/ppermute | solution.py:488
  46.7 11.3 %collective-permute-start.11 = (bf16[128,1024]{1,0:T(8,128)(2,1)S(1)}, bf16[128,1024]{1,0:T(8,128)(2,1)S(1)}, u32[]{:S(2)}, u32[]{:S(2)}) collective-permute-start(bf16[128,1024]{1,0:T(8,128)(2,1)S(1)} %shard_map.71.rows3_ref), channel_id=1, source_target_pairs={{2,1},{6,5},{10,9},{14,13},{18,17},{22,21},{26,25},{30,29}} | collective-permute-start | bytes 786440 | tf_op jit(solution)/shard_map/ppermute | solution.py:488
  54.0 17.4 %collective-permute-start.8 = (bf16[128,1536]{1,0:T(8,128)(2,1)S(1)}, bf16[128,1536]{1,0:T(8,128)(2,1)S(1)}, u32[]{:S(2)}, u32[]{:S(2)}) collective-permute-start(bf16[128,1536]{1,0:T(8,128)(2,1)S(1)} %get-tuple-element.61), channel_id=1, source_target_pairs={{0,4},{1,5},{2,6},{4,8},{5,9},{6,10},{8,12},{9,13},{10,14},{12,16}... | collective-permute-start | bytes 1179656 | tf_op jit(solution)/shard_map/ppermute | solution.py:493
  55.9 15.5 %collective-permute-start.9 = (bf16[128,1536]{1,0:T(8,128)(2,1)S(1)}, bf16[128,1536]{1,0:T(8,128)(2,1)S(1)}, u32[]{:S(2)}, u32[]{:S(2)}) collective-permute-start(bf16[128,1536]{1,0:T(8,128)(2,1)S(1)} %get-tuple-element.62), channel_id=1, source_target_pairs={{2,7},{6,11},{10,15},{14,19},{18,23},{22,27},{26,31},{30,3}} | collective-permute-start | bytes 1179656 | tf_op jit(solution)/shard_map/ppermute | solution.py:493
  56.6 7.0 %collective-permute-start.14 = (bf16[128,1024]{1,0:T(8,128)(2,1)S(1)}, bf16[128,1024]{1,0:T(8,128)(2,1)S(1)}, u32[]{:S(2)}, u32[]{:S(2)}) collective-permute-start(bf16[128,1024]{1,0:T(8,128)(2,1)S(1)} %shard_map.75), channel_id=1, source_target_pairs={{3,4},{7,8},{11,12},{15,16},{19,20},{23,24},{27,28},{31,0}} | collective-permute-start | bytes 786440 | tf_op jit(solution)/shard_map/ppermute | solution.py:493
  58.3 5.4 %collective-permute-start.12 = (bf16[128,512]{1,0:T(8,128)(2,1)S(1)}, bf16[128,512]{1,0:T(8,128)(2,1)S(1)}, u32[]{:S(2)}, u32[]{:S(2)}) collective-permute-start(bf16[128,512]{1,0:T(8,128)(2,1)S(1)} %shard_map.74), channel_id=1, source_target_pairs={{1,6},{5,10},{9,14},{13,18},{17,22},{21,26},{25,30},{29,2}} | collective-permute-start | bytes 393224 | tf_op jit(solution)/shard_map/ppermute | solution.py:493
  59.6 11.8 %collective-permute-start.15 = (bf16[128,512]{1,0:T(8,128)(2,1)S(1)}, bf16[128,512]{1,0:T(8,128)(2,1)S(1)}, u32[]{:S(2)}, u32[]{:S(2)}) collective-permute-start(bf16[128,512]{1,0:T(8,128)(2,1)S(1)} %shard_map.73), channel_id=1, source_target_pairs={{2,5},{1,7},{6,9},{5,11},{10,13},{9,15},{14,17},{13,19},{18,21},{1... | collective-permute-start | bytes 393224 | tf_op jit(solution)/shard_map/ppermute | solution.py:493

commit v7 on v4

--- a/solution.py
+++ b/solution.py
@@ -242,7 +242,6 @@
         (x, taps),
         [((half, channels), f32)],
         scratch=[pltpu.VMEM((8 + half, channels), f32)],
-        cost=2**27,
     )[0]
 
 
@@ -381,25 +380,22 @@
     return normed_rows(out, gain_ref[:, lanes])
 
 
-def first_rows_kernel(direct_ref, gain_ref, out_ref):
+def early_rows_kernel(direct_ref, reach_ref, gain_ref, state_ref, out_ref):
     @on_shard(0)
     def _():
-        for head, lanes in head_lanes(direct_ref.shape[1] // HK):
+        for head, lanes in head_lanes(state_ref.shape[0]):
             out_ref[:, lanes] = normed_rows(direct_ref[:, lanes], gain_ref[:, lanes])
 
-
-def second_rows_kernel(direct_ref, reach_ref, gain_ref, state_ref, out_ref):
     @on_shard(1)
     def _():
         rows_with_state(direct_ref, reach_ref, gain_ref, state_ref, out_ref)
 
 
-def third_columns_kernel(both_ref, gain_ref, state_ref, left_ref, out_ref, rows_ref):
+def third_rows_kernel(both_ref, gain_ref, state_ref, out_ref):
     @on_shard(1)
     def _():
         for head, lanes in head_lanes(state_ref.shape[0]):
-            rows_ref[:, lanes] = rows_of_next(both_ref, gain_ref, head, lanes, state_ref[head])
-        project_to(out_ref, rows_ref[...], left_ref)
+            out_ref[:, lanes] = rows_of_next(both_ref, gain_ref, head, lanes, state_ref[head])
 
 
 def fourth_rows_kernel(map_ref, add_ref, both_ref, gain_ref, state_ref, out_ref):
@@ -414,40 +410,45 @@
 
 
 def near_columns_kernel(
-    direct_ref, reach_ref, gain_ref, state_ref, rows0_ref, rows1_ref, rows3_ref, own_ref, left_ref, right_ref,
+    direct_ref, reach_ref, gain_ref, state_ref, early_ref, rows3_ref, own_ref, left_ref, right_ref,
     own_three, next_three, rows_ref,
 ):
-    weights = (own_ref, right_ref, left_ref)
-
-    @on_shard(0)
-    def _():
-        project_to(own_three, rows0_ref[...], *weights[:2])
-
-    @on_shard(1)
-    def _():
-        project_to(own_three, rows1_ref[...], *weights)
+    @pl.when(lax.axis_index("ctx") < 2)
+    def _():
+        project_to(own_three, early_ref[...], own_ref, right_ref)
 
     @on_shard(2)
     def _():
+        weights = (own_ref, right_ref, left_ref)
         project_to(next_three, rows3_ref[...], *weights)
         rows_with_state(direct_ref, reach_ref, gain_ref, state_ref, rows_ref)
         project_to(own_three, rows_ref[...], *weights)
 
 
-def first_columns_kernel(rows_ref, own_ref, left_ref, out_ref):
+def early_columns_kernel(rows_ref, own_ref, left_ref, out_ref):
+    @on_shard(0)
+    def _():
+        project_to(out_ref, rows_ref[...], own_ref)
+
     @on_shard(3)
     def _():
         project_to(out_ref, rows_ref[...], left_ref, own_ref)
 
 
-def far_columns_kernel(rows1_ref, rows3_ref, left_ref, right_ref, out_ref):
-    @on_shard(1)
-    def _():
-        project_to(out_ref, rows3_ref[...], left_ref)
+def far_columns_kernel(rows1_ref, rows3_ref, own_ref, right_ref, out_ref):
+    @on_shard(0)
+    def _():
+        project_to(out_ref, rows3_ref[...], own_ref)
 
     @on_shard(2)
     def _():
         project_to(out_ref, rows1_ref[...], right_ref)
+
+
+def third_columns_kernel(rows_ref, own_ref, out_ref):
+    @on_shard(0)
+    def _():
+        project_to(out_ref, rows_ref[...], own_ref)
 
 
 def call(kernel, operands, out_shapes, scratch=()):
@@ -465,13 +466,14 @@
     return found if len(shapes) > 1 else found[0]
 
 
-def assemble_kernel(own_three, next_three, third_one, first_two, far_one, out_ref):
+def assemble_kernel(own_three, next_three, third_one, early_two, far_one, out_ref):
     cols = far_one.shape[1]
     own = [(own_three, index) for index in range(3)]
     after = [(next_three, index) for index in range(3)]
+    early = [(early_two, index) for index in range(2)]
     sources = (
-        (own[0], own[1], (first_two, 0), (first_two, 1)),
-        (own[2], own[0], own[1], (far_one, 0)),
+        (own[0], own[1], early[0], early[1]),
+        (early[0], own[0], own[1], (far_one, 0)),
         ((third_one, 0), own[2], own[0], own[1]),
         ((far_one, 0), after[2], after[0], after[1]),
     )
@@ -508,10 +510,13 @@
     )
     rim = moved(edge, [(c, c + 1) for c in range(count - 1)])
     later_acts = later_activations(x, taps)
-    rim, later_acts, own = lax.optimization_barrier((rim, later_acts, w_out[0]))
-    rights = [moved(own, [(c, c + 1) for c in range(count - 1)])]
+    own = w_out[0]
     lefts = [moved(own, [(c, c - 1) for c in range(1, count)])]
-    if count != 4:
+    if count == 4:
+        rim, later_acts, held = lax.optimization_barrier((rim, later_acts, own))
+        left = moved(held, [(1, 2), (2, 3)])
+    else:
+        rights = [moved(own, [(c, c + 1) for c in range(count - 1)])]
         for turn in range(2, count):
             rights.append(moved(rights[-1], [(c, c + 1) for c in range(turn - 1, count - 1)]))
             lefts.append(moved(lefts[-1], [(c, c - 1) for c in range(1, count - turn + 1)]))
@@ -525,40 +530,41 @@
         mixed = project(states, direct, reach, norm_gain, own, rights, lefts)
         return handed(mixed, [(c, c) for c in range(count)])[None]
 
-    left, right = rights[0], lefts[0]
+    right = lefts[0]
     cols = own.shape[1]
     rows = (toks, width)
     one, two, three = ((toks, blocks * cols) for blocks in (1, 2, 3))
+    sent, right = lax.optimization_barrier((sent, lefts[0]))
     first = moved(sent, [(0, 1)])
     both = moved(both, [(3, 2), (2, 1)])
-    rows0 = call(first_rows_kernel, [direct, norm_gain], [rows])
-    far0 = moved(rows0, [(0, 3)])
-    first, far0 = lax.optimization_barrier((first, far0))
     out1 = hand_on(total_map, total_add, first)
     second = moved(out1, [(1, 2)])
-    rows1 = call(second_rows_kernel, [direct, reach, norm_gain, first], [rows])
-    far1 = moved(rows1, [(1, 2)])
-    third_one = call(third_columns_kernel, [both, norm_gain, out1, left], [one], [rows])
-    first_two = call(first_columns_kernel, [far0, own, left], [two])
-    third_one, first_two, rows1 = lax.optimization_barrier((third_one, first_two, rows1))
-    third_one, first_two = handed(third_one, [(1, 2)]), handed(first_two, [(3, 0)])
+    early = call(early_rows_kernel, [direct, reach, norm_gain, first], [rows])
+    early_far = moved(early, [(0, 3), (1, 0)])
+    far1 = moved(early, [(1, 2)])
+    both, second = lax.optimization_barrier((both, second))
     rows3 = call(fourth_rows_kernel, [total_map, total_add, both, norm_gain, second], [rows])
-    far3 = moved(rows3, [(2, 1)])
+    far3 = moved(rows3, [(2, 0)])
+    rows2 = call(third_rows_kernel, [both, norm_gain, out1], [rows])
+    far2 = moved(rows2, [(1, 0)])
     own_three, next_three = call(
         near_columns_kernel,
-        [direct, reach, norm_gain, second, rows0, rows1, rows3, own, left, right],
+        [direct, reach, norm_gain, second, early, rows3, own, left, right],
         [three, three],
         [rows],
     )
-    far_one = call(far_columns_kernel, [far1, far3, left, right], [one])
+    early_two = call(early_columns_kernel, [early_far, own, left], [two])
+    far_one = call(far_columns_kernel, [far1, far3, own, right], [one])
+    far_one, far2 = lax.optimization_barrier((far_one, far2))
+    third_one = call(third_columns_kernel, [far2, own], [one])
     return call(
         assemble_kernel,
         [
             handed(own_three, [(0, 0), (1, 1), (2, 2)]),
             handed(next_three, [(2, 3)]),
-            third_one,
-            first_two,
-            handed(far_one, [(2, 1), (1, 3)]),
+            handed(third_one, [(0, 2)]),
+            handed(early_two, [(3, 0), (0, 1)]),
+            handed(far_one, [(2, 1), (0, 3)]),
         ],
         [(toks, 4 * cols)],
     )[None]

time: 73.9 us -> 76.8 us (1.039)
  the two profiles are of different devices: /device:TPU:24 before, /device:TPU:0 now
where the time goes in v7:
time: 76.8 us; the launch traced here: 76.4 us
  starting transfers between devices  34.7 us (45%)
  waiting for transfers between devices  21.2 us (28%)
  Pallas kernels  20.2 us (26%)
    ppermute x10, starting transfers between devices, moved(): return lax.ppermute(value, 'ctx', pairs)  18.4 us
    ppermute x10, waiting for transfers between devices, moved(): return lax.ppermute(value, 'ctx', pairs)  18.1 us
    ppermute x5, starting transfers between devices, handed(): lax.ppermute(value, ('section', 'ctx'), [(s * count + a, (s + 1) % sectio...  16.4 us
    pallas_call x3, Pallas kernels, kernel_call(): pl.pallas_call(kernel, in_specs=[pl.BlockSpec(memory_space=space)] * len(...  15.8 us
    ppermute x5, waiting for transfers between devices, handed(): lax.ppermute(value, ('section', 'ctx'), [(s * count + a, (s + 1) % sectio...  3.09 us
    pallas_call x8, Pallas kernels, call(): pl.pallas_call(kernel, in_specs=[vmem] * len(operands), out_specs=[vmem]...  2.7 us
  transfers between devices with their start and end apart: 15, of which 8 were waited for; matrix products, arithmetic and copies ran while one was open for 0% of the time, Pallas kernels for 25%

profile of v7, /device:TPU:0, one launch (start us, length us, event | category | flops | bytes accessed | tf_op | source)
XLA Modules:
  0.0 76.4 jit_solution(17003904120010261710)
XLA Ops:
  0.0 1.3 %collective-permute-start.2 = (bf16[1024,512]{1,0:T(8,128)(2,1)}, bf16[1024,512]{1,0:T(8,128)(2,1)S(1)}, u32[]{:S(2)}, u32[]{:S(2)}) collective-permute-start(bf16[1024,512]{1,0:T(8,128)(2,1)} %bitcast.10), channel_id=1, source_target_pairs={{1,0},{2,1},{3,2},{5,4},{6,5},{7,6},{9,8},{10,9},{11,10},{13,12},{... | collective-permute-start | bytes 3145736 | tf_op jit(solution)/shard_map/ppermute | solution.py:489
  1.3 1.4 %shard_map.64 = (bf16[128,5120]{1,0:T(8,128)(2,1)S(1)}, bf16[4,5120]{1,0:T(4,128)(2,1)S(1)}, f32[16,128]{1,0:T(8,128)S(1)}, f32[8,128]{1,0:T(8,128)S(1)}, bf16[3,5120]{1,0:T(4,128)(2,1)S(1)}) custom-call(bf16[128,5120]{1,0:T(8,128)(2,1)} %bitcast.16, bf16[4,5120]{1,0:T(4,128)(2,1)} %bitcast.17, f32[16,128]{1,0:T(8,128)} %bitcast.18, f32[8,128]{1,0:T(8,128)} %bitcast.19), custom_call_target="tpu_custom_call" | custom-call | tf_op jit(solution)/shard_map/pallas_call | solution.py:227
  2.7 5.6 %collective-permute-start = (bf16[3,5120]{1,0:T(4,128)(2,1)S(1)}, bf16[3,5120]{1,0:T(4,128)(2,1)S(1)}, u32[]{:S(2)}, u32[]{:S(2)}) collective-permute-start(bf16[3,5120]{1,0:T(4,128)(2,1)S(1)} %get-tuple-element.31), channel_id=1, source_target_pairs={{0,1},{1,2},{2,3},{4,5},{5,6},{6,7},{8,9},{9,10},{10,11},{12,13},{... | collective-permute-start | bytes 92168 | tf_op jit(solution)/shard_map/ppermute | solution.py:489
  8.3 1.4 %shard_map.65.act_ref = f32[64,5120]{1,0:T(8,128)S(1)} custom-call(bf16[128,5120]{1,0:T(8,128)(2,1)S(1)} %get-tuple-element.32.x_ref, bf16[4,5120]{1,0:T(4,128)(2,1)S(1)} %get-tuple-element.33.taps_ref), custom_call_target="tpu_custom_call" | custom-call | flops 1048576 | bytes 65536 | tf_op jit(solution)/shard_map/pallas_call | solution.py:213
  9.9 0.7 collective-permute-start.5
  10.6 6.5 %shard_map.66 = (f32[8,128,128]{2,1,0:T(8,128)S(1)}, f32[8,128,128]{2,1,0:T(8,128)S(1)}, f32[64,1024]{1,0:T(8,128)S(1)}, f32[64,1024]{1,0:T(8,128)S(1)}) custom-call(f32[64,5120]{1,0:T(8,128)S(1)} %shard_map.65.act_ref, f32[16,128]{1,0:T(8,128)S(1)} %get-tuple-element.35.beta_ref, f32[8,128]{1,0:T(8,128)S(1)} %get-tuple-element.36.gate_ref), custom_call_target="tpu_custom_call" | custom-call | flops 1048576 | bytes 65536 | tf_op jit(solution)/shard_map/pallas_call | solution.py:213
  17.1 7.9 %shard_map.67 = (f32[8,128,128]{2,1,0:T(8,128)S(1)}, f32[8,128,128]{2,1,0:T(8,128)S(1)}, bf16[8,128,128]{2,1,0:T(8,128)(2,1)S(1)}, f32[128,1024]{1,0:T(8,128)S(1...) custom-call(bf16[3,5120]{1,0:T(4,128)(2,1)S(1)} %collective-permute-done.rim_ref, ...), custom_call_target="tpu_custom_call" | custom-call | flops 1048576 | bytes 65536 | tf_op jit(solution)/shard_map/pallas_call | solution.py:213
  25.0 3.2 %collective-permute-done.2.right_ref = bf16[1024,512]{1,0:T(8,128)(2,1)S(1)} collective-permute-done((bf16[1024,512]{1,0:T(8,128)(2,1)}, bf16[1024,512]{1,0:T(8,128)(2,1)S(1)}, u32[]{:S(2)}, u32[]{:S(2)}) %collective-permute-start.2) | collective-permute-done | bytes 1048608 | tf_op jit(solution)/shard_map/ppermute | solution.py:489
  28.3 4.3 %collective-permute-start.3 = (bf16[8,128,128]{2,1,0:T(8,128)(2,1)S(1)}, bf16[8,128,128]{2,1,0:T(8,128)(2,1)S(1)}, u32[]{:S(2)}, u32[]{:S(2)}) collective-permute-start(bf16[8,128,128]{2,1,0:T(8,128)(2,1)S(1)} %get-tuple-element.48), channel_id=1, source_target_pairs={{0,1},{4,5},{8,9},{12,13},{16,17},{20,21},{24,25},{28,29}} | collective-permute-start | bytes 786440 | tf_op jit(solution)/shard_map/ppermute | solution.py:489
  32.6 0.7 collective-permute-start.1
  33.3 3.4 %collective-permute-done.3.state_ref = bf16[8,128,128]{2,1,0:T(8,128)(2,1)S(1)} collective-permute-done((bf16[8,128,128]{2,1,0:T(8,128)(2,1)S(1)}, bf16[8,128,128]{2,1,0:T(8,128)(2,1)S(1)}, u32[]{:S(2)}, u32[]{:S(2)}) %collective-permute-start.3) | collective-permute-done | bytes 262176 | tf_op jit(solution)/shard_map/ppermute | solution.py:489
  37.9 1.9 %collective-permute-start.12 = (bf16[128,1024]{1,0:T(8,128)(2,1)S(1)}, bf16[128,1024]{1,0:T(8,128)(2,1)S(1)}, u32[]{:S(2)}, u32[]{:S(2)}) collective-permute-start(bf16[128,1024]{1,0:T(8,128)(2,1)S(1)} %shard_map.69.early_ref), channel_id=1, source_target_pairs={{0,3},{1,0},{4,7},{5,4},{8,11},{9,8},{12,15},{13,12},{16,19},{17,1... | collective-permute-start | bytes 786440 | tf_op jit(solution)/shard_map/ppermute | solution.py:489
  40.7 1.3 %collective-permute-start.9 = (bf16[128,1024]{1,0:T(8,128)(2,1)S(1)}, bf16[128,1024]{1,0:T(8,128)(2,1)S(1)}, u32[]{:S(2)}, u32[]{:S(2)}) collective-permute-start(bf16[128,1024]{1,0:T(8,128)(2,1)S(1)} %shard_map.70.rows3_ref), channel_id=1, source_target_pairs={{2,0},{6,4},{10,8},{14,12},{18,16},{22,20},{26,24},{30,28}} | collective-permute-start | bytes 786440 | tf_op jit(solution)/shard_map/ppermute | solution.py:489
  42.1 1.3 %collective-permute-start.10 = (bf16[128,1024]{1,0:T(8,128)(2,1)S(1)}, bf16[128,1024]{1,0:T(8,128)(2,1)S(1)}, u32[]{:S(2)}, u32[]{:S(2)}) collective-permute-start(bf16[128,1024]{1,0:T(8,128)(2,1)S(1)} %shard_map.73), channel_id=1, source_target_pairs={{1,0},{5,4},{9,8},{13,12},{17,16},{21,20},{25,24},{29,28}} | collective-permute-start | bytes 786440 | tf_op jit(solution)/shard_map/ppermute | solution.py:489
  43.8 1.9 %collective-permute-start.6 = (bf16[128,1536]{1,0:T(8,128)(2,1)S(1)}, bf16[128,1536]{1,0:T(8,128)(2,1)S(1)}, u32[]{:S(2)}, u32[]{:S(2)}) collective-permute-start(bf16[128,1536]{1,0:T(8,128)(2,1)S(1)} %get-tuple-element.53), channel_id=1, source_target_pairs={{0,4},{1,5},{2,6},{4,8},{5,9},{6,10},{8,12},{9,13},{10,14},{12,16}... | collective-permute-start | bytes 1179656 | tf_op jit(solution)/shard_map/ppermute | solution.py:494
  45.8 1.0 %collective-permute-done.12.rows_ref = bf16[128,1024]{1,0:T(8,128)(2,1)S(1)} collective-permute-done((bf16[128,1024]{1,0:T(8,128)(2,1)S(1)}, bf16[128,1024]{1,0:T(8,128)(2,1)S(1)}, u32[]{:S(2)}, u32[]{:S(2)}) %collective-permute-start.12) | collective-permute-done | bytes 262176 | tf_op jit(solution)/shard_map/ppermute | solution.py:489
  47.8 11.2 %collective-permute-start.13 = (bf16[128,1024]{1,0:T(8,128)(2,1)S(1)}, bf16[128,1024]{1,0:T(8,128)(2,1)S(1)}, u32[]{:S(2)}, u32[]{:S(2)}) collective-permute-start(bf16[128,1024]{1,0:T(8,128)(2,1)S(1)} %shard_map.75), channel_id=1, source_target_pairs={{3,4},{0,5},{7,8},{4,9},{11,12},{8,13},{15,16},{12,17},{19,20},{16... | collective-permute-start | bytes 786440 | tf_op jit(solution)/shard_map/ppermute | solution.py:494
  59.0 7.4 %collective-permute-done.9.rows3_ref = bf16[128,1024]{1,0:T(8,128)(2,1)S(1)} collective-permute-done((bf16[128,1024]{1,0:T(8,128)(2,1)S(1)}, bf16[128,1024]{1,0:T(8,128)(2,1)S(1)}, u32[]{:S(2)}, u32[]{:S(2)}) %collective-permute-start.9) | collective-permute-done | bytes 262176 | tf_op jit(solution)/shard_map/ppermute | solution.py:489
  66.8 2.7 %collective-permute-done.10.rows_ref = bf16[128,1024]{1,0:T(8,128)(2,1)S(1)} collective-permute-done((bf16[128,1024]{1,0:T(8,128)(2,1)S(1)}, bf16[128,1024]{1,0:T(8,128)(2,1)S(1)}, u32[]{:S(2)}, u32[]{:S(2)}) %collective-permute-start.10) | collective-permute-done | bytes 262176 | tf_op jit(solution)/shard_map/ppermute | solution.py:489
  69.8 1.3 %collective-permute-start.11 = (bf16[128,512]{1,0:T(8,128)(2,1)S(1)}, bf16[128,512]{1,0:T(8,128)(2,1)S(1)}, u32[]{:S(2)}, u32[]{:S(2)}) collective-permute-start(bf16[128,512]{1,0:T(8,128)(2,1)S(1)} %shard_map.74), channel_id=1, source_target_pairs={{0,6},{4,10},{8,14},{12,18},{16,22},{20,26},{24,30},{28,2}} | collective-permute-start | bytes 393224 | tf_op jit(solution)/shard_map/ppermute | solution.py:494
  71.1 1.3 %collective-permute-start.14 = (bf16[128,512]{1,0:T(8,128)(2,1)S(1)}, bf16[128,512]{1,0:T(8,128)(2,1)S(1)}, u32[]{:S(2)}, u32[]{:S(2)}) collective-permute-start(bf16[128,512]{1,0:T(8,128)(2,1)S(1)} %shard_map.72), channel_id=1, source_target_pairs={{2,5},{0,7},{6,9},{4,11},{10,13},{8,15},{14,17},{12,19},{18,21},{1... | collective-permute-start | bytes 393224 | tf_op jit(solution)/shard_map/ppermute | solution.py:494
  72.5 1.7 %collective-permute-done.11.third_one = bf16[128,512]{1,0:T(8,128)(2,1)S(1)} collective-permute-done((bf16[128,512]{1,0:T(8,128)(2,1)S(1)}, bf16[128,512]{1,0:T(8,128)(2,1)S(1)}, u32[]{:S(2)}, u32[]{:S(2)}) %collective-permute-start.11) | collective-permute-done | bytes 131104 | tf_op jit(solution)/shard_map/ppermute | solution.py:494
  74.1 1.4 %collective-permute-done.14.far_one = bf16[128,512]{1,0:T(8,128)(2,1)S(1)} collective-permute-done((bf16[128,512]{1,0:T(8,128)(2,1)S(1)}, bf16[128,512]{1,0:T(8,128)(2,1)S(1)}, u32[]{:S(2)}, u32[]{:S(2)}) %collective-permute-start.14) | collective-permute-done | bytes 131104 | tf_op jit(solution)/shard_map/ppermute | solution.py:494
  75.5 0.8 %shard_map.76 = bf16[128,2048]{1,0:T(8,128)(2,1)} custom-call(bf16[128,1536]{1,0:T(8,128)(2,1)S(1)} %collective-permute-done.6.own_three, bf16[128,1536]{1,0:T(8,128)(2,1)S(1)} %collective-permute-done.7.next_three, bf16[128,512]{1,0:T(8,128)(2,1)S(1)} %collective-permute-done.11.third_one, bf16[128,1024]{1,0:T(8,128)(2,1)S(1)} %collective-permute-done.13.early_two, ...), custom_call_target="tpu_custom_call" | custom-call | flops 1048576 | bytes 65536 | tf_op jit(solution)/shard_map/pallas_call | solution.py:457
  (23 shorter events, 4.4 us)
Async XLA Ops:
  0.0 28.3 %collective-permute-start.2 = (bf16[1024,512]{1,0:T(8,128)(2,1)}, bf16[1024,512]{1,0:T(8,128)(2,1)S(1)}, u32[]{:S(2)}, u32[]{:S(2)}) collective-permute-start(bf16[1024,512]{1,0:T(8,128)(2,1)} %bitcast.10), channel_id=1, source_target_pairs={{1,0},{2,1},{3,2},{5,4},{6,5},{7,6},{9,8},{10,9},{11,10},{13,12},{... | collective-permute-start | bytes 3145736 | tf_op jit(solution)/shard_map/ppermute | solution.py:489
  2.7 7.2 %collective-permute-start = (bf16[3,5120]{1,0:T(4,128)(2,1)S(1)}, bf16[3,5120]{1,0:T(4,128)(2,1)S(1)}, u32[]{:S(2)}, u32[]{:S(2)}) collective-permute-start(bf16[3,5120]{1,0:T(4,128)(2,1)S(1)} %get-tuple-element.31), channel_id=1, source_target_pairs={{0,1},{1,2},{2,3},{4,5},{5,6},{6,7},{8,9},{9,10},{10,11},{12,13},{... | collective-permute-start | bytes 92168 | tf_op jit(solution)/shard_map/ppermute | solution.py:489
  8.2 1.7 %copy-start = (bf16[1,1024,512]{2,1,0:T(8,128)(2,1)S(1)}, bf16[1,1024,512]{2,1,0:T(8,128)(2,1)}, u32[]{:S(2)}) copy-start(bf16[1,1024,512]{2,1,0:T(8,128)(2,1)} %param.11) | copy-start | bytes 3145732
  9.9 33.5 %collective-permute-start.5 = (bf16[1024,512]{1,0:T(8,128)(2,1)S(1)}, bf16[1024,512]{1,0:T(8,128)(2,1)S(1)}, u32[]{:S(2)}, u32[]{:S(2)}) collective-permute-start(bf16[1024,512]{1,0:T(8,128)(2,1)S(1)} %bitcast.11), channel_id=1, source_target_pairs={{1,2},{2,3},{5,6},{6,7},{9,10},{10,11},{13,14},{14,15},{17,18},{18... | collective-permute-start | bytes 3145736 | tf_op jit(solution)/shard_map/ppermute | solution.py:489
  25.0 12.6 %copy-start.1 = (f32[1,1024]{1,0:T(1,128)S(1)}, f32[1,1024]{1,0:T(1,128)}, u32[]{:S(2)}) copy-start(f32[1,1024]{1,0:T(1,128)} %gain_ref.7) | copy-start | bytes 12292
  28.3 8.4 %collective-permute-start.3 = (bf16[8,128,128]{2,1,0:T(8,128)(2,1)S(1)}, bf16[8,128,128]{2,1,0:T(8,128)(2,1)S(1)}, u32[]{:S(2)}, u32[]{:S(2)}) collective-permute-start(bf16[8,128,128]{2,1,0:T(8,128)(2,1)S(1)} %get-tuple-element.48), channel_id=1, source_target_pairs={{0,1},{4,5},{8,9},{12,13},{16,17},{20,21},{24,25},{28,29}} | collective-permute-start | bytes 786440 | tf_op jit(solution)/shard_map/ppermute | solution.py:489
  32.6 8.0 %collective-permute-start.1 = (bf16[2,128,1024]{2,1,0:T(8,128)(2,1)S(1)}, bf16[2,128,1024]{2,1,0:T(8,128)(2,1)S(1)}, u32[]{:S(2)}, u32[]{:S(2)}) collective-permute-start(bf16[2,128,1024]{2,1,0:T(8,128)(2,1)S(1)} %get-tuple-element.44), channel_id=1, source_target_pairs={{3,2},{2,1},{7,6},{6,5},{11,10},{10,9},{15,14},{14,13},{19,18},{18... | collective-permute-start | bytes 1572872 | tf_op jit(solution)/shard_map/ppermute | solution.py:489
  37.0 3.6 %collective-permute-start.4 = (bf16[8,128,128]{2,1,0:T(8,128)(2,1)S(1)}, bf16[8,128,128]{2,1,0:T(8,128)(2,1)S(1)}, u32[]{:S(2)}, u32[]{:S(2)}) collective-permute-start(bf16[8,128,128]{2,1,0:T(8,128)(2,1)S(1)} %shard_map.68.state_ref), channel_id=1, source_target_pairs={{1,2},{5,6},{9,10},{13,14},{17,18},{21,22},{25,26},{29,30}} | collective-permute-start | bytes 786440 | tf_op jit(solution)/shard_map/ppermute | solution.py:489
  37.9 8.9 %collective-permute-start.12 = (bf16[128,1024]{1,0:T(8,128)(2,1)S(1)}, bf16[128,1024]{1,0:T(8,128)(2,1)S(1)}, u32[]{:S(2)}, u32[]{:S(2)}) collective-permute-start(bf16[128,1024]{1,0:T(8,128)(2,1)S(1)} %shard_map.69.early_ref), channel_id=1, source_target_pairs={{0,3},{1,0},{4,7},{5,4},{8,11},{9,8},{12,15},{13,12},{16,19},{17,1... | collective-permute-start | bytes 786440 | tf_op jit(solution)/shard_map/ppermute | solution.py:489
  39.8 8.0 %collective-permute-start.8 = (bf16[128,1024]{1,0:T(8,128)(2,1)S(1)}, bf16[128,1024]{1,0:T(8,128)(2,1)S(1)}, u32[]{:S(2)}, u32[]{:S(2)}) collective-permute-start(bf16[128,1024]{1,0:T(8,128)(2,1)S(1)} %shard_map.69.early_ref), channel_id=1, source_target_pairs={{1,2},{5,6},{9,10},{13,14},{17,18},{21,22},{25,26},{29,30}} | collective-permute-start | bytes 786440 | tf_op jit(solution)/shard_map/ppermute | solution.py:489
  40.7 25.7 %collective-permute-start.9 = (bf16[128,1024]{1,0:T(8,128)(2,1)S(1)}, bf16[128,1024]{1,0:T(8,128)(2,1)S(1)}, u32[]{:S(2)}, u32[]{:S(2)}) collective-permute-start(bf16[128,1024]{1,0:T(8,128)(2,1)S(1)} %shard_map.70.rows3_ref), channel_id=1, source_target_pairs={{2,0},{6,4},{10,8},{14,12},{18,16},{22,20},{26,24},{30,28}} | collective-permute-start | bytes 786440 | tf_op jit(solution)/shard_map/ppermute | solution.py:489
  42.1 27.4 %collective-permute-start.10 = (bf16[128,1024]{1,0:T(8,128)(2,1)S(1)}, bf16[128,1024]{1,0:T(8,128)(2,1)S(1)}, u32[]{:S(2)}, u32[]{:S(2)}) collective-permute-start(bf16[128,1024]{1,0:T(8,128)(2,1)S(1)} %shard_map.73), channel_id=1, source_target_pairs={{1,0},{5,4},{9,8},{13,12},{17,16},{21,20},{25,24},{29,28}} | collective-permute-start | bytes 786440 | tf_op jit(solution)/shard_map/ppermute | solution.py:489
  43.8 28.6 %collective-permute-start.6 = (bf16[128,1536]{1,0:T(8,128)(2,1)S(1)}, bf16[128,1536]{1,0:T(8,128)(2,1)S(1)}, u32[]{:S(2)}, u32[]{:S(2)}) collective-permute-start(bf16[128,1536]{1,0:T(8,128)(2,1)S(1)} %get-tuple-element.53), channel_id=1, source_target_pairs={{0,4},{1,5},{2,6},{4,8},{5,9},{6,10},{8,12},{9,13},{10,14},{12,16}... | collective-permute-start | bytes 1179656 | tf_op jit(solution)/shard_map/ppermute | solution.py:494
  46.8 25.6 %collective-permute-start.7 = (bf16[128,1536]{1,0:T(8,128)(2,1)S(1)}, bf16[128,1536]{1,0:T(8,128)(2,1)S(1)}, u32[]{:S(2)}, u32[]{:S(2)}) collective-permute-start(bf16[128,1536]{1,0:T(8,128)(2,1)S(1)} %get-tuple-element.54), channel_id=1, source_target_pairs={{2,7},{6,11},{10,15},{14,19},{18,23},{22,27},{26,31},{30,3}} | collective-permute-start | bytes 1179656 | tf_op jit(solution)/shard_map/ppermute | solution.py:494
  47.8 24.6 %collective-permute-start.13 = (bf16[128,1024]{1,0:T(8,128)(2,1)S(1)}, bf16[128,1024]{1,0:T(8,128)(2,1)S(1)}, u32[]{:S(2)}, u32[]{:S(2)}) collective-permute-start(bf16[128,1024]{1,0:T(8,128)(2,1)S(1)} %shard_map.75), channel_id=1, source_target_pairs={{3,4},{0,5},{7,8},{4,9},{11,12},{8,13},{15,16},{12,17},{19,20},{16... | collective-permute-start | bytes 786440 | tf_op jit(solution)/shard_map/ppermute | solution.py:494
  69.8 4.3 %collective-permute-start.11 = (bf16[128,512]{1,0:T(8,128)(2,1)S(1)}, bf16[128,512]{1,0:T(8,128)(2,1)S(1)}, u32[]{:S(2)}, u32[]{:S(2)}) collective-permute-start(bf16[128,512]{1,0:T(8,128)(2,1)S(1)} %shard_map.74), channel_id=1, source_target_pairs={{0,6},{4,10},{8,14},{12,18},{16,22},{20,26},{24,30},{28,2}} | collective-permute-start | bytes 393224 | tf_op jit(solution)/shard_map/ppermute | solution.py:494
  71.1 4.4 %collective-permute-start.14 = (bf16[128,512]{1,0:T(8,128)(2,1)S(1)}, bf16[128,512]{1,0:T(8,128)(2,1)S(1)}, u32[]{:S(2)}, u32[]{:S(2)}) collective-permute-start(bf16[128,512]{1,0:T(8,128)(2,1)S(1)} %shard_map.72), channel_id=1, source_target_pairs={{2,5},{0,7},{6,9},{4,11},{10,13},{8,15},{14,17},{12,19},{18,21},{1... | collective-permute-start | bytes 393224 | tf_op jit(solution)/shard_map/ppermute | solution.py:494

commit v8 on v6

--- a/solution.py
+++ b/solution.py
@@ -9,7 +9,7 @@
 HK = 128
 STEPS = 2
 CONV = 4
-LEVELS = (1, 2, 4, 8, 16, 32)
+LEVELS = 6
 f32, bf16 = jnp.float32, jnp.bfloat16
 
 
@@ -41,16 +41,11 @@
     return pair_rows(x[:, :HK], x[:, HK:])
 
 
-def pick(table, lane):
-    index = lax.broadcasted_iota(jnp.int32, table.shape, 1)
-    return jnp.sum(jnp.where(index == lane, table, 0.0), axis=1, keepdims=True)
-
-
 def half_terms(u, heads, half, acts, beta_t, gate_t):
     size, toks = STEPS * half, 2 * half
     virt = lax.broadcasted_iota(jnp.int32, (size, toks), 0)
-    tok = lax.broadcasted_iota(jnp.int32, (size, toks), 1)
-    inside = ((tok >= u * half) & (tok - u * half <= virt % half)).astype(f32)
+    tok = lax.broadcasted_iota(jnp.int32, (size, toks), 1) - u * half
+    inside = ((tok >= 0) & (tok <= (virt & (half - 1)))).astype(f32)
     exact = dict(precision=lax.Precision.HIGHEST, preferred_element_type=f32)
     over_lanes = (((1,), (1,)), ((), ()))
     sums = lax.dot_general(inside, gate_t, over_lanes, **exact)
@@ -59,20 +54,15 @@
 
     row = lax.broadcasted_iota(jnp.int32, (size, size), 0)
     col = lax.broadcasted_iota(jnp.int32, (size, size), 1)
-    row_tok, col_tok = row % half, col % half
-    strict = (col_tok < row_tok) | ((col_tok == row_tok) & (col < row))
+    row_tok, col_tok = row & (half - 1), col & (half - 1)
+    apart = row_tok ^ col_tok
+    strict = (col_tok < row_tok) | ((apart == 0) & (col < row))
     upto = (col_tok <= row_tok)[:half]
     eye = (row == col).astype(f32)
-    same = row_tok == col_tok
     twice = lambda x: jnp.concatenate([x, x], axis=1)
-    level_masks = [
-        twice(
-            ((row_tok // (2 * b)) == (col_tok // (2 * b)))
-            & ((row_tok // b) % 2 == 1)
-            & ((col_tok // b) % 2 == 0)
-        )
-        for b in LEVELS
-    ]
+    same = twice(apart == 0)
+    before = twice(jnp.where(col_tok < row_tok, apart, 0))
+    level_masks = [(before >> level) == 1 for level in range(LEVELS)]
 
     work = []
     for head in range(heads):
@@ -81,8 +71,10 @@
         queries = unit(acts[0][:, lanes])
         keys = unit(jnp.concatenate([acts[1][:, lanes], acts[2][:, lanes]], axis=0))
         vals = jnp.concatenate([acts[3][:, lanes], acts[4][:, lanes]], axis=0)
-        size_col = jnp.concatenate([pick(steps, head), pick(steps, heads + head)], axis=0)
-        c_col = pick(sums, head)
+        size_col = jnp.concatenate(
+            [steps[:, head : head + 1], steps[:, heads + head : heads + head + 1]], axis=0
+        )
+        c_col = sums[:, head : head + 1]
         c_row = sums_t[head : head + 1]
         c_end = c_col[half - 1 : half]
         keys_t = keys.T
@@ -103,7 +95,7 @@
     for i in pairs:
         low = jnp.concatenate([work[2 * i][0], work[2 * i + 1][0]], axis=1)
         lows.append(low.astype(bf16))
-        invs.append((twice(eye) - jnp.where(twice(same), low, 0.0)).astype(bf16))
+        invs.append((twice(eye) - jnp.where(same, low, 0.0)).astype(bf16))
     for mask in level_masks:
         inner = [
             dot(jnp.where(mask, lows[i], jnp.zeros_like(lows[i])), blockwise(invs[i])).astype(bf16)
@@ -396,12 +388,16 @@
         rows_with_state(direct_ref, reach_ref, gain_ref, state_ref, out_ref)
 
 
-def third_columns_kernel(both_ref, gain_ref, state_ref, left_a, left_b, out_ref, rows_ref):
+def middle_columns_kernel(both_ref, gain_ref, state_ref, rows1_ref, left_a, left_b, right_ref, out_ref, rows_ref):
     @on_shard(1)
     def _():
         for head, lanes in head_lanes(state_ref.shape[0]):
             rows_ref[:, lanes] = rows_of_next(both_ref, gain_ref, head, lanes, state_ref[head])
         project_to(out_ref, rows_ref[...], (left_a, left_b))
+
+    @on_shard(2)
+    def _():
+        project_to(out_ref, rows1_ref[...], right_ref)
 
 
 def fourth_rows_kernel(map_ref, add_ref, both_ref, gain_ref, state_ref, out_ref):
@@ -441,14 +437,10 @@
         project_to(out_ref, rows_ref[...], left_ref, own_ref)
 
 
-def far_columns_kernel(rows1_ref, rows3_ref, left_a, left_b, right_ref, out_ref):
+def last_columns_kernel(rows3_ref, left_a, left_b, out_ref):
     @on_shard(1)
     def _():
         project_to(out_ref, rows3_ref[...], (left_a, left_b))
-
-    @on_shard(2)
-    def _():
-        project_to(out_ref, rows1_ref[...], right_ref)
 
 
 def call(kernel, operands, out_shapes, scratch=()):
@@ -466,15 +458,15 @@
     return found if len(shapes) > 1 else found[0]
 
 
-def assemble_kernel(own_three, next_three, third_one, first_two, far_one, out_ref):
-    cols = far_one.shape[1]
+def assemble_kernel(own_three, next_three, middle_one, first_two, last_one, out_ref):
+    cols = last_one.shape[1]
     own = [(own_three, index) for index in range(3)]
     after = [(next_three, index) for index in range(3)]
     sources = (
         (own[0], own[1], (first_two, 0), (first_two, 1)),
-        (own[2], own[0], own[1], (far_one, 0)),
-        ((third_one, 0), own[2], own[0], own[1]),
-        ((far_one, 0), after[2], after[0], after[1]),
+        (own[2], own[0], own[1], (middle_one, 0)),
+        ((middle_one, 0), own[2], own[0], own[1]),
+        ((last_one, 0), after[2], after[0], after[1]),
     )
     for place, blocks in enumerate(sources):
 
@@ -543,7 +535,6 @@
     rows0 = call(first_rows_kernel, [direct, norm_gain], [rows])
     far0 = moved(rows0, [(0, 3)])
     rows1 = call(second_rows_kernel, [direct, reach, norm_gain, first], [rows])
-    rows1, rest = lax.optimization_barrier((rows1, rest))
     far1 = moved(rows1, [(1, 2)])
     rest = moved(rest, [(0, 1)])
     both, second = lax.optimization_barrier((both, second))
@@ -555,18 +546,20 @@
         [three, three],
         [rows],
     )
-    third_one = call(third_columns_kernel, [both, norm_gain, out1, top, rest], [one], [rows])
+    middle_one = call(
+        middle_columns_kernel, [both, norm_gain, out1, far1, top, rest, right], [one], [rows]
+    )
     first_two = call(first_columns_kernel, [far0, whole, left], [two])
-    far_one = call(far_columns_kernel, [far1, far3, top, rest, right], [one])
-    far_one, third_one = lax.optimization_barrier((far_one, third_one))
+    far3, middle_one = lax.optimization_barrier((far3, middle_one))
+    last_one = call(last_columns_kernel, [far3, top, rest], [one])
     return call(
         assemble_kernel,
         [
             handed(own_three, [(0, 0), (1, 1), (2, 2)]),
             handed(next_three, [(2, 3)]),
-            handed(third_one, [(1, 2)]),
+            handed(middle_one, [(1, 2), (2, 1)]),
             handed(first_two, [(3, 0)]),
-            handed(far_one, [(2, 1), (1, 3)]),
+            handed(last_one, [(1, 3)]),
         ],
         [(toks, 4 * cols)],
     )[None]

time: 72.7 us -> 71.9 us (0.989)
  the two profiles are of different devices: /device:TPU:8 before, /device:TPU:24 now
where the time goes in v8:
time: 71.9 us; the launch traced here: 71.5 us
  waiting for transfers between devices  31.3 us (44%)
  starting transfers between devices  21.2 us (29%)
  Pallas kernels  18.6 us (26%)
    ppermute x11, waiting for transfers between devices, moved(): return lax.ppermute(value, 'ctx', pairs)  18.6 us
    pallas_call x3, Pallas kernels, kernel_call(): pl.pallas_call(kernel, in_specs=[pl.BlockSpec(memory_space=space)] * len(...  15.4 us
    ppermute x11, starting transfers between devices, moved(): return lax.ppermute(value, 'ctx', pairs)  15.1 us
    ppermute x5, waiting for transfers between devices, handed(): lax.ppermute(value, ('section', 'ctx'), [(s * count + a, (s + 1) % sectio...  12.7 us
    ppermute x5, starting transfers between devices, handed(): lax.ppermute(value, ('section', 'ctx'), [(s * count + a, (s + 1) % sectio...  6.18 us
    pallas_call x8, Pallas kernels, call(): pl.pallas_call(kernel, in_specs=[vmem] * len(operands), out_specs=[vmem]...  1.55 us
  transfers between devices with their start and end apart: 16, of which 6 were waited for; matrix products, arithmetic and copies ran while one was open for 0% of the time, Pallas kernels for 25%

profile of v8, /device:TPU:24, one launch (start us, length us, event | category | flops | bytes accessed | tf_op | source)
XLA Modules:
  0.0 71.5 jit_solution(7892243903855006172)
XLA Ops:
  0.0 2.5 %collective-permute-start.3 = (bf16[1024,512]{1,0:T(8,128)(2,1)}, bf16[1024,512]{1,0:T(8,128)(2,1)S(1)}, u32[]{:S(2)}, u32[]{:S(2)}) collective-permute-start(bf16[1024,512]{1,0:T(8,128)(2,1)} %bitcast.14), channel_id=1, source_target_pairs={{1,0},{2,1},{3,2},{5,4},{6,5},{7,6},{9,8},{10,9},{11,10},{13,12},{... | collective-permute-start | bytes 3145736 | tf_op jit(solution)/shard_map/ppermute | solution.py:480
  2.5 1.4 %shard_map.64 = (bf16[128,5120]{1,0:T(8,128)(2,1)S(1)}, bf16[4,5120]{1,0:T(4,128)(2,1)S(1)}, f32[16,128]{1,0:T(8,128)S(1)}, f32[8,128]{1,0:T(8,128)S(1)}, bf16[3,5120]{1,0:T(4,128)(2,1)S(1)}) custom-call(bf16[128,5120]{1,0:T(8,128)(2,1)} %bitcast.18, bf16[4,5120]{1,0:T(4,128)(2,1)} %bitcast.19, f32[16,128]{1,0:T(8,128)} %bitcast.20, f32[8,128]{1,0:T(8,128)} %bitcast.21), custom_call_target="tpu_custom_call" | custom-call | tf_op jit(solution)/shard_map/pallas_call | solution.py:219
  3.9 1.3 %collective-permute-start = (bf16[3,5120]{1,0:T(4,128)(2,1)S(1)}, bf16[3,5120]{1,0:T(4,128)(2,1)S(1)}, u32[]{:S(2)}, u32[]{:S(2)}) collective-permute-start(bf16[3,5120]{1,0:T(4,128)(2,1)S(1)} %get-tuple-element.33), channel_id=1, source_target_pairs={{0,1},{1,2},{2,3},{4,5},{5,6},{6,7},{8,9},{9,10},{10,11},{12,13},{... | collective-permute-start | bytes 92168 | tf_op jit(solution)/shard_map/ppermute | solution.py:480
  5.3 1.4 %shard_map.65.act_ref = f32[64,5120]{1,0:T(8,128)S(1)} custom-call(bf16[128,5120]{1,0:T(8,128)(2,1)S(1)} %get-tuple-element.34.x_ref, bf16[4,5120]{1,0:T(4,128)(2,1)S(1)} %get-tuple-element.35.taps_ref), custom_call_target="tpu_custom_call" | custom-call | flops 1048576 | bytes 65536 | tf_op jit(solution)/shard_map/pallas_call | solution.py:205
  6.8 3.1 %collective-permute-done.rim_ref = bf16[3,5120]{1,0:T(4,128)(2,1)S(1)} collective-permute-done((bf16[3,5120]{1,0:T(4,128)(2,1)S(1)}, bf16[3,5120]{1,0:T(4,128)(2,1)S(1)}, u32[]{:S(2)}, u32[]{:S(2)}) %collective-permute-start) | collective-permute-done | bytes 30752 | tf_op jit(solution)/shard_map/ppermute | solution.py:480
  9.8 0.7 collective-permute-start.2
  10.5 1.3 %collective-permute-start.6 = (bf16[1024,512]{1,0:T(8,128)(2,1)S(1)}, bf16[1024,512]{1,0:T(8,128)(2,1)S(1)}, u32[]{:S(2)}, u32[]{:S(2)}) collective-permute-start(bf16[1024,512]{1,0:T(8,128)(2,1)S(1)} %bitcast.15), channel_id=1, source_target_pairs={{1,2},{2,3},{5,6},{6,7},{9,10},{10,11},{13,14},{14,15},{17,18},{18... | collective-permute-start | bytes 3145736 | tf_op jit(solution)/shard_map/ppermute | solution.py:480
  11.8 6.3 %shard_map.66 = (f32[8,128,128]{2,1,0:T(8,128)S(1)}, f32[8,128,128]{2,1,0:T(8,128)S(1)}, f32[64,1024]{1,0:T(8,128)S(1)}, f32[64,1024]{1,0:T(8,128)S(1)}) custom-call(f32[64,5120]{1,0:T(8,128)S(1)} %shard_map.65.act_ref, f32[16,128]{1,0:T(8,128)S(1)} %get-tuple-element.37.beta_ref, f32[8,128]{1,0:T(8,128)S(1)} %get-tuple-element.38.gate_ref), custom_call_target="tpu_custom_call" | custom-call | flops 1048576 | bytes 65536 | tf_op jit(solution)/shard_map/pallas_call | solution.py:205
  18.2 7.6 %shard_map.67 = (f32[8,128,128]{2,1,0:T(8,128)S(1)}, f32[8,128,128]{2,1,0:T(8,128)S(1)}, bf16[8,128,128]{2,1,0:T(8,128)(2,1)S(1)}, f32[128,1024]{1,0:T(8,128)S(1...) custom-call(bf16[3,5120]{1,0:T(4,128)(2,1)S(1)} %collective-permute-done.rim_ref, ...), custom_call_target="tpu_custom_call" | custom-call | flops 1048576 | bytes 65536 | tf_op jit(solution)/shard_map/pallas_call | solution.py:205
  25.8 0.7 collective-permute-start.4
  26.5 4.6 %collective-permute-start.1 = (bf16[2,128,1024]{2,1,0:T(8,128)(2,1)S(1)}, bf16[2,128,1024]{2,1,0:T(8,128)(2,1)S(1)}, u32[]{:S(2)}, u32[]{:S(2)}) collective-permute-start(bf16[2,128,1024]{2,1,0:T(8,128)(2,1)S(1)} %get-tuple-element.46), channel_id=1, source_target_pairs={{3,2},{2,1},{7,6},{6,5},{11,10},{10,9},{15,14},{14,13},{19,18},{18... | collective-permute-start | bytes 1572872 | tf_op jit(solution)/shard_map/ppermute | solution.py:480
  31.1 0.7 collective-permute-start.7
  32.8 1.3 %collective-permute-start.13 = (bf16[128,1024]{1,0:T(8,128)(2,1)S(1)}, bf16[128,1024]{1,0:T(8,128)(2,1)S(1)}, u32[]{:S(2)}, u32[]{:S(2)}) collective-permute-start(bf16[128,1024]{1,0:T(8,128)(2,1)S(1)} %shard_map.69.rows0_ref), channel_id=1, source_target_pairs={{0,3},{4,7},{8,11},{12,15},{16,19},{20,23},{24,27},{28,31}} | collective-permute-start | bytes 786440 | tf_op jit(solution)/shard_map/ppermute | solution.py:480
  34.1 6.4 %collective-permute-done.1.both_ref = bf16[2,128,1024]{2,1,0:T(8,128)(2,1)S(1)} collective-permute-done((bf16[2,128,1024]{2,1,0:T(8,128)(2,1)S(1)}, bf16[2,128,1024]{2,1,0:T(8,128)(2,1)S(1)}, u32[]{:S(2)}, u32[]{:S(2)}) %collective-permute-start.1) | collective-permute-done | bytes 524320 | tf_op jit(solution)/shard_map/ppermute | solution.py:480
  41.4 0.7 collective-permute-start.10
  42.2 0.7 collective-permute-start.8
  42.8 1.3 %collective-permute-start.9 = (bf16[128,1536]{1,0:T(8,128)(2,1)S(1)}, bf16[128,1536]{1,0:T(8,128)(2,1)S(1)}, u32[]{:S(2)}, u32[]{:S(2)}) collective-permute-start(bf16[128,1536]{1,0:T(8,128)(2,1)S(1)} %get-tuple-element.58), channel_id=1, source_target_pairs={{2,7},{6,11},{10,15},{14,19},{18,23},{22,27},{26,31},{30,3}} | collective-permute-start | bytes 1179656 | tf_op jit(solution)/shard_map/ppermute | solution.py:485
  44.1 9.1 %collective-permute-done.13.rows_ref = bf16[128,1024]{1,0:T(8,128)(2,1)S(1)} collective-permute-done((bf16[128,1024]{1,0:T(8,128)(2,1)S(1)}, bf16[128,1024]{1,0:T(8,128)(2,1)S(1)}, u32[]{:S(2)}, u32[]{:S(2)}) %collective-permute-start.13) | collective-permute-done | bytes 262176 | tf_op jit(solution)/shard_map/ppermute | solution.py:480
  53.7 2.2 %collective-permute-start.14 = (bf16[128,1024]{1,0:T(8,128)(2,1)S(1)}, bf16[128,1024]{1,0:T(8,128)(2,1)S(1)}, u32[]{:S(2)}, u32[]{:S(2)}) collective-permute-start(bf16[128,1024]{1,0:T(8,128)(2,1)S(1)} %shard_map.74), channel_id=1, source_target_pairs={{3,4},{7,8},{11,12},{15,16},{19,20},{23,24},{27,28},{31,0}} | collective-permute-start | bytes 786440 | tf_op jit(solution)/shard_map/ppermute | solution.py:485
  56.0 1.3 %collective-permute-start.15 = (bf16[128,512]{1,0:T(8,128)(2,1)S(1)}, bf16[128,512]{1,0:T(8,128)(2,1)S(1)}, u32[]{:S(2)}, u32[]{:S(2)}) collective-permute-start(bf16[128,512]{1,0:T(8,128)(2,1)S(1)} %shard_map.75), channel_id=1, source_target_pairs={{1,7},{5,11},{9,15},{13,19},{17,23},{21,27},{25,31},{29,3}} | collective-permute-start | bytes 393224 | tf_op jit(solution)/shard_map/ppermute | solution.py:485
  58.0 3.8 %collective-permute-done.14.first_two = bf16[128,1024]{1,0:T(8,128)(2,1)S(1)} collective-permute-done((bf16[128,1024]{1,0:T(8,128)(2,1)S(1)}, bf16[128,1024]{1,0:T(8,128)(2,1)S(1)}, u32[]{:S(2)}, u32[]{:S(2)}) %collective-permute-start.14) | collective-permute-done | bytes 262176 | tf_op jit(solution)/shard_map/ppermute | solution.py:485
  61.8 4.2 %collective-permute-done.15.last_one = bf16[128,512]{1,0:T(8,128)(2,1)S(1)} collective-permute-done((bf16[128,512]{1,0:T(8,128)(2,1)S(1)}, bf16[128,512]{1,0:T(8,128)(2,1)S(1)}, u32[]{:S(2)}, u32[]{:S(2)}) %collective-permute-start.15) | collective-permute-done | bytes 131104 | tf_op jit(solution)/shard_map/ppermute | solution.py:485
  65.9 4.7 %collective-permute-done.9.next_three = bf16[128,1536]{1,0:T(8,128)(2,1)S(1)} collective-permute-done((bf16[128,1536]{1,0:T(8,128)(2,1)S(1)}, bf16[128,1536]{1,0:T(8,128)(2,1)S(1)}, u32[]{:S(2)}, u32[]{:S(2)}) %collective-permute-start.9) | collective-permute-done | bytes 393248 | tf_op jit(solution)/shard_map/ppermute | solution.py:485
  70.7 0.8 %shard_map.76 = bf16[128,2048]{1,0:T(8,128)(2,1)} custom-call(bf16[128,1536]{1,0:T(8,128)(2,1)S(1)} %collective-permute-done.8.own_three, bf16[128,1536]{1,0:T(8,128)(2,1)S(1)} %collective-permute-done.9.next_three, bf16[128,512]{1,0:T(8,128)(2,1)S(1)} %collective-permute-done.12.middle_one, bf16[128,1024]{1,0:T(8,128)(2,1)S(1)} %collective-permute-done.14.first_two, ...), custom_call_target="tpu_custom_call" | custom-call | flops 1048576 | bytes 65536 | tf_op jit(solution)/shard_map/pallas_call | solution.py:449
  (26 shorter events, 3.1 us)
Async XLA Ops:
  0.0 5.2 %copy-start = (bf16[1,1024,512]{2,1,0:T(8,128)(2,1)S(1)}, bf16[1,1024,512]{2,1,0:T(8,128)(2,1)}, u32[]{:S(2)}) copy-start(bf16[1,1024,512]{2,1,0:T(8,128)(2,1)} %param.11) | copy-start | bytes 3145732
  0.0 25.8 %collective-permute-start.3 = (bf16[1024,512]{1,0:T(8,128)(2,1)}, bf16[1024,512]{1,0:T(8,128)(2,1)S(1)}, u32[]{:S(2)}, u32[]{:S(2)}) collective-permute-start(bf16[1024,512]{1,0:T(8,128)(2,1)} %bitcast.14), channel_id=1, source_target_pairs={{1,0},{2,1},{3,2},{5,4},{6,5},{7,6},{9,8},{10,9},{11,10},{13,12},{... | collective-permute-start | bytes 3145736 | tf_op jit(solution)/shard_map/ppermute | solution.py:480
  3.9 5.9 %collective-permute-start = (bf16[3,5120]{1,0:T(4,128)(2,1)S(1)}, bf16[3,5120]{1,0:T(4,128)(2,1)S(1)}, u32[]{:S(2)}, u32[]{:S(2)}) collective-permute-start(bf16[3,5120]{1,0:T(4,128)(2,1)S(1)} %get-tuple-element.33), channel_id=1, source_target_pairs={{0,1},{1,2},{2,3},{4,5},{5,6},{6,7},{8,9},{9,10},{10,11},{12,13},{... | collective-permute-start | bytes 92168 | tf_op jit(solution)/shard_map/ppermute | solution.py:480
  9.8 16.0 %collective-permute-start.2 = (bf16[512,512]{1,0:T(8,128)(2,1)S(1)}, bf16[512,512]{1,0:T(8,128)(2,1)S(1)}, u32[]{:S(2)}, u32[]{:S(2)}) collective-permute-start(bf16[512,512]{1,0:T(8,128)(2,1)S(1)} %get-tuple-element.50), channel_id=1, source_target_pairs={{0,1},{4,5},{8,9},{12,13},{16,17},{20,21},{24,25},{28,29}} | collective-permute-start | bytes 1572872 | tf_op jit(solution)/shard_map/ppermute | solution.py:480
  10.5 31.6 %collective-permute-start.6 = (bf16[1024,512]{1,0:T(8,128)(2,1)S(1)}, bf16[1024,512]{1,0:T(8,128)(2,1)S(1)}, u32[]{:S(2)}, u32[]{:S(2)}) collective-permute-start(bf16[1024,512]{1,0:T(8,128)(2,1)S(1)} %bitcast.15), channel_id=1, source_target_pairs={{1,2},{2,3},{5,6},{6,7},{9,10},{10,11},{13,14},{14,15},{17,18},{18... | collective-permute-start | bytes 3145736 | tf_op jit(solution)/shard_map/ppermute | solution.py:480
  25.8 7.0 %copy-start.1 = (f32[1,1024]{1,0:T(1,128)S(1)}, f32[1,1024]{1,0:T(1,128)}, u32[]{:S(2)}) copy-start(f32[1,1024]{1,0:T(1,128)} %gain_ref.9) | copy-start | bytes 12292
  25.8 6.0 %collective-permute-start.4 = (bf16[8,128,128]{2,1,0:T(8,128)(2,1)S(1)}, bf16[8,128,128]{2,1,0:T(8,128)(2,1)S(1)}, u32[]{:S(2)}, u32[]{:S(2)}) collective-permute-start(bf16[8,128,128]{2,1,0:T(8,128)(2,1)S(1)} %get-tuple-element.51), channel_id=1, source_target_pairs={{0,1},{4,5},{8,9},{12,13},{16,17},{20,21},{24,25},{28,29}} | collective-permute-start | bytes 786440 | tf_op jit(solution)/shard_map/ppermute | solution.py:480
  26.5 14.0 %collective-permute-start.1 = (bf16[2,128,1024]{2,1,0:T(8,128)(2,1)S(1)}, bf16[2,128,1024]{2,1,0:T(8,128)(2,1)S(1)}, u32[]{:S(2)}, u32[]{:S(2)}) collective-permute-start(bf16[2,128,1024]{2,1,0:T(8,128)(2,1)S(1)} %get-tuple-element.46), channel_id=1, source_target_pairs={{3,2},{2,1},{7,6},{6,5},{11,10},{10,9},{15,14},{14,13},{19,18},{18... | collective-permute-start | bytes 1572872 | tf_op jit(solution)/shard_map/ppermute | solution.py:480
  31.1 11.0 %collective-permute-start.7 = (bf16[512,512]{1,0:T(8,128)(2,1)S(1)}, bf16[512,512]{1,0:T(8,128)(2,1)S(1)}, u32[]{:S(2)}, u32[]{:S(2)}) collective-permute-start(bf16[512,512]{1,0:T(8,128)(2,1)S(1)} %get-tuple-element.61), channel_id=1, source_target_pairs={{0,1},{4,5},{8,9},{12,13},{16,17},{20,21},{24,25},{28,29}} | collective-permute-start | bytes 1572872 | tf_op jit(solution)/shard_map/ppermute | solution.py:480
  32.1 9.1 %collective-permute-start.5 = (bf16[8,128,128]{2,1,0:T(8,128)(2,1)S(1)}, bf16[8,128,128]{2,1,0:T(8,128)(2,1)S(1)}, u32[]{:S(2)}, u32[]{:S(2)}) collective-permute-start(bf16[8,128,128]{2,1,0:T(8,128)(2,1)S(1)} %shard_map.68.state_ref), channel_id=1, source_target_pairs={{1,2},{5,6},{9,10},{13,14},{17,18},{21,22},{25,26},{29,30}} | collective-permute-start | bytes 786440 | tf_op jit(solution)/shard_map/ppermute | solution.py:480
  32.8 20.4 %collective-permute-start.13 = (bf16[128,1024]{1,0:T(8,128)(2,1)S(1)}, bf16[128,1024]{1,0:T(8,128)(2,1)S(1)}, u32[]{:S(2)}, u32[]{:S(2)}) collective-permute-start(bf16[128,1024]{1,0:T(8,128)(2,1)S(1)} %shard_map.69.rows0_ref), channel_id=1, source_target_pairs={{0,3},{4,7},{8,11},{12,15},{16,19},{20,23},{24,27},{28,31}} | collective-permute-start | bytes 786440 | tf_op jit(solution)/shard_map/ppermute | solution.py:480
  40.5 15.4 %collective-permute-start.11 = (bf16[128,1024]{1,0:T(8,128)(2,1)S(1)}, bf16[128,1024]{1,0:T(8,128)(2,1)S(1)}, u32[]{:S(2)}, u32[]{:S(2)}) collective-permute-start(bf16[128,1024]{1,0:T(8,128)(2,1)S(1)} %shard_map.70.rows1_ref), channel_id=1, source_target_pairs={{1,2},{5,6},{9,10},{13,14},{17,18},{21,22},{25,26},{29,30}} | collective-permute-start | bytes 786440 | tf_op jit(solution)/shard_map/ppermute | solution.py:480
  41.4 14.6 %collective-permute-start.10 = (bf16[128,1024]{1,0:T(8,128)(2,1)S(1)}, bf16[128,1024]{1,0:T(8,128)(2,1)S(1)}, u32[]{:S(2)}, u32[]{:S(2)}) collective-permute-start(bf16[128,1024]{1,0:T(8,128)(2,1)S(1)} %shard_map.71.rows3_ref), channel_id=1, source_target_pairs={{2,1},{6,5},{10,9},{14,13},{18,17},{22,21},{26,25},{30,29}} | collective-permute-start | bytes 786440 | tf_op jit(solution)/shard_map/ppermute | solution.py:480
  42.2 23.8 %collective-permute-start.8 = (bf16[128,1536]{1,0:T(8,128)(2,1)S(1)}, bf16[128,1536]{1,0:T(8,128)(2,1)S(1)}, u32[]{:S(2)}, u32[]{:S(2)}) collective-permute-start(bf16[128,1536]{1,0:T(8,128)(2,1)S(1)} %get-tuple-element.57), channel_id=1, source_target_pairs={{0,4},{1,5},{2,6},{4,8},{5,9},{6,10},{8,12},{9,13},{10,14},{12,16}... | collective-permute-start | bytes 1179656 | tf_op jit(solution)/shard_map/ppermute | solution.py:485
  42.8 27.8 %collective-permute-start.9 = (bf16[128,1536]{1,0:T(8,128)(2,1)S(1)}, bf16[128,1536]{1,0:T(8,128)(2,1)S(1)}, u32[]{:S(2)}, u32[]{:S(2)}) collective-permute-start(bf16[128,1536]{1,0:T(8,128)(2,1)S(1)} %get-tuple-element.58), channel_id=1, source_target_pairs={{2,7},{6,11},{10,15},{14,19},{18,23},{22,27},{26,31},{30,3}} | collective-permute-start | bytes 1179656 | tf_op jit(solution)/shard_map/ppermute | solution.py:485
  53.7 8.1 %collective-permute-start.14 = (bf16[128,1024]{1,0:T(8,128)(2,1)S(1)}, bf16[128,1024]{1,0:T(8,128)(2,1)S(1)}, u32[]{:S(2)}, u32[]{:S(2)}) collective-permute-start(bf16[128,1024]{1,0:T(8,128)(2,1)S(1)} %shard_map.74), channel_id=1, source_target_pairs={{3,4},{7,8},{11,12},{15,16},{19,20},{23,24},{27,28},{31,0}} | collective-permute-start | bytes 786440 | tf_op jit(solution)/shard_map/ppermute | solution.py:485
  56.0 9.9 %collective-permute-start.15 = (bf16[128,512]{1,0:T(8,128)(2,1)S(1)}, bf16[128,512]{1,0:T(8,128)(2,1)S(1)}, u32[]{:S(2)}, u32[]{:S(2)}) collective-permute-start(bf16[128,512]{1,0:T(8,128)(2,1)S(1)} %shard_map.75), channel_id=1, source_target_pairs={{1,7},{5,11},{9,15},{13,19},{17,23},{21,27},{25,31},{29,3}} | collective-permute-start | bytes 393224 | tf_op jit(solution)/shard_map/ppermute | solution.py:485
  57.3 8.6 %collective-permute-start.12 = (bf16[128,512]{1,0:T(8,128)(2,1)S(1)}, bf16[128,512]{1,0:T(8,128)(2,1)S(1)}, u32[]{:S(2)}, u32[]{:S(2)}) collective-permute-start(bf16[128,512]{1,0:T(8,128)(2,1)S(1)} %shard_map.73), channel_id=1, source_target_pairs={{1,6},{2,5},{5,10},{6,9},{9,14},{10,13},{13,18},{14,17},{17,22},{1... | collective-permute-start | bytes 393224 | tf_op jit(solution)/shard_map/ppermute | solution.py:485

commit v9 on v8

--- a/solution.py
+++ b/solution.py
@@ -28,6 +28,10 @@
     return dot(
         jnp.concatenate([ah, ah, al], axis=1), jnp.concatenate([bh, bl, bh], axis=0)
     )
+
+
+def dot2(a, b):
+    return dot(jnp.concatenate(split(a), axis=1), jnp.concatenate([b, b], axis=0))
 
 
 def pair_rows(left, right):
@@ -103,22 +107,25 @@
         ]
         invs = [invs[i] - dot(invs[i], blockwise(inner[i])).astype(bf16) for i in pairs]
 
-    results = []
-    for head in range(heads):
-        lower, right, outer, reach0, map0 = work[head]
-        inv = invs[head // 2][:, head % 2 * HK : (head % 2 + 1) * HK]
-        first = dot(inv, right.astype(bf16))
-        rest = right - first - dot3(lower, first)
-        solved = first + dot(inv, rest.astype(bf16))
-        both = dot3(outer, solved)
-        results.append(
-            (
-                map0 - both[:size, HK:],
-                both[:size, :HK],
-                both[size:, :HK],
-                reach0 - both[size:, HK:],
-            )
-        )
+    every = range(heads)
+    of_head = lambda head: invs[head // 2][:, head % 2 * HK : (head % 2 + 1) * HK]
+    firsts = [dot(of_head(head), work[head][1].astype(bf16)).astype(bf16) for head in every]
+    rests = [
+        work[head][1] - firsts[head].astype(f32) - dot2(work[head][0], firsts[head]) for head in every
+    ]
+    solved = [
+        firsts[head].astype(f32) + dot(of_head(head), rests[head].astype(bf16)) for head in every
+    ]
+    joint = [dot3(work[head][2], solved[head]) for head in every]
+    results = [
+        (
+            work[head][4] - joint[head][:size, HK:],
+            joint[head][:size, :HK],
+            joint[head][size:, :HK],
+            work[head][3] - joint[head][size:, HK:],
+        )
+        for head in every
+    ]
     return results
 
 
@@ -181,12 +188,18 @@
     ext[8:] = x_ref[:half].astype(f32)
     acts = activations(ext, taps_ref, half, heads)
     found = half_terms(0, heads, half, acts, beta_ref[...], gate_ref[...])
-    for head, (map1, add1, direct1, reach1) in enumerate(found):
+    all_joined = [
+        dot3(
+            jnp.concatenate(
+                [map2_ref[head], reach2_ref[:, head * HK : (head + 1) * HK]], axis=0
+            ),
+            jnp.concatenate([map1, add1], axis=1),
+        )
+        for head, (map1, add1, _, _) in enumerate(found)
+    ]
+    for head, (_, _, direct1, reach1) in enumerate(found):
         lanes = slice(head * HK, (head + 1) * HK)
-        joined = dot3(
-            jnp.concatenate([map2_ref[head], reach2_ref[:, lanes]], axis=0),
-            jnp.concatenate([map1, add1], axis=1),
-        )
+        joined = all_joined[head]
         total = joined[:HK, HK:] + add2_ref[head]
         map_ref[head] = joined[:HK, :HK]
         add_ref[head] = total
@@ -527,7 +540,8 @@
     cols = own.shape[1]
     rows = (toks, width)
     one, two, three = ((toks, blocks * cols) for blocks in (1, 2, 3))
-    sent, top, right = lax.optimization_barrier((sent, top, lefts[0]))
+    sent, top = lax.optimization_barrier((sent, top))
+    both, right = lax.optimization_barrier((both, lefts[0]))
     first = moved(sent, [(0, 1)])
     both = moved(both, [(3, 2), (2, 1)])
     out1 = hand_on(total_map, total_add, first)

time: 71.9 us -> 68.5 us (0.953)
  Pallas kernels: 18.6 us -> 14.3 us
  waiting for transfers between devices: 31.3 us -> 33.3 us
  starting transfers between devices: 21.2 us -> 20 us
    pallas_call x3, Pallas kernels: 15.4 us -> 11.3 us  [kernel_call(): pl.pallas_call(kernel, in_specs=[pl.BlockSpec(memory_space=space)] * len(...]
    ppermute x5, waiting for transfers between devices: 12.7 us -> 14.2 us  [handed(): lax.ppermute(value, ('section', 'ctx'), [(s * count + a, (s + 1) % sectio...]
    ppermute x5, starting transfers between devices: 6.18 us -> 5.24 us  [handed(): lax.ppermute(value, ('section', 'ctx'), [(s * count + a, (s + 1) % sectio...]
  transfers between devices with their start and end apart: 16 -> 16, of which waited for: 6 -> 7; matrix products, arithmetic and copies ran while one was open for 0% -> 0% of each run, Pallas kernels for 25% -> 20%
where the time goes in v9:
time: 68.5 us; the launch traced here: 68.1 us
  waiting for transfers between devices  33.3 us (49%)
  starting transfers between devices  20 us (29%)
  Pallas kernels  14.3 us (21%)
    ppermute x11, waiting for transfers between devices, moved(): return lax.ppermute(value, 'ctx', pairs)  19.1 us
    ppermute x11, starting transfers between devices, moved(): return lax.ppermute(value, 'ctx', pairs)  14.8 us
    ppermute x5, waiting for transfers between devices, handed(): lax.ppermute(value, ('section', 'ctx'), [(s * count + a, (s + 1) % sectio...  14.2 us
    pallas_call x3, Pallas kernels, kernel_call(): pl.pallas_call(kernel, in_specs=[pl.BlockSpec(memory_space=space)] * len(...  11.3 us
    ppermute x5, starting transfers between devices, handed(): lax.ppermute(value, ('section', 'ctx'), [(s * count + a, (s + 1) % sectio...  5.24 us
    pallas_call x1, Pallas kernels, load(): pl.pallas_call(load_kernel, in_specs=[pl.BlockSpec(memory_space=pltpu.HBM...  1.38 us
  transfers between devices with their start and end apart: 16, of which 7 were waited for; matrix products, arithmetic and copies ran while one was open for 0% of the time, Pallas kernels for 20%

profile of v9, /device:TPU:24, one launch (start us, length us, event | category | flops | bytes accessed | tf_op | source)
XLA Modules:
  0.0 68.1 jit_solution(9234126410591421068)
XLA Ops:
  0.0 2.5 %collective-permute-start.1 = (bf16[1024,512]{1,0:T(8,128)(2,1)}, bf16[1024,512]{1,0:T(8,128)(2,1)S(1)}, u32[]{:S(2)}, u32[]{:S(2)}) collective-permute-start(bf16[1024,512]{1,0:T(8,128)(2,1)} %bitcast.14), channel_id=1, source_target_pairs={{1,0},{2,1},{3,2},{5,4},{6,5},{7,6},{9,8},{10,9},{11,10},{13,12},{... | collective-permute-start | bytes 3145736 | tf_op jit(solution)/shard_map/ppermute | solution.py:493
  2.5 1.4 %shard_map.64 = (bf16[128,5120]{1,0:T(8,128)(2,1)S(1)}, bf16[4,5120]{1,0:T(4,128)(2,1)S(1)}, f32[16,128]{1,0:T(8,128)S(1)}, f32[8,128]{1,0:T(8,128)S(1)}, bf16[3,5120]{1,0:T(4,128)(2,1)S(1)}) custom-call(bf16[128,5120]{1,0:T(8,128)(2,1)} %bitcast.18, bf16[4,5120]{1,0:T(4,128)(2,1)} %bitcast.19, f32[16,128]{1,0:T(8,128)} %bitcast.20, f32[8,128]{1,0:T(8,128)} %bitcast.21), custom_call_target="tpu_custom_call" | custom-call | tf_op jit(solution)/shard_map/pallas_call | solution.py:232
  3.9 1.3 %collective-permute-start = (bf16[3,5120]{1,0:T(4,128)(2,1)S(1)}, bf16[3,5120]{1,0:T(4,128)(2,1)S(1)}, u32[]{:S(2)}, u32[]{:S(2)}) collective-permute-start(bf16[3,5120]{1,0:T(4,128)(2,1)S(1)} %get-tuple-element.34), channel_id=1, source_target_pairs={{0,1},{1,2},{2,3},{4,5},{5,6},{6,7},{8,9},{9,10},{10,11},{12,13},{... | collective-permute-start | bytes 92168 | tf_op jit(solution)/shard_map/ppermute | solution.py:493
  5.3 1.4 %shard_map.65.act_ref = f32[64,5120]{1,0:T(8,128)S(1)} custom-call(bf16[128,5120]{1,0:T(8,128)(2,1)S(1)} %get-tuple-element.35.x_ref, bf16[4,5120]{1,0:T(4,128)(2,1)S(1)} %get-tuple-element.36.taps_ref), custom_call_target="tpu_custom_call" | custom-call | flops 1048576 | bytes 65536 | tf_op jit(solution)/shard_map/pallas_call | solution.py:218
  6.8 3.1 %collective-permute-done.rim_ref = bf16[3,5120]{1,0:T(4,128)(2,1)S(1)} collective-permute-done((bf16[3,5120]{1,0:T(4,128)(2,1)S(1)}, bf16[3,5120]{1,0:T(4,128)(2,1)S(1)}, u32[]{:S(2)}, u32[]{:S(2)}) %collective-permute-start) | collective-permute-done | bytes 30752 | tf_op jit(solution)/shard_map/ppermute | solution.py:493
  9.8 0.7 %collective-permute-start.3 = (bf16[512,512]{1,0:T(8,128)(2,1)S(1)}, bf16[512,512]{1,0:T(8,128)(2,1)S(1)}, u32[]{:S(2)}, u32[]{:S(2)}) collective-permute-start(bf16[512,512]{1,0:T(8,128)(2,1)S(1)} %get-tuple-element.52), channel_id=1, source_target_pairs={{0,1},{4,5},{8,9},{12,13},{16,17},{20,21},{24,25},{28,29}} | collective-permute-start | bytes 1572872 | tf_op jit(solution)/shard_map/ppermute | solution.py:493
  10.5 1.3 %collective-permute-start.6 = (bf16[1024,512]{1,0:T(8,128)(2,1)S(1)}, bf16[1024,512]{1,0:T(8,128)(2,1)S(1)}, u32[]{:S(2)}, u32[]{:S(2)}) collective-permute-start(bf16[1024,512]{1,0:T(8,128)(2,1)S(1)} %bitcast.15), channel_id=1, source_target_pairs={{1,2},{2,3},{5,6},{6,7},{9,10},{10,11},{13,14},{14,15},{17,18},{18... | collective-permute-start | bytes 3145736 | tf_op jit(solution)/shard_map/ppermute | solution.py:493
  11.8 4.2 %shard_map.66 = (f32[8,128,128]{2,1,0:T(8,128)S(1)}, f32[8,128,128]{2,1,0:T(8,128)S(1)}, f32[64,1024]{1,0:T(8,128)S(1)}, f32[64,1024]{1,0:T(8,128)S(1)}) custom-call(f32[64,5120]{1,0:T(8,128)S(1)} %shard_map.65.act_ref, f32[16,128]{1,0:T(8,128)S(1)} %get-tuple-element.38.beta_ref, f32[8,128]{1,0:T(8,128)S(1)} %get-tuple-element.39.gate_ref), custom_call_target="tpu_custom_call" | custom-call | flops 1048576 | bytes 65536 | tf_op jit(solution)/shard_map/pallas_call | solution.py:218
  16.0 5.7 %shard_map.67 = (f32[8,128,128]{2,1,0:T(8,128)S(1)}, f32[8,128,128]{2,1,0:T(8,128)S(1)}, bf16[8,128,128]{2,1,0:T(8,128)(2,1)S(1)}, f32[128,1024]{1,0:T(8,128)S(1...) custom-call(bf16[3,5120]{1,0:T(4,128)(2,1)S(1)} %collective-permute-done.rim_ref, ...), custom_call_target="tpu_custom_call" | custom-call | flops 1048576 | bytes 65536 | tf_op jit(solution)/shard_map/pallas_call | solution.py:218
  21.7 0.7 collective-permute-start.4
  22.4 2.8 %collective-permute-done.1.right_ref = bf16[1024,512]{1,0:T(8,128)(2,1)S(1)} collective-permute-done((bf16[1024,512]{1,0:T(8,128)(2,1)}, bf16[1024,512]{1,0:T(8,128)(2,1)S(1)}, u32[]{:S(2)}, u32[]{:S(2)}) %collective-permute-start.1) | collective-permute-done | bytes 1048608 | tf_op jit(solution)/shard_map/ppermute | solution.py:493
  25.2 4.3 %collective-permute-start.2 = (bf16[2,128,1024]{2,1,0:T(8,128)(2,1)S(1)}, bf16[2,128,1024]{2,1,0:T(8,128)(2,1)S(1)}, u32[]{:S(2)}, u32[]{:S(2)}) collective-permute-start(bf16[2,128,1024]{2,1,0:T(8,128)(2,1)S(1)} %get-tuple-element.48), channel_id=1, source_target_pairs={{3,2},{2,1},{7,6},{6,5},{11,10},{10,9},{15,14},{14,13},{19,18},{18... | collective-permute-start | bytes 1572872 | tf_op jit(solution)/shard_map/ppermute | solution.py:493
  29.5 0.7 %collective-permute-start.7 = (bf16[512,512]{1,0:T(8,128)(2,1)S(1)}, bf16[512,512]{1,0:T(8,128)(2,1)S(1)}, u32[]{:S(2)}, u32[]{:S(2)}) collective-permute-start(bf16[512,512]{1,0:T(8,128)(2,1)S(1)} %get-tuple-element.63), channel_id=1, source_target_pairs={{0,1},{4,5},{8,9},{12,13},{16,17},{20,21},{24,25},{28,29}} | collective-permute-start | bytes 1572872 | tf_op jit(solution)/shard_map/ppermute | solution.py:493
  31.2 1.3 %collective-permute-start.13 = (bf16[128,1024]{1,0:T(8,128)(2,1)S(1)}, bf16[128,1024]{1,0:T(8,128)(2,1)S(1)}, u32[]{:S(2)}, u32[]{:S(2)}) collective-permute-start(bf16[128,1024]{1,0:T(8,128)(2,1)S(1)} %shard_map.69.rows0_ref), channel_id=1, source_target_pairs={{0,3},{4,7},{8,11},{12,15},{16,19},{20,23},{24,27},{28,31}} | collective-permute-start | bytes 786440 | tf_op jit(solution)/shard_map/ppermute | solution.py:493
  33.3 6.5 %collective-permute-done.2.both_ref = bf16[2,128,1024]{2,1,0:T(8,128)(2,1)S(1)} collective-permute-done((bf16[2,128,1024]{2,1,0:T(8,128)(2,1)S(1)}, bf16[2,128,1024]{2,1,0:T(8,128)(2,1)S(1)}, u32[]{:S(2)}, u32[]{:S(2)}) %collective-permute-start.2) | collective-permute-done | bytes 524320 | tf_op jit(solution)/shard_map/ppermute | solution.py:493
  40.5 0.7 %collective-permute-start.8 = (bf16[128,1536]{1,0:T(8,128)(2,1)S(1)}, bf16[128,1536]{1,0:T(8,128)(2,1)S(1)}, u32[]{:S(2)}, u32[]{:S(2)}) collective-permute-start(bf16[128,1536]{1,0:T(8,128)(2,1)S(1)} %get-tuple-element.59), channel_id=1, source_target_pairs={{0,4},{1,5},{2,6},{4,8},{5,9},{6,10},{8,12},{9,13},{10,14},{12,16}... | collective-permute-start | bytes 1179656 | tf_op jit(solution)/shard_map/ppermute | solution.py:498
  41.2 1.3 %collective-permute-start.9 = (bf16[128,1536]{1,0:T(8,128)(2,1)S(1)}, bf16[128,1536]{1,0:T(8,128)(2,1)S(1)}, u32[]{:S(2)}, u32[]{:S(2)}) collective-permute-start(bf16[128,1536]{1,0:T(8,128)(2,1)S(1)} %get-tuple-element.60), channel_id=1, source_target_pairs={{2,7},{6,11},{10,15},{14,19},{18,23},{22,27},{26,31},{30,3}} | collective-permute-start | bytes 1179656 | tf_op jit(solution)/shard_map/ppermute | solution.py:498
  42.5 6.7 %collective-permute-done.13.rows_ref = bf16[128,1024]{1,0:T(8,128)(2,1)S(1)} collective-permute-done((bf16[128,1024]{1,0:T(8,128)(2,1)S(1)}, bf16[128,1024]{1,0:T(8,128)(2,1)S(1)}, u32[]{:S(2)}, u32[]{:S(2)}) %collective-permute-start.13) | collective-permute-done | bytes 262176 | tf_op jit(solution)/shard_map/ppermute | solution.py:493
  49.6 1.3 %collective-permute-start.14 = (bf16[128,1024]{1,0:T(8,128)(2,1)S(1)}, bf16[128,1024]{1,0:T(8,128)(2,1)S(1)}, u32[]{:S(2)}, u32[]{:S(2)}) collective-permute-start(bf16[128,1024]{1,0:T(8,128)(2,1)S(1)} %shard_map.74), channel_id=1, source_target_pairs={{3,4},{7,8},{11,12},{15,16},{19,20},{23,24},{27,28},{31,0}} | collective-permute-start | bytes 786440 | tf_op jit(solution)/shard_map/ppermute | solution.py:498
  51.0 1.3 %collective-permute-start.15 = (bf16[128,512]{1,0:T(8,128)(2,1)S(1)}, bf16[128,512]{1,0:T(8,128)(2,1)S(1)}, u32[]{:S(2)}, u32[]{:S(2)}) collective-permute-start(bf16[128,512]{1,0:T(8,128)(2,1)S(1)} %shard_map.75), channel_id=1, source_target_pairs={{1,7},{5,11},{9,15},{13,19},{17,23},{21,27},{25,31},{29,3}} | collective-permute-start | bytes 393224 | tf_op jit(solution)/shard_map/ppermute | solution.py:498
  53.0 4.6 %collective-permute-done.14.first_two = bf16[128,1024]{1,0:T(8,128)(2,1)S(1)} collective-permute-done((bf16[128,1024]{1,0:T(8,128)(2,1)S(1)}, bf16[128,1024]{1,0:T(8,128)(2,1)S(1)}, u32[]{:S(2)}, u32[]{:S(2)}) %collective-permute-start.14) | collective-permute-done | bytes 262176 | tf_op jit(solution)/shard_map/ppermute | solution.py:498
  57.6 3.2 %collective-permute-done.15.last_one = bf16[128,512]{1,0:T(8,128)(2,1)S(1)} collective-permute-done((bf16[128,512]{1,0:T(8,128)(2,1)S(1)}, bf16[128,512]{1,0:T(8,128)(2,1)S(1)}, u32[]{:S(2)}, u32[]{:S(2)}) %collective-permute-start.15) | collective-permute-done | bytes 131104 | tf_op jit(solution)/shard_map/ppermute | solution.py:498
  60.8 6.5 %collective-permute-done.9.next_three = bf16[128,1536]{1,0:T(8,128)(2,1)S(1)} collective-permute-done((bf16[128,1536]{1,0:T(8,128)(2,1)S(1)}, bf16[128,1536]{1,0:T(8,128)(2,1)S(1)}, u32[]{:S(2)}, u32[]{:S(2)}) %collective-permute-start.9) | collective-permute-done | bytes 393248 | tf_op jit(solution)/shard_map/ppermute | solution.py:498
  67.2 0.8 %shard_map.76 = bf16[128,2048]{1,0:T(8,128)(2,1)} custom-call(bf16[128,1536]{1,0:T(8,128)(2,1)S(1)} %collective-permute-done.8.own_three, bf16[128,1536]{1,0:T(8,128)(2,1)S(1)} %collective-permute-done.9.next_three, bf16[128,512]{1,0:T(8,128)(2,1)S(1)} %collective-permute-done.12.middle_one, bf16[128,1024]{1,0:T(8,128)(2,1)S(1)} %collective-permute-done.14.first_two, ...), custom_call_target="tpu_custom_call" | custom-call | flops 1048576 | bytes 65536 | tf_op jit(solution)/shard_map/pallas_call | solution.py:462
  (26 shorter events, 3.6 us)
Async XLA Ops:
  0.0 5.2 %copy-start = (bf16[1,1024,512]{2,1,0:T(8,128)(2,1)S(1)}, bf16[1,1024,512]{2,1,0:T(8,128)(2,1)}, u32[]{:S(2)}) copy-start(bf16[1,1024,512]{2,1,0:T(8,128)(2,1)} %param.11) | copy-start | bytes 3145732
  0.0 25.2 %collective-permute-start.1 = (bf16[1024,512]{1,0:T(8,128)(2,1)}, bf16[1024,512]{1,0:T(8,128)(2,1)S(1)}, u32[]{:S(2)}, u32[]{:S(2)}) collective-permute-start(bf16[1024,512]{1,0:T(8,128)(2,1)} %bitcast.14), channel_id=1, source_target_pairs={{1,0},{2,1},{3,2},{5,4},{6,5},{7,6},{9,8},{10,9},{11,10},{13,12},{... | collective-permute-start | bytes 3145736 | tf_op jit(solution)/shard_map/ppermute | solution.py:493
  3.9 5.9 %collective-permute-start = (bf16[3,5120]{1,0:T(4,128)(2,1)S(1)}, bf16[3,5120]{1,0:T(4,128)(2,1)S(1)}, u32[]{:S(2)}, u32[]{:S(2)}) collective-permute-start(bf16[3,5120]{1,0:T(4,128)(2,1)S(1)} %get-tuple-element.34), channel_id=1, source_target_pairs={{0,1},{1,2},{2,3},{4,5},{5,6},{6,7},{8,9},{9,10},{10,11},{12,13},{... | collective-permute-start | bytes 92168 | tf_op jit(solution)/shard_map/ppermute | solution.py:493
  9.8 11.9 %collective-permute-start.3 = (bf16[512,512]{1,0:T(8,128)(2,1)S(1)}, bf16[512,512]{1,0:T(8,128)(2,1)S(1)}, u32[]{:S(2)}, u32[]{:S(2)}) collective-permute-start(bf16[512,512]{1,0:T(8,128)(2,1)S(1)} %get-tuple-element.52), channel_id=1, source_target_pairs={{0,1},{4,5},{8,9},{12,13},{16,17},{20,21},{24,25},{28,29}} | collective-permute-start | bytes 1572872 | tf_op jit(solution)/shard_map/ppermute | solution.py:493
  10.5 29.9 %collective-permute-start.6 = (bf16[1024,512]{1,0:T(8,128)(2,1)S(1)}, bf16[1024,512]{1,0:T(8,128)(2,1)S(1)}, u32[]{:S(2)}, u32[]{:S(2)}) collective-permute-start(bf16[1024,512]{1,0:T(8,128)(2,1)S(1)} %bitcast.15), channel_id=1, source_target_pairs={{1,2},{2,3},{5,6},{6,7},{9,10},{10,11},{13,14},{14,15},{17,18},{18... | collective-permute-start | bytes 3145736 | tf_op jit(solution)/shard_map/ppermute | solution.py:493
  21.7 9.5 %copy-start.1 = (f32[1,1024]{1,0:T(1,128)S(1)}, f32[1,1024]{1,0:T(1,128)}, u32[]{:S(2)}) copy-start(f32[1,1024]{1,0:T(1,128)} %gain_ref.9) | copy-start | bytes 12292
  21.7 8.5 %collective-permute-start.4 = (bf16[8,128,128]{2,1,0:T(8,128)(2,1)S(1)}, bf16[8,128,128]{2,1,0:T(8,128)(2,1)S(1)}, u32[]{:S(2)}, u32[]{:S(2)}) collective-permute-start(bf16[8,128,128]{2,1,0:T(8,128)(2,1)S(1)} %get-tuple-element.53), channel_id=1, source_target_pairs={{0,1},{4,5},{8,9},{12,13},{16,17},{20,21},{24,25},{28,29}} | collective-permute-start | bytes 786440 | tf_op jit(solution)/shard_map/ppermute | solution.py:493
  25.2 14.6 %collective-permute-start.2 = (bf16[2,128,1024]{2,1,0:T(8,128)(2,1)S(1)}, bf16[2,128,1024]{2,1,0:T(8,128)(2,1)S(1)}, u32[]{:S(2)}, u32[]{:S(2)}) collective-permute-start(bf16[2,128,1024]{2,1,0:T(8,128)(2,1)S(1)} %get-tuple-element.48), channel_id=1, source_target_pairs={{3,2},{2,1},{7,6},{6,5},{11,10},{10,9},{15,14},{14,13},{19,18},{18... | collective-permute-start | bytes 1572872 | tf_op jit(solution)/shard_map/ppermute | solution.py:493
  29.5 10.9 %collective-permute-start.7 = (bf16[512,512]{1,0:T(8,128)(2,1)S(1)}, bf16[512,512]{1,0:T(8,128)(2,1)S(1)}, u32[]{:S(2)}, u32[]{:S(2)}) collective-permute-start(bf16[512,512]{1,0:T(8,128)(2,1)S(1)} %get-tuple-element.63), channel_id=1, source_target_pairs={{0,1},{4,5},{8,9},{12,13},{16,17},{20,21},{24,25},{28,29}} | collective-permute-start | bytes 1572872 | tf_op jit(solution)/shard_map/ppermute | solution.py:493
  30.5 2.0 %collective-permute-start.5 = (bf16[8,128,128]{2,1,0:T(8,128)(2,1)S(1)}, bf16[8,128,128]{2,1,0:T(8,128)(2,1)S(1)}, u32[]{:S(2)}, u32[]{:S(2)}) collective-permute-start(bf16[8,128,128]{2,1,0:T(8,128)(2,1)S(1)} %shard_map.68.state_ref), channel_id=1, source_target_pairs={{1,2},{5,6},{9,10},{13,14},{17,18},{21,22},{25,26},{29,30}} | collective-permute-start | bytes 786440 | tf_op jit(solution)/shard_map/ppermute | solution.py:493
  31.2 17.9 %collective-permute-start.13 = (bf16[128,1024]{1,0:T(8,128)(2,1)S(1)}, bf16[128,1024]{1,0:T(8,128)(2,1)S(1)}, u32[]{:S(2)}, u32[]{:S(2)}) collective-permute-start(bf16[128,1024]{1,0:T(8,128)(2,1)S(1)} %shard_map.69.rows0_ref), channel_id=1, source_target_pairs={{0,3},{4,7},{8,11},{12,15},{16,19},{20,23},{24,27},{28,31}} | collective-permute-start | bytes 786440 | tf_op jit(solution)/shard_map/ppermute | solution.py:493
  32.6 18.4 %collective-permute-start.11 = (bf16[128,1024]{1,0:T(8,128)(2,1)S(1)}, bf16[128,1024]{1,0:T(8,128)(2,1)S(1)}, u32[]{:S(2)}, u32[]{:S(2)}) collective-permute-start(bf16[128,1024]{1,0:T(8,128)(2,1)S(1)} %shard_map.70.rows1_ref), channel_id=1, source_target_pairs={{1,2},{5,6},{9,10},{13,14},{17,18},{21,22},{25,26},{29,30}} | collective-permute-start | bytes 786440 | tf_op jit(solution)/shard_map/ppermute | solution.py:493
  39.8 11.2 %collective-permute-start.10 = (bf16[128,1024]{1,0:T(8,128)(2,1)S(1)}, bf16[128,1024]{1,0:T(8,128)(2,1)S(1)}, u32[]{:S(2)}, u32[]{:S(2)}) collective-permute-start(bf16[128,1024]{1,0:T(8,128)(2,1)S(1)} %shard_map.71.rows3_ref), channel_id=1, source_target_pairs={{2,1},{6,5},{10,9},{14,13},{18,17},{22,21},{26,25},{30,29}} | collective-permute-start | bytes 786440 | tf_op jit(solution)/shard_map/ppermute | solution.py:493
  40.5 20.3 %collective-permute-start.8 = (bf16[128,1536]{1,0:T(8,128)(2,1)S(1)}, bf16[128,1536]{1,0:T(8,128)(2,1)S(1)}, u32[]{:S(2)}, u32[]{:S(2)}) collective-permute-start(bf16[128,1536]{1,0:T(8,128)(2,1)S(1)} %get-tuple-element.59), channel_id=1, source_target_pairs={{0,4},{1,5},{2,6},{4,8},{5,9},{6,10},{8,12},{9,13},{10,14},{12,16}... | collective-permute-start | bytes 1179656 | tf_op jit(solution)/shard_map/ppermute | solution.py:498
  41.2 26.1 %collective-permute-start.9 = (bf16[128,1536]{1,0:T(8,128)(2,1)S(1)}, bf16[128,1536]{1,0:T(8,128)(2,1)S(1)}, u32[]{:S(2)}, u32[]{:S(2)}) collective-permute-start(bf16[128,1536]{1,0:T(8,128)(2,1)S(1)} %get-tuple-element.60), channel_id=1, source_target_pairs={{2,7},{6,11},{10,15},{14,19},{18,23},{22,27},{26,31},{30,3}} | collective-permute-start | bytes 1179656 | tf_op jit(solution)/shard_map/ppermute | solution.py:498
  49.6 8.0 %collective-permute-start.14 = (bf16[128,1024]{1,0:T(8,128)(2,1)S(1)}, bf16[128,1024]{1,0:T(8,128)(2,1)S(1)}, u32[]{:S(2)}, u32[]{:S(2)}) collective-permute-start(bf16[128,1024]{1,0:T(8,128)(2,1)S(1)} %shard_map.74), channel_id=1, source_target_pairs={{3,4},{7,8},{11,12},{15,16},{19,20},{23,24},{27,28},{31,0}} | collective-permute-start | bytes 786440 | tf_op jit(solution)/shard_map/ppermute | solution.py:498
  51.0 9.8 %collective-permute-start.15 = (bf16[128,512]{1,0:T(8,128)(2,1)S(1)}, bf16[128,512]{1,0:T(8,128)(2,1)S(1)}, u32[]{:S(2)}, u32[]{:S(2)}) collective-permute-start(bf16[128,512]{1,0:T(8,128)(2,1)S(1)} %shard_map.75), channel_id=1, source_target_pairs={{1,7},{5,11},{9,15},{13,19},{17,23},{21,27},{25,31},{29,3}} | collective-permute-start | bytes 393224 | tf_op jit(solution)/shard_map/ppermute | solution.py:498
  52.3 8.5 %collective-permute-start.12 = (bf16[128,512]{1,0:T(8,128)(2,1)S(1)}, bf16[128,512]{1,0:T(8,128)(2,1)S(1)}, u32[]{:S(2)}, u32[]{:S(2)}) collective-permute-start(bf16[128,512]{1,0:T(8,128)(2,1)S(1)} %shard_map.73), channel_id=1, source_target_pairs={{1,6},{2,5},{5,10},{6,9},{9,14},{10,13},{13,18},{14,17},{17,22},{1... | collective-permute-start | bytes 393224 | tf_op jit(solution)/shard_map/ppermute | solution.py:498

commit v10 on v9

--- a/solution.py
+++ b/solution.py
@@ -375,17 +375,27 @@
 
 
 def rows_with_state(direct_ref, reach_ref, gain_ref, state_ref, out_ref):
-    for head, lanes in head_lanes(state_ref.shape[0]):
-        state = state_ref[head]
-        out = direct_ref[:, lanes] + dot(
-            jnp.concatenate(split(reach_ref[:, lanes]), axis=1), jnp.concatenate([state, state], axis=0)
+    places = head_lanes(state_ref.shape[0])
+    outs = [
+        direct_ref[:, lanes]
+        + dot(
+            jnp.concatenate(split(reach_ref[:, lanes]), axis=1),
+            jnp.concatenate([state_ref[head], state_ref[head]], axis=0),
         )
-        out_ref[:, lanes] = normed_rows(out, gain_ref[:, lanes])
-
-
-def rows_of_next(both_ref, gain_ref, head, lanes, state):
-    out = both_ref[0, :, lanes].astype(f32) + dot(both_ref[1, :, lanes], state)
-    return normed_rows(out, gain_ref[:, lanes])
+        for head, lanes in places
+    ]
+    for head, lanes in places:
+        out_ref[:, lanes] = normed_rows(outs[head], gain_ref[:, lanes])
+
+
+def rows_of_next(both_ref, gain_ref, states, out_ref):
+    places = head_lanes(len(states))
+    outs = [
+        both_ref[0, :, lanes].astype(f32) + dot(both_ref[1, :, lanes], states[head])
+        for head, lanes in places
+    ]
+    for head, lanes in places:
+        out_ref[:, lanes] = normed_rows(outs[head], gain_ref[:, lanes])
 
 
 def first_rows_kernel(direct_ref, gain_ref, out_ref):
@@ -404,8 +414,8 @@
 def middle_columns_kernel(both_ref, gain_ref, state_ref, rows1_ref, left_a, left_b, right_ref, out_ref, rows_ref):
     @on_shard(1)
     def _():
-        for head, lanes in head_lanes(state_ref.shape[0]):
-            rows_ref[:, lanes] = rows_of_next(both_ref, gain_ref, head, lanes, state_ref[head])
+        states = [state_ref[head] for head in range(state_ref.shape[0])]
+        rows_of_next(both_ref, gain_ref, states, rows_ref)
         project_to(out_ref, rows_ref[...], (left_a, left_b))
 
     @on_shard(2)
@@ -416,12 +426,15 @@
 def fourth_rows_kernel(map_ref, add_ref, both_ref, gain_ref, state_ref, out_ref):
     @on_shard(2)
     def _():
-        for head, lanes in head_lanes(state_ref.shape[0]):
-            state = state_ref[head]
-            left = add_ref[head] + dot(
-                jnp.concatenate(split(map_ref[head]), axis=1), jnp.concatenate([state, state], axis=0)
+        lefts = [
+            add_ref[head]
+            + dot(
+                jnp.concatenate(split(map_ref[head]), axis=1),
+                jnp.concatenate([state_ref[head], state_ref[head]], axis=0),
             )
-            out_ref[:, lanes] = rows_of_next(both_ref, gain_ref, head, lanes, left.astype(bf16))
+            for head in range(state_ref.shape[0])
+        ]
+        rows_of_next(both_ref, gain_ref, [left.astype(bf16) for left in lefts], out_ref)
 
 
 def near_columns_kernel(
@@ -564,7 +577,6 @@
         middle_columns_kernel, [both, norm_gain, out1, far1, top, rest, right], [one], [rows]
     )
     first_two = call(first_columns_kernel, [far0, whole, left], [two])
-    far3, middle_one = lax.optimization_barrier((far3, middle_one))
     last_one = call(last_columns_kernel, [far3, top, rest], [one])
     return call(
         assemble_kernel,

time: 68.5 us -> 68.5 us (level)
  no operation moved by 1% of the time
where the time goes in v10:
time: 68.5 us; the launch traced here: 68.1 us
  waiting for transfers between devices  33.3 us (49%)
  starting transfers between devices  20 us (29%)
  Pallas kernels  14.3 us (21%)
    ppermute x11, waiting for transfers between devices, moved(): return lax.ppermute(value, 'ctx', pairs)  19.1 us
    ppermute x11, starting transfers between devices, moved(): return lax.ppermute(value, 'ctx', pairs)  14.8 us
    ppermute x5, waiting for transfers between devices, handed(): lax.ppermute(value, ('section', 'ctx'), [(s * count + a, (s + 1) % sectio...  14.2 us
    pallas_call x3, Pallas kernels, kernel_call(): pl.pallas_call(kernel, in_specs=[pl.BlockSpec(memory_space=space)] * len(...  11.3 us
    ppermute x5, starting transfers between devices, handed(): lax.ppermute(value, ('section', 'ctx'), [(s * count + a, (s + 1) % sectio...  5.24 us
    pallas_call x1, Pallas kernels, load(): pl.pallas_call(load_kernel, in_specs=[pl.BlockSpec(memory_space=pltpu.HBM...  1.38 us
  transfers between devices with their start and end apart: 16, of which 7 were waited for; matrix products, arithmetic and copies ran while one was open for 0% of the time, Pallas kernels for 20%

profile of v10, /device:TPU:24, one launch (start us, length us, event | category | flops | bytes accessed | tf_op | source)
XLA Modules:
  0.0 68.1 jit_solution(4905619028090059163)
XLA Ops:
  0.0 2.5 %collective-permute-start.1 = (bf16[1024,512]{1,0:T(8,128)(2,1)}, bf16[1024,512]{1,0:T(8,128)(2,1)S(1)}, u32[]{:S(2)}, u32[]{:S(2)}) collective-permute-start(bf16[1024,512]{1,0:T(8,128)(2,1)} %bitcast.14), channel_id=1, source_target_pairs={{1,0},{2,1},{3,2},{5,4},{6,5},{7,6},{9,8},{10,9},{11,10},{13,12},{... | collective-permute-start | bytes 3145736 | tf_op jit(solution)/shard_map/ppermute | solution.py:506
  2.5 1.4 %shard_map.64 = (bf16[128,5120]{1,0:T(8,128)(2,1)S(1)}, bf16[4,5120]{1,0:T(4,128)(2,1)S(1)}, f32[16,128]{1,0:T(8,128)S(1)}, f32[8,128]{1,0:T(8,128)S(1)}, bf16[3,5120]{1,0:T(4,128)(2,1)S(1)}) custom-call(bf16[128,5120]{1,0:T(8,128)(2,1)} %bitcast.18, bf16[4,5120]{1,0:T(4,128)(2,1)} %bitcast.19, f32[16,128]{1,0:T(8,128)} %bitcast.20, f32[8,128]{1,0:T(8,128)} %bitcast.21), custom_call_target="tpu_custom_call" | custom-call | tf_op jit(solution)/shard_map/pallas_call | solution.py:232
  3.9 1.3 %collective-permute-start = (bf16[3,5120]{1,0:T(4,128)(2,1)S(1)}, bf16[3,5120]{1,0:T(4,128)(2,1)S(1)}, u32[]{:S(2)}, u32[]{:S(2)}) collective-permute-start(bf16[3,5120]{1,0:T(4,128)(2,1)S(1)} %get-tuple-element.32), channel_id=1, source_target_pairs={{0,1},{1,2},{2,3},{4,5},{5,6},{6,7},{8,9},{9,10},{10,11},{12,13},{... | collective-permute-start | bytes 92168 | tf_op jit(solution)/shard_map/ppermute | solution.py:506
  5.3 1.4 %shard_map.65.act_ref = f32[64,5120]{1,0:T(8,128)S(1)} custom-call(bf16[128,5120]{1,0:T(8,128)(2,1)S(1)} %get-tuple-element.33.x_ref, bf16[4,5120]{1,0:T(4,128)(2,1)S(1)} %get-tuple-element.34.taps_ref), custom_call_target="tpu_custom_call" | custom-call | flops 1048576 | bytes 65536 | tf_op jit(solution)/shard_map/pallas_call | solution.py:218
  6.8 3.1 %collective-permute-done.rim_ref = bf16[3,5120]{1,0:T(4,128)(2,1)S(1)} collective-permute-done((bf16[3,5120]{1,0:T(4,128)(2,1)S(1)}, bf16[3,5120]{1,0:T(4,128)(2,1)S(1)}, u32[]{:S(2)}, u32[]{:S(2)}) %collective-permute-start) | collective-permute-done | bytes 30752 | tf_op jit(solution)/shard_map/ppermute | solution.py:506
  9.8 0.7 %collective-permute-start.3 = (bf16[512,512]{1,0:T(8,128)(2,1)S(1)}, bf16[512,512]{1,0:T(8,128)(2,1)S(1)}, u32[]{:S(2)}, u32[]{:S(2)}) collective-permute-start(bf16[512,512]{1,0:T(8,128)(2,1)S(1)} %get-tuple-element.50), channel_id=1, source_target_pairs={{0,1},{4,5},{8,9},{12,13},{16,17},{20,21},{24,25},{28,29}} | collective-permute-start | bytes 1572872 | tf_op jit(solution)/shard_map/ppermute | solution.py:506
  10.5 1.3 %collective-permute-start.6 = (bf16[1024,512]{1,0:T(8,128)(2,1)S(1)}, bf16[1024,512]{1,0:T(8,128)(2,1)S(1)}, u32[]{:S(2)}, u32[]{:S(2)}) collective-permute-start(bf16[1024,512]{1,0:T(8,128)(2,1)S(1)} %bitcast.15), channel_id=1, source_target_pairs={{1,2},{2,3},{5,6},{6,7},{9,10},{10,11},{13,14},{14,15},{17,18},{18... | collective-permute-start | bytes 3145736 | tf_op jit(solution)/shard_map/ppermute | solution.py:506
  11.8 4.2 %shard_map.66 = (f32[8,128,128]{2,1,0:T(8,128)S(1)}, f32[8,128,128]{2,1,0:T(8,128)S(1)}, f32[64,1024]{1,0:T(8,128)S(1)}, f32[64,1024]{1,0:T(8,128)S(1)}) custom-call(f32[64,5120]{1,0:T(8,128)S(1)} %shard_map.65.act_ref, f32[16,128]{1,0:T(8,128)S(1)} %get-tuple-element.36.beta_ref, f32[8,128]{1,0:T(8,128)S(1)} %get-tuple-element.37.gate_ref), custom_call_target="tpu_custom_call" | custom-call | flops 1048576 | bytes 65536 | tf_op jit(solution)/shard_map/pallas_call | solution.py:218
  16.0 5.7 %shard_map.67 = (f32[8,128,128]{2,1,0:T(8,128)S(1)}, f32[8,128,128]{2,1,0:T(8,128)S(1)}, bf16[8,128,128]{2,1,0:T(8,128)(2,1)S(1)}, f32[128,1024]{1,0:T(8,128)S(1...) custom-call(bf16[3,5120]{1,0:T(4,128)(2,1)S(1)} %collective-permute-done.rim_ref, ...), custom_call_target="tpu_custom_call" | custom-call | flops 1048576 | bytes 65536 | tf_op jit(solution)/shard_map/pallas_call | solution.py:218
  21.7 0.7 collective-permute-start.4
  22.4 2.8 %collective-permute-done.1.right_ref = bf16[1024,512]{1,0:T(8,128)(2,1)S(1)} collective-permute-done((bf16[1024,512]{1,0:T(8,128)(2,1)}, bf16[1024,512]{1,0:T(8,128)(2,1)S(1)}, u32[]{:S(2)}, u32[]{:S(2)}) %collective-permute-start.1) | collective-permute-done | bytes 1048608 | tf_op jit(solution)/shard_map/ppermute | solution.py:506
  25.2 4.3 %collective-permute-start.2 = (bf16[2,128,1024]{2,1,0:T(8,128)(2,1)S(1)}, bf16[2,128,1024]{2,1,0:T(8,128)(2,1)S(1)}, u32[]{:S(2)}, u32[]{:S(2)}) collective-permute-start(bf16[2,128,1024]{2,1,0:T(8,128)(2,1)S(1)} %get-tuple-element.46), channel_id=1, source_target_pairs={{3,2},{2,1},{7,6},{6,5},{11,10},{10,9},{15,14},{14,13},{19,18},{18... | collective-permute-start | bytes 1572872 | tf_op jit(solution)/shard_map/ppermute | solution.py:506
  29.5 0.7 %collective-permute-start.7 = (bf16[512,512]{1,0:T(8,128)(2,1)S(1)}, bf16[512,512]{1,0:T(8,128)(2,1)S(1)}, u32[]{:S(2)}, u32[]{:S(2)}) collective-permute-start(bf16[512,512]{1,0:T(8,128)(2,1)S(1)} %get-tuple-element.59), channel_id=1, source_target_pairs={{0,1},{4,5},{8,9},{12,13},{16,17},{20,21},{24,25},{28,29}} | collective-permute-start | bytes 1572872 | tf_op jit(solution)/shard_map/ppermute | solution.py:506
  30.5 0.7 collective-permute-start.5
  31.2 1.3 %collective-permute-start.12 = (bf16[128,1024]{1,0:T(8,128)(2,1)S(1)}, bf16[128,1024]{1,0:T(8,128)(2,1)S(1)}, u32[]{:S(2)}, u32[]{:S(2)}) collective-permute-start(bf16[128,1024]{1,0:T(8,128)(2,1)S(1)} %shard_map.69.rows0_ref), channel_id=1, source_target_pairs={{0,3},{4,7},{8,11},{12,15},{16,19},{20,23},{24,27},{28,31}} | collective-permute-start | bytes 786440 | tf_op jit(solution)/shard_map/ppermute | solution.py:506
  33.3 6.5 %collective-permute-done.2.both_ref = bf16[2,128,1024]{2,1,0:T(8,128)(2,1)S(1)} collective-permute-done((bf16[2,128,1024]{2,1,0:T(8,128)(2,1)S(1)}, bf16[2,128,1024]{2,1,0:T(8,128)(2,1)S(1)}, u32[]{:S(2)}, u32[]{:S(2)}) %collective-permute-start.2) | collective-permute-done | bytes 524320 | tf_op jit(solution)/shard_map/ppermute | solution.py:506
  40.5 0.7 %collective-permute-start.8 = (bf16[128,1536]{1,0:T(8,128)(2,1)S(1)}, bf16[128,1536]{1,0:T(8,128)(2,1)S(1)}, u32[]{:S(2)}, u32[]{:S(2)}) collective-permute-start(bf16[128,1536]{1,0:T(8,128)(2,1)S(1)} %get-tuple-element.57), channel_id=1, source_target_pairs={{0,4},{1,5},{2,6},{4,8},{5,9},{6,10},{8,12},{9,13},{10,14},{12,16}... | collective-permute-start | bytes 1179656 | tf_op jit(solution)/shard_map/ppermute | solution.py:511
  41.2 1.3 %collective-permute-start.9 = (bf16[128,1536]{1,0:T(8,128)(2,1)S(1)}, bf16[128,1536]{1,0:T(8,128)(2,1)S(1)}, u32[]{:S(2)}, u32[]{:S(2)}) collective-permute-start(bf16[128,1536]{1,0:T(8,128)(2,1)S(1)} %get-tuple-element.58), channel_id=1, source_target_pairs={{2,7},{6,11},{10,15},{14,19},{18,23},{22,27},{26,31},{30,3}} | collective-permute-start | bytes 1179656 | tf_op jit(solution)/shard_map/ppermute | solution.py:511
  42.5 6.7 %collective-permute-done.12.rows_ref = bf16[128,1024]{1,0:T(8,128)(2,1)S(1)} collective-permute-done((bf16[128,1024]{1,0:T(8,128)(2,1)S(1)}, bf16[128,1024]{1,0:T(8,128)(2,1)S(1)}, u32[]{:S(2)}, u32[]{:S(2)}) %collective-permute-start.12) | collective-permute-done | bytes 262176 | tf_op jit(solution)/shard_map/ppermute | solution.py:506
  49.6 1.3 %collective-permute-start.13 = (bf16[128,1024]{1,0:T(8,128)(2,1)S(1)}, bf16[128,1024]{1,0:T(8,128)(2,1)S(1)}, u32[]{:S(2)}, u32[]{:S(2)}) collective-permute-start(bf16[128,1024]{1,0:T(8,128)(2,1)S(1)} %shard_map.74), channel_id=1, source_target_pairs={{3,4},{7,8},{11,12},{15,16},{19,20},{23,24},{27,28},{31,0}} | collective-permute-start | bytes 786440 | tf_op jit(solution)/shard_map/ppermute | solution.py:511
  51.7 1.3 %collective-permute-start.15 = (bf16[128,512]{1,0:T(8,128)(2,1)S(1)}, bf16[128,512]{1,0:T(8,128)(2,1)S(1)}, u32[]{:S(2)}, u32[]{:S(2)}) collective-permute-start(bf16[128,512]{1,0:T(8,128)(2,1)S(1)} %shard_map.75), channel_id=1, source_target_pairs={{1,7},{5,11},{9,15},{13,19},{17,23},{21,27},{25,31},{29,3}} | collective-permute-start | bytes 393224 | tf_op jit(solution)/shard_map/ppermute | solution.py:511
  53.0 4.6 %collective-permute-done.13.first_two = bf16[128,1024]{1,0:T(8,128)(2,1)S(1)} collective-permute-done((bf16[128,1024]{1,0:T(8,128)(2,1)S(1)}, bf16[128,1024]{1,0:T(8,128)(2,1)S(1)}, u32[]{:S(2)}, u32[]{:S(2)}) %collective-permute-start.13) | collective-permute-done | bytes 262176 | tf_op jit(solution)/shard_map/ppermute | solution.py:511
  57.6 9.0 %collective-permute-done.15.last_one = bf16[128,512]{1,0:T(8,128)(2,1)S(1)} collective-permute-done((bf16[128,512]{1,0:T(8,128)(2,1)S(1)}, bf16[128,512]{1,0:T(8,128)(2,1)S(1)}, u32[]{:S(2)}, u32[]{:S(2)}) %collective-permute-start.15) | collective-permute-done | bytes 131104 | tf_op jit(solution)/shard_map/ppermute | solution.py:511
  67.2 0.8 %shard_map.76 = bf16[128,2048]{1,0:T(8,128)(2,1)} custom-call(bf16[128,1536]{1,0:T(8,128)(2,1)S(1)} %collective-permute-done.8.own_three, bf16[128,1536]{1,0:T(8,128)(2,1)S(1)} %collective-permute-done.9.next_three, bf16[128,512]{1,0:T(8,128)(2,1)S(1)} %collective-permute-done.11.middle_one, bf16[128,1024]{1,0:T(8,128)(2,1)S(1)} %collective-permute-done.13.first_two, ...), custom_call_target="tpu_custom_call" | custom-call | flops 1048576 | bytes 65536 | tf_op jit(solution)/shard_map/pallas_call | solution.py:475
  (26 shorter events, 3.6 us)
Async XLA Ops:
  0.0 5.2 %copy-start = (bf16[1,1024,512]{2,1,0:T(8,128)(2,1)S(1)}, bf16[1,1024,512]{2,1,0:T(8,128)(2,1)}, u32[]{:S(2)}) copy-start(bf16[1,1024,512]{2,1,0:T(8,128)(2,1)} %param.11) | copy-start | bytes 3145732
  0.0 25.2 %collective-permute-start.1 = (bf16[1024,512]{1,0:T(8,128)(2,1)}, bf16[1024,512]{1,0:T(8,128)(2,1)S(1)}, u32[]{:S(2)}, u32[]{:S(2)}) collective-permute-start(bf16[1024,512]{1,0:T(8,128)(2,1)} %bitcast.14), channel_id=1, source_target_pairs={{1,0},{2,1},{3,2},{5,4},{6,5},{7,6},{9,8},{10,9},{11,10},{13,12},{... | collective-permute-start | bytes 3145736 | tf_op jit(solution)/shard_map/ppermute | solution.py:506
  3.9 5.9 %collective-permute-start = (bf16[3,5120]{1,0:T(4,128)(2,1)S(1)}, bf16[3,5120]{1,0:T(4,128)(2,1)S(1)}, u32[]{:S(2)}, u32[]{:S(2)}) collective-permute-start(bf16[3,5120]{1,0:T(4,128)(2,1)S(1)} %get-tuple-element.32), channel_id=1, source_target_pairs={{0,1},{1,2},{2,3},{4,5},{5,6},{6,7},{8,9},{9,10},{10,11},{12,13},{... | collective-permute-start | bytes 92168 | tf_op jit(solution)/shard_map/ppermute | solution.py:506
  9.8 11.9 %collective-permute-start.3 = (bf16[512,512]{1,0:T(8,128)(2,1)S(1)}, bf16[512,512]{1,0:T(8,128)(2,1)S(1)}, u32[]{:S(2)}, u32[]{:S(2)}) collective-permute-start(bf16[512,512]{1,0:T(8,128)(2,1)S(1)} %get-tuple-element.50), channel_id=1, source_target_pairs={{0,1},{4,5},{8,9},{12,13},{16,17},{20,21},{24,25},{28,29}} | collective-permute-start | bytes 1572872 | tf_op jit(solution)/shard_map/ppermute | solution.py:506
  10.5 29.9 %collective-permute-start.6 = (bf16[1024,512]{1,0:T(8,128)(2,1)S(1)}, bf16[1024,512]{1,0:T(8,128)(2,1)S(1)}, u32[]{:S(2)}, u32[]{:S(2)}) collective-permute-start(bf16[1024,512]{1,0:T(8,128)(2,1)S(1)} %bitcast.15), channel_id=1, source_target_pairs={{1,2},{2,3},{5,6},{6,7},{9,10},{10,11},{13,14},{14,15},{17,18},{18... | collective-permute-start | bytes 3145736 | tf_op jit(solution)/shard_map/ppermute | solution.py:506
  21.7 9.5 %copy-start.1 = (f32[1,1024]{1,0:T(1,128)S(1)}, f32[1,1024]{1,0:T(1,128)}, u32[]{:S(2)}) copy-start(f32[1,1024]{1,0:T(1,128)} %gain_ref.9) | copy-start | bytes 12292
  21.7 8.5 %collective-permute-start.4 = (bf16[8,128,128]{2,1,0:T(8,128)(2,1)S(1)}, bf16[8,128,128]{2,1,0:T(8,128)(2,1)S(1)}, u32[]{:S(2)}, u32[]{:S(2)}) collective-permute-start(bf16[8,128,128]{2,1,0:T(8,128)(2,1)S(1)} %get-tuple-element.51), channel_id=1, source_target_pairs={{0,1},{4,5},{8,9},{12,13},{16,17},{20,21},{24,25},{28,29}} | collective-permute-start | bytes 786440 | tf_op jit(solution)/shard_map/ppermute | solution.py:506
  25.2 14.6 %collective-permute-start.2 = (bf16[2,128,1024]{2,1,0:T(8,128)(2,1)S(1)}, bf16[2,128,1024]{2,1,0:T(8,128)(2,1)S(1)}, u32[]{:S(2)}, u32[]{:S(2)}) collective-permute-start(bf16[2,128,1024]{2,1,0:T(8,128)(2,1)S(1)} %get-tuple-element.46), channel_id=1, source_target_pairs={{3,2},{2,1},{7,6},{6,5},{11,10},{10,9},{15,14},{14,13},{19,18},{18... | collective-permute-start | bytes 1572872 | tf_op jit(solution)/shard_map/ppermute | solution.py:506
  29.5 10.9 %collective-permute-start.7 = (bf16[512,512]{1,0:T(8,128)(2,1)S(1)}, bf16[512,512]{1,0:T(8,128)(2,1)S(1)}, u32[]{:S(2)}, u32[]{:S(2)}) collective-permute-start(bf16[512,512]{1,0:T(8,128)(2,1)S(1)} %get-tuple-element.59), channel_id=1, source_target_pairs={{0,1},{4,5},{8,9},{12,13},{16,17},{20,21},{24,25},{28,29}} | collective-permute-start | bytes 1572872 | tf_op jit(solution)/shard_map/ppermute | solution.py:506
  30.5 2.0 %collective-permute-start.5 = (bf16[8,128,128]{2,1,0:T(8,128)(2,1)S(1)}, bf16[8,128,128]{2,1,0:T(8,128)(2,1)S(1)}, u32[]{:S(2)}, u32[]{:S(2)}) collective-permute-start(bf16[8,128,128]{2,1,0:T(8,128)(2,1)S(1)} %shard_map.68.state_ref), channel_id=1, source_target_pairs={{1,2},{5,6},{9,10},{13,14},{17,18},{21,22},{25,26},{29,30}} | collective-permute-start | bytes 786440 | tf_op jit(solution)/shard_map/ppermute | solution.py:506
  31.2 17.9 %collective-permute-start.12 = (bf16[128,1024]{1,0:T(8,128)(2,1)S(1)}, bf16[128,1024]{1,0:T(8,128)(2,1)S(1)}, u32[]{:S(2)}, u32[]{:S(2)}) collective-permute-start(bf16[128,1024]{1,0:T(8,128)(2,1)S(1)} %shard_map.69.rows0_ref), channel_id=1, source_target_pairs={{0,3},{4,7},{8,11},{12,15},{16,19},{20,23},{24,27},{28,31}} | collective-permute-start | bytes 786440 | tf_op jit(solution)/shard_map/ppermute | solution.py:506
  32.6 18.4 %collective-permute-start.10 = (bf16[128,1024]{1,0:T(8,128)(2,1)S(1)}, bf16[128,1024]{1,0:T(8,128)(2,1)S(1)}, u32[]{:S(2)}, u32[]{:S(2)}) collective-permute-start(bf16[128,1024]{1,0:T(8,128)(2,1)S(1)} %shard_map.70.rows1_ref), channel_id=1, source_target_pairs={{1,2},{5,6},{9,10},{13,14},{17,18},{21,22},{25,26},{29,30}} | collective-permute-start | bytes 786440 | tf_op jit(solution)/shard_map/ppermute | solution.py:506
  39.8 11.9 %collective-permute-start.14 = (bf16[128,1024]{1,0:T(8,128)(2,1)S(1)}, bf16[128,1024]{1,0:T(8,128)(2,1)S(1)}, u32[]{:S(2)}, u32[]{:S(2)}) collective-permute-start(bf16[128,1024]{1,0:T(8,128)(2,1)S(1)} %shard_map.71.rows3_ref), channel_id=1, source_target_pairs={{2,1},{6,5},{10,9},{14,13},{18,17},{22,21},{26,25},{30,29}} | collective-permute-start | bytes 786440 | tf_op jit(solution)/shard_map/ppermute | solution.py:506
  40.5 26.1 %collective-permute-start.8 = (bf16[128,1536]{1,0:T(8,128)(2,1)S(1)}, bf16[128,1536]{1,0:T(8,128)(2,1)S(1)}, u32[]{:S(2)}, u32[]{:S(2)}) collective-permute-start(bf16[128,1536]{1,0:T(8,128)(2,1)S(1)} %get-tuple-element.57), channel_id=1, source_target_pairs={{0,4},{1,5},{2,6},{4,8},{5,9},{6,10},{8,12},{9,13},{10,14},{12,16}... | collective-permute-start | bytes 1179656 | tf_op jit(solution)/shard_map/ppermute | solution.py:511
  41.2 26.1 %collective-permute-start.9 = (bf16[128,1536]{1,0:T(8,128)(2,1)S(1)}, bf16[128,1536]{1,0:T(8,128)(2,1)S(1)}, u32[]{:S(2)}, u32[]{:S(2)}) collective-permute-start(bf16[128,1536]{1,0:T(8,128)(2,1)S(1)} %get-tuple-element.58), channel_id=1, source_target_pairs={{2,7},{6,11},{10,15},{14,19},{18,23},{22,27},{26,31},{30,3}} | collective-permute-start | bytes 1179656 | tf_op jit(solution)/shard_map/ppermute | solution.py:511
  49.6 8.0 %collective-permute-start.13 = (bf16[128,1024]{1,0:T(8,128)(2,1)S(1)}, bf16[128,1024]{1,0:T(8,128)(2,1)S(1)}, u32[]{:S(2)}, u32[]{:S(2)}) collective-permute-start(bf16[128,1024]{1,0:T(8,128)(2,1)S(1)} %shard_map.74), channel_id=1, source_target_pairs={{3,4},{7,8},{11,12},{15,16},{19,20},{23,24},{27,28},{31,0}} | collective-permute-start | bytes 786440 | tf_op jit(solution)/shard_map/ppermute | solution.py:511
  51.0 6.6 %collective-permute-start.11 = (bf16[128,512]{1,0:T(8,128)(2,1)S(1)}, bf16[128,512]{1,0:T(8,128)(2,1)S(1)}, u32[]{:S(2)}, u32[]{:S(2)}) collective-permute-start(bf16[128,512]{1,0:T(8,128)(2,1)S(1)} %shard_map.73), channel_id=1, source_target_pairs={{1,6},{2,5},{5,10},{6,9},{9,14},{10,13},{13,18},{14,17},{17,22},{1... | collective-permute-start | bytes 393224 | tf_op jit(solution)/shard_map/ppermute | solution.py:511
  51.7 14.9 %collective-permute-start.15 = (bf16[128,512]{1,0:T(8,128)(2,1)S(1)}, bf16[128,512]{1,0:T(8,128)(2,1)S(1)}, u32[]{:S(2)}, u32[]{:S(2)}) collective-permute-start(bf16[128,512]{1,0:T(8,128)(2,1)S(1)} %shard_map.75), channel_id=1, source_target_pairs={{1,7},{5,11},{9,15},{13,19},{17,23},{21,27},{25,31},{29,3}} | collective-permute-start | bytes 393224 | tf_op jit(solution)/shard_map/ppermute | solution.py:511
